TPU v7x, 32 devices: a whole 2x2x4 slice. The times are simulated.
32 devices in a mesh: dp: 4 (over z), fsdp: 4 (over x, core), seq: 2 (over y).
Axes of the slice: x: 2, y: 2, z: 4, core: 2. Of those that a mesh axis runs over, the one named last changes fastest.
Arguments:
- hidden_in: bfloat16 [16, 1024, 1024], P(('dp', 'fsdp'), 'seq'), may hold values from -6 to 6
- lengths: int32 [16, 4], P(('dp', 'fsdp')), may hold values from 0 to 1024, as said below
- ln1_gain: bfloat16 [1024], P('fsdp'), may hold values from 0.25 to 1.75
- ln1_bias: bfloat16 [1024], P('fsdp'), may hold values from -1.5 to 1.5
- qkv_weight: bfloat16 [1024, 3072], P('fsdp'), may hold values from -0.1875 to 0.1875
- qv_bias: bfloat16 [2048], P('fsdp'), may hold values from -2.5 to 2.5
- dense_weight: bfloat16 [1024, 1024], P('fsdp'), may hold values from -0.25 to 0.25
- dense_bias: bfloat16 [1024], P('fsdp'), may hold values from -1.5 to 1.5
- ln2_gain: bfloat16 [1024], P('fsdp'), may hold values from 0.25 to 1.75
- ln2_bias: bfloat16 [1024], P('fsdp'), may hold values from -1.5 to 1.5
- fc1_weight: bfloat16 [1024, 4096], P('fsdp'), may hold values from -0.1875 to 0.1875
- fc1_bias: bfloat16 [4096], P('fsdp'), may hold values from -2.5 to 2.5
- fc2_weight: bfloat16 [4096, 1024], P('fsdp'), may hold values from -0.125 to 0.125
- fc2_bias: bfloat16 [1024], P('fsdp'), may hold values from -1.5 to 1.5
- cotangent: bfloat16 [16, 1024, 1024], P(('dp', 'fsdp'), 'seq'), may hold values from -12 to 12
Outputs:
- output: bfloat16 [16, 1024, 1024], P(('dp', 'fsdp'), 'seq')
- grad_input: bfloat16 [16, 1024, 1024], P(('dp', 'fsdp'), 'seq')
- grad_ln1_gain: float32 [1024], P('fsdp')
- grad_ln1_bias: float32 [1024], P('fsdp')
- grad_qkv_weight: float32 [1024, 3072], P('fsdp')
- grad_qv_bias: float32 [2048], P('fsdp')
- grad_dense_weight: float32 [1024, 1024], P('fsdp')
- grad_dense_bias: float32 [1024], P('fsdp')
- grad_ln2_gain: float32 [1024], P('fsdp')
- grad_ln2_bias: float32 [1024], P('fsdp')
- grad_fc1_weight: float32 [1024, 4096], P('fsdp')
- grad_fc1_bias: float32 [4096], P('fsdp')
- grad_fc2_weight: float32 [4096, 1024], P('fsdp')
- grad_fc2_bias: float32 [1024], P('fsdp')
Inputs may be any that keep to these rules, and one draw needn't show every extreme that they name: Row r lists, in order, the lengths of the 4 documents packed into slot r; they sum to 1024, and a length may be 0. Of the 1 row of each group of devices along seq, one, drawn from the seed, begins with a document longer than 1024 - 1024 // 2 tokens; one row of the whole array, drawn from the seed, holds a single document of 1024 tokens.
All inputs are finite; a program needn't handle non-finite values.
Results may differ from a plain program's by a relative error of at most 0.015.
Values may be sent and summed in bfloat16 or wider, within the bound.
A program may use at most 192 MiB of HBM per device.

v0:
```python
import math

import jax
import jax.numpy as jnp
from jax import lax
from jax.sharding import PartitionSpec as P

H = 16
HD = 64
BLOCK = 512


EPSILON = 1e-05
GELU_COEF = 0.7978845608028654


def norm_layer(values, gain_vec, shift_vec):
    row_mean = jnp.mean(values, axis=-1, keepdims=True)
    centered = values - row_mean
    variance = jnp.mean(centered * centered, axis=-1, keepdims=True)
    return centered * lax.rsqrt(variance + EPSILON) * gain_vec + shift_vec


def gelu_tanh(values):
    return (
        0.5 * values * (1.0 + jnp.tanh(GELU_COEF * (values + 0.044715 * values * values * values)))
    )


def contract_rows(left_side, right_side):
    return lax.dot_general(
        left_side, right_side, (((0,), (0,)), ((), ())), preferred_element_type=jnp.float32
    )


def contract_cols(left_side, right_side):
    return lax.dot_general(
        left_side, right_side, (((1,), (1,)), ((), ())), preferred_element_type=jnp.float32
    )


def doc_numbers(length_row, seq_length):
    doc_ends = jnp.cumsum(length_row)
    positions = jnp.arange(seq_length, dtype=jnp.int32)
    return jnp.sum((positions[:, None] >= doc_ends[None, :]).astype(jnp.int32), axis=1)


def expand_bias(pair_bias):
    grouped = pair_bias.reshape(H, 2, HD)
    zero_keys = jnp.zeros((H, 1, HD), grouped.dtype)
    return jnp.concatenate([grouped[:, :1], zero_keys, grouped[:, 1:]], axis=1).reshape(3 * H * HD)


def block_scores(block_query, key_rows, row_start, doc_of, slopes):
    block_rows = block_query.shape[0]
    seq_length = key_rows.shape[0]
    query_pos = row_start + jnp.arange(block_rows, dtype=jnp.int32)
    key_pos = jnp.arange(seq_length, dtype=jnp.int32)
    query_doc = lax.dynamic_slice_in_dim(doc_of, row_start, block_rows, 0)
    raw_scores = jnp.einsum(
        "qhd,khd->hqk", block_query, key_rows, preferred_element_type=jnp.float32
    ) * (1.0 / math.sqrt(HD))
    offsets = (key_pos[None, :] - query_pos[:, None]).astype(jnp.float32)
    raw_scores = raw_scores + slopes[:, None, None] * offsets[None]
    allowed = (key_pos[None, :] <= query_pos[:, None]) & (doc_of[None, :] == query_doc[:, None])
    return jnp.where(allowed[None], raw_scores, -1e30)


def split_parts(mixed_seq):
    seq_length, heads_here, triple = mixed_seq.shape
    split_cols = mixed_seq.reshape(seq_length, heads_here, 3, triple // 3)
    return (split_cols[:, :, 0], split_cols[:, :, 1], split_cols[:, :, 2])


def sequence_forward(mixed_seq, length_row, slopes, block_rows):
    query_rows, key_rows, value_rows = split_parts(mixed_seq)
    seq_length, heads_here, head_width = query_rows.shape
    doc_of = doc_numbers(length_row, seq_length)

    def one_block(row_start):
        block_query = lax.dynamic_slice_in_dim(query_rows, row_start, block_rows, 0)
        scores = block_scores(block_query, key_rows, row_start, doc_of, slopes)
        row_max = jnp.max(scores, axis=-1, keepdims=True)
        exp_terms = jnp.exp(scores - row_max)
        row_total = jnp.sum(exp_terms, axis=-1, keepdims=True)
        attn_probs = (exp_terms / row_total).astype(jnp.bfloat16)
        block_out = jnp.einsum(
            "hqk,khd->qhd", attn_probs, value_rows, preferred_element_type=jnp.float32
        )
        return (block_out.astype(jnp.bfloat16), (row_max + jnp.log(row_total))[:, :, 0])

    starts = jnp.arange(seq_length // block_rows, dtype=jnp.int32) * block_rows
    block_outs, log_sums = lax.map(one_block, starts)
    return (block_outs.reshape(seq_length, heads_here, head_width), log_sums)


def sequence_backward(mixed_seq, grad_seq, log_sums, length_row, slopes, block_rows):
    query_rows, key_rows, value_rows = split_parts(mixed_seq)
    seq_length, heads_here, head_width = query_rows.shape
    doc_of = doc_numbers(length_row, seq_length)
    score_scale = 1.0 / math.sqrt(HD)

    def one_block(running, inputs):
        grad_keys, grad_values = running
        row_start, block_sums = inputs
        block_query = lax.dynamic_slice_in_dim(query_rows, row_start, block_rows, 0)
        block_grad = lax.dynamic_slice_in_dim(grad_seq, row_start, block_rows, 0)
        scores = block_scores(block_query, key_rows, row_start, doc_of, slopes)
        attn_probs = jnp.exp(scores - block_sums[:, :, None])
        probs_low = attn_probs.astype(jnp.bfloat16)
        grad_probs = jnp.einsum(
            "qhd,khd->hqk", block_grad, value_rows, preferred_element_type=jnp.float32
        )
        inner_sum = jnp.sum(grad_probs * attn_probs, axis=-1, keepdims=True)
        grad_scores = (attn_probs * (grad_probs - inner_sum)).astype(jnp.bfloat16)
        grad_query = (
            jnp.einsum("hqk,khd->qhd", grad_scores, key_rows, preferred_element_type=jnp.float32)
            * score_scale
        )
        grad_keys = (
            grad_keys
            + jnp.einsum(
                "hqk,qhd->khd", grad_scores, block_query, preferred_element_type=jnp.float32
            )
            * score_scale
        )
        grad_values = grad_values + jnp.einsum(
            "hqk,qhd->khd", probs_low, block_grad, preferred_element_type=jnp.float32
        )
        return ((grad_keys, grad_values), grad_query)

    starts = jnp.arange(seq_length // block_rows, dtype=jnp.int32) * block_rows
    zero_keys = jnp.zeros((seq_length, heads_here, head_width), jnp.float32)
    (grad_keys, grad_values), grad_queries = lax.scan(
        one_block, (zero_keys, zero_keys), (starts, log_sums)
    )
    grad_queries = grad_queries.reshape(seq_length, heads_here, head_width)
    stacked = jnp.stack([grad_queries, grad_keys, grad_values], axis=2)
    return stacked.astype(jnp.bfloat16).reshape(seq_length, heads_here, 3 * head_width)


def per_device(
    hidden_in,
    lengths,
    ln1_gain,
    ln1_bias,
    qkv_weight,
    qv_bias,
    dense_weight,
    dense_bias,
    ln2_gain,
    ln2_bias,
    fc1_weight,
    fc1_bias,
    fc2_weight,
    fc2_bias,
    cotangent,
):
    seqs_here, local_len, model_width = hidden_in.shape
    token_rows = seqs_here * local_len
    seq_ranks = lax.axis_size("seq")
    heads_here = H // seq_ranks
    block_rows = min(BLOCK, local_len * seq_ranks)
    gain_one, shift_one, w_mixed, pair_bias, w_dense, bias_dense = (
        lax.all_gather(ln1_gain, "fsdp", axis=0, tiled=True),
        lax.all_gather(ln1_bias, "fsdp", axis=0, tiled=True),
        lax.all_gather(qkv_weight, "fsdp", axis=0, tiled=True),
        lax.all_gather(qv_bias, "fsdp", axis=0, tiled=True),
        lax.all_gather(dense_weight, "fsdp", axis=0, tiled=True),
        lax.all_gather(dense_bias, "fsdp", axis=0, tiled=True),
    )
    gain_two, shift_two, w_up, bias_up, w_down, bias_down = (
        lax.all_gather(ln2_gain, "fsdp", axis=0, tiled=True),
        lax.all_gather(ln2_bias, "fsdp", axis=0, tiled=True),
        lax.all_gather(fc1_weight, "fsdp", axis=0, tiled=True),
        lax.all_gather(fc1_bias, "fsdp", axis=0, tiled=True),
        lax.all_gather(fc2_weight, "fsdp", axis=0, tiled=True),
        lax.all_gather(fc2_bias, "fsdp", axis=0, tiled=True),
    )
    tokens = hidden_in.reshape(token_rows, model_width).astype(jnp.float32)
    normed_f, norm_pull_one = jax.vjp(
        norm_layer, tokens, gain_one.astype(jnp.float32), shift_one.astype(jnp.float32)
    )
    normed = normed_f.astype(jnp.bfloat16)
    mixed_cols = (
        jnp.dot(normed, w_mixed, preferred_element_type=jnp.float32)
        + expand_bias(pair_bias.astype(jnp.float32))
    ).astype(jnp.bfloat16)
    mixed_cols = mixed_cols.reshape(seqs_here, local_len, H, 3 * HD)
    head_cols = lax.all_to_all(mixed_cols, "seq", split_axis=2, concat_axis=1, tiled=True)
    head_ids = lax.axis_index("seq") * heads_here + jnp.arange(heads_here, dtype=jnp.int32)
    slopes = 2.0 ** (-8.0 * (head_ids + 1).astype(jnp.float32) / H)

    def forward_one(paired):
        return sequence_forward(paired[0], paired[1], slopes, block_rows)

    attended_heads, log_sums = lax.map(forward_one, (head_cols, lengths))
    attended_back = lax.all_to_all(attended_heads, "seq", split_axis=1, concat_axis=2, tiled=True)
    attended_rows = attended_back.reshape(token_rows, model_width)
    hidden = (
        tokens
        + jnp.dot(attended_rows, w_dense, preferred_element_type=jnp.float32)
        + bias_dense.astype(jnp.float32)
    )
    normed_two_f, norm_pull_two = jax.vjp(
        norm_layer, hidden, gain_two.astype(jnp.float32), shift_two.astype(jnp.float32)
    )
    normed_two = normed_two_f.astype(jnp.bfloat16)
    activation = jnp.dot(normed_two, w_up, preferred_element_type=jnp.float32) + bias_up.astype(
        jnp.float32
    )
    gelu_f, gelu_pull = jax.vjp(gelu_tanh, activation)
    gelu_out = gelu_f.astype(jnp.bfloat16)
    result = (
        hidden
        + jnp.dot(gelu_out, w_down, preferred_element_type=jnp.float32)
        + bias_down.astype(jnp.float32)
    )
    output = result.astype(jnp.bfloat16).reshape(seqs_here, local_len, model_width)
    grad_out = cotangent.reshape(token_rows, model_width)
    grad_out_f = grad_out.astype(jnp.float32)
    g_w_down = contract_rows(gelu_out, grad_out)
    g_bias_down = jnp.sum(grad_out_f, axis=0)
    grad_gelu = contract_cols(grad_out, w_down)
    grad_act = gelu_pull(grad_gelu)[0]
    g_bias_up = jnp.sum(grad_act, axis=0)
    grad_act_low = grad_act.astype(jnp.bfloat16)
    g_w_up = contract_rows(normed_two, grad_act_low)
    grad_normed_two = contract_cols(grad_act_low, w_up)
    grad_hidden_norm, g_gain_two, g_shift_two = norm_pull_two(grad_normed_two)
    mlp_part = (
        lax.psum_scatter(g_gain_two, ("fsdp", "seq"), scatter_dimension=0, tiled=True),
        lax.psum_scatter(g_shift_two, ("fsdp", "seq"), scatter_dimension=0, tiled=True),
        lax.psum_scatter(g_w_up, ("fsdp", "seq"), scatter_dimension=0, tiled=True),
        lax.psum_scatter(g_bias_up, ("fsdp", "seq"), scatter_dimension=0, tiled=True),
        lax.psum_scatter(g_w_down, ("fsdp", "seq"), scatter_dimension=0, tiled=True),
        lax.psum_scatter(g_bias_down, ("fsdp", "seq"), scatter_dimension=0, tiled=True),
    )
    grad_hidden = grad_out_f + grad_hidden_norm
    g_bias_dense = jnp.sum(grad_hidden, axis=0)
    grad_hidden_low = grad_hidden.astype(jnp.bfloat16)
    g_w_dense = contract_rows(attended_rows, grad_hidden_low)
    grad_attended = contract_cols(grad_hidden_low, w_dense).astype(jnp.bfloat16)
    grad_attended = grad_attended.reshape(seqs_here, local_len, H, HD)
    grad_heads = lax.all_to_all(grad_attended, "seq", split_axis=2, concat_axis=1, tiled=True)

    def backward_one(grouped):
        return sequence_backward(grouped[0], grouped[1], grouped[2], grouped[3], slopes, block_rows)

    grad_mixed_heads = lax.map(backward_one, (head_cols, grad_heads, log_sums, lengths))
    grad_mixed = lax.all_to_all(grad_mixed_heads, "seq", split_axis=1, concat_axis=2, tiled=True)
    grad_mixed = grad_mixed.reshape(token_rows, 3 * model_width)
    g_w_mixed = contract_rows(normed, grad_mixed)
    bias_total = jnp.sum(grad_mixed, axis=0, dtype=jnp.float32).reshape(H, 3, HD)
    g_pair_bias = jnp.concatenate([bias_total[:, :1], bias_total[:, 2:]], axis=1).reshape(
        2 * H * HD
    )
    grad_normed = contract_cols(grad_mixed, w_mixed)
    grad_token_norm, g_gain_one, g_shift_one = norm_pull_one(grad_normed)
    grad_input = (
        (grad_hidden + grad_token_norm)
        .astype(jnp.bfloat16)
        .reshape(seqs_here, local_len, model_width)
    )
    attn_part = (
        lax.psum_scatter(g_gain_one, ("fsdp", "seq"), scatter_dimension=0, tiled=True),
        lax.psum_scatter(g_shift_one, ("fsdp", "seq"), scatter_dimension=0, tiled=True),
        lax.psum_scatter(g_w_mixed, ("fsdp", "seq"), scatter_dimension=0, tiled=True),
        lax.psum_scatter(g_pair_bias, ("fsdp", "seq"), scatter_dimension=0, tiled=True),
        lax.psum_scatter(g_w_dense, ("fsdp", "seq"), scatter_dimension=0, tiled=True),
        lax.psum_scatter(g_bias_dense, ("fsdp", "seq"), scatter_dimension=0, tiled=True),
    )
    summed = (
        lax.psum(attn_part[0].astype(jnp.bfloat16), "dp").astype(jnp.float32),
        lax.psum(attn_part[1].astype(jnp.bfloat16), "dp").astype(jnp.float32),
        lax.psum(attn_part[2].astype(jnp.bfloat16), "dp").astype(jnp.float32),
        lax.psum(attn_part[3].astype(jnp.bfloat16), "dp").astype(jnp.float32),
        lax.psum(attn_part[4].astype(jnp.bfloat16), "dp").astype(jnp.float32),
        lax.psum(attn_part[5].astype(jnp.bfloat16), "dp").astype(jnp.float32),
        lax.psum(mlp_part[0].astype(jnp.bfloat16), "dp").astype(jnp.float32),
        lax.psum(mlp_part[1].astype(jnp.bfloat16), "dp").astype(jnp.float32),
        lax.psum(mlp_part[2].astype(jnp.bfloat16), "dp").astype(jnp.float32),
        lax.psum(mlp_part[3].astype(jnp.bfloat16), "dp").astype(jnp.float32),
        lax.psum(mlp_part[4].astype(jnp.bfloat16), "dp").astype(jnp.float32),
        lax.psum(mlp_part[5].astype(jnp.bfloat16), "dp").astype(jnp.float32),
    )
    totals = (
        lax.all_gather(summed[0].astype(jnp.bfloat16), "seq", axis=0, tiled=True).astype(
            jnp.float32
        ),
        lax.all_gather(summed[1].astype(jnp.bfloat16), "seq", axis=0, tiled=True).astype(
            jnp.float32
        ),
        lax.all_gather(summed[2].astype(jnp.bfloat16), "seq", axis=0, tiled=True).astype(
            jnp.float32
        ),
        lax.all_gather(summed[3].astype(jnp.bfloat16), "seq", axis=0, tiled=True).astype(
            jnp.float32
        ),
        lax.all_gather(summed[4].astype(jnp.bfloat16), "seq", axis=0, tiled=True).astype(
            jnp.float32
        ),
        lax.all_gather(summed[5].astype(jnp.bfloat16), "seq", axis=0, tiled=True).astype(
            jnp.float32
        ),
        lax.all_gather(summed[6].astype(jnp.bfloat16), "seq", axis=0, tiled=True).astype(
            jnp.float32
        ),
        lax.all_gather(summed[7].astype(jnp.bfloat16), "seq", axis=0, tiled=True).astype(
            jnp.float32
        ),
        lax.all_gather(summed[8].astype(jnp.bfloat16), "seq", axis=0, tiled=True).astype(
            jnp.float32
        ),
        lax.all_gather(summed[9].astype(jnp.bfloat16), "seq", axis=0, tiled=True).astype(
            jnp.float32
        ),
        lax.all_gather(summed[10].astype(jnp.bfloat16), "seq", axis=0, tiled=True).astype(
            jnp.float32
        ),
        lax.all_gather(summed[11].astype(jnp.bfloat16), "seq", axis=0, tiled=True).astype(
            jnp.float32
        ),
    )
    return (output, grad_input) + tuple(totals)


def solution(mesh):
    placed = (
        P(("dp", "fsdp"), "seq", None),
        P(("dp", "fsdp"), None),
        P("fsdp"),
        P("fsdp"),
        P("fsdp", None),
        P("fsdp"),
        P("fsdp", None),
        P("fsdp"),
        P("fsdp"),
        P("fsdp"),
        P("fsdp", None),
        P("fsdp"),
        P("fsdp", None),
        P("fsdp"),
        P(("dp", "fsdp"), "seq", None),
    )
    return jax.shard_map(
        per_device,
        mesh=mesh,
        in_specs=placed,
        out_specs=(
            P(("dp", "fsdp"), "seq", None),
            P(("dp", "fsdp"), "seq", None),
            P("fsdp"),
            P("fsdp"),
            P("fsdp", None),
            P("fsdp"),
            P("fsdp", None),
            P("fsdp"),
            P("fsdp"),
            P("fsdp"),
            P("fsdp", None),
            P("fsdp"),
            P("fsdp", None),
            P("fsdp"),
        ),
        check_vma=False,
    )
```

profile of v0, /device:TPU:0, one launch (start us, length us, event | category | flops | bytes accessed | tf_op | source)
XLA Modules:
  0.0 1054.1 jit_solution(6210540624446652010)
XLA Ops:
  9.5 6.1 all-gather.2
  16.0 5.3 all-gather.1
  21.3 5.1 all-gather
  27.6 31.1 %all-gather.23.cloned.1.call-done = bf16[1024,3072]{1,0:T(8,128)(2,1)} async-done(((bf16[256,3072]{1,0:T(8,128)(2,1)}), bf16[1024,3072]{1,0:T(8,128)(2,1)}) %all-gather.23.cloned.1.call-update) | async-done | bytes 6291472 | tf_op jit(solution)/shard_map/all_gather | solution.py:167
  58.8 7.8 add_convert_fusion
  66.6 4.7 copy.81
  71.3 4.1 all-to-all-start
  76.3 35.8 %all-to-all-done = bf16[1,512,16,192]{1,3,0,2:T(8,128)(2,1)S(1)} async-done(((bf16[1,512,16,192]{1,3,0,2:T(8,128)(2,1)}), bf16[1,512,16,192]{1,3,0,2:T(8,128)(2,1)S(1)}, u32[]{:S(2)}, u32[]{:S(2)}) %all-to-all-start) | async-done | bytes 3145760 | tf_op jit(solution)/shard_map/all_to_all | solution.py:190
  112.1 4.9 copy.102
  117.0 4.7 reshape.392
  123.5 38.9 %while.46 = (s32[]{:T(128)}, bf16[2,512,8,64]{1,3,2,0:T(8,128)(2,1)}, f32[2,8,512]{2,1,0:T(8,128)S(1)}, s32[2]{0:T(128)S(1)}, s32[1024]{0:T(1024)S(1)}, /*index=...) while((s32[]{:T(128)}, ...), condition=%wide.region_7.8_spmd.clone, body=%wide.region_4.7_spmd.clone.sunk | while | flops 1118564864 | bytes 67256632 | solution.py:93
  127.5 6.5 fusion.131
  137.5 4.5 fusion.133
  146.9 6.4 fusion.131
  156.9 4.5 fusion.133
  171.1 5.1 all-gather.3
  176.2 5.1 all-gather.5
  181.3 5.1 all-gather.4
  186.4 5.4 all_gather.81
  201.9 10.7 %fusion.81 = f32[512,4096]{1,0:T(8,128)} fusion(bf16[1024,4096]{1,0:T(8,128)(2,1)} %all-gather.27.cloned.1.call-done, f32[512,1024]{1,0:T(8,128)S(1)} %get-tuple-element.319, f32[1024]{0:T(1024)S(1)} %bitcast.230, f32[1024]{0:T(1024)S(1)} %bitcast.224, f32[512]{0:T(512)S(1)} %fusion.79, f32[512]{0:T(512)S(1)} %broadcast_multiply_fusion), kind=kOutput, calls=%fused_computation.142 | convolution fusion | flops 4297588736 | bytes 18886656 | tf_op jit(solution)/shard_map/dot_general | solution.py:209
  212.6 15.6 %fusion.89 = (f32[4096]{0:T(1024)}, bf16[512,4096]{1,0:T(8,128)(2,1)S(1)}) fusion(bf16[4096,1024]{1,0:T(8,128)(2,1)} %all-gather.29.cloned.1.call-done, bf16[1,512,1024]{2,1,0:T(8,128)(2,1)S(1)} %copy-done.13, f32[512,4096]{1,0:T(8,128)} %fusion.81, f32[4096]{0:T(1024)S(1)} %convert_element_type.226), kind=kOutput, calls=%fused_computation.150 | convolution fusion | flops 4349489152 | bytes 22052864 | tf_op jit(solution)/shard_map/dot_general | solution.py:37
  228.2 5.5 multiply_reduce_fusion.1
  240.5 4.4 all-to-all-start.2
  245.0 4.6 fusion.75
  249.7 9.8 all-to-all-done.2
  263.5 107.1 %while.47 = (s32[]{:T(128)}, f32[1024,8,64]{0,2,1:T(8,128)}, f32[1024,8,64]{0,2,1:T(8,128)}, bf16[2,512,8,64]{1,3,2,0:T(8,128)(2,1)}, s32[2]{0:T(128)S(1)}, /*in...) while((s32[]{:T(128)}, f32[1024,8,64]{0,2,1:T(8,128)}, ...), condition=%wide.region_14.15_spmd.clone, body=%wide.region_12.14_spmd.clone.sunk | while | flops 2735993344 | bytes 305234336 | solution.py:134
  269.0 8.4 subtract_exponential_fusion.3
  277.4 11.2 %multiply_reduce_fusion.5 = (f32[8,512]{1,0:T(8,128)S(1)}, f32[8,512,1024]{2,1,0:T(8,128)}) fusion(f32[8,512,1024]{2,1,0:T(8,128)S(1)} %subtract_exponential_fusion.3, bf16[1024,8,64]{0,2,1:T(8,128)(2,1)} %get-tuple-element.540, bf16[1024,8,64]{0,2,1:T(8,128)(2,1)} %get-tuple-element.539, s32[]{:T(128)S(6)} %select_n.27), kind=kOutput, calls=%fused_computation.19.clone.1 | convolution fusion | flops 545255424 | bytes 35143684 | tf_op jit(solution)/shard_map/while/body/eval_jaxpr/while/body/eval_jaxpr/qhd,khd->hqk/dot_general | solution.py:111
  288.9 9.5 multiply_convert_fusion.5
  298.4 6.8 bitcast_add_fusion.4
  307.7 4.2 bitcast_add_fusion.5
  311.9 4.7 fusion.144
  321.9 8.4 subtract_exponential_fusion.3
  330.3 11.0 %multiply_reduce_fusion.5 = (f32[8,512]{1,0:T(8,128)S(1)}, f32[8,512,1024]{2,1,0:T(8,128)}) fusion(f32[8,512,1024]{2,1,0:T(8,128)S(1)} %subtract_exponential_fusion.3, bf16[1024,8,64]{0,2,1:T(8,128)(2,1)} %get-tuple-element.540, bf16[1024,8,64]{0,2,1:T(8,128)(2,1)} %get-tuple-element.539, s32[]{:T(128)S(6)} %select_n.27), kind=kOutput, calls=%fused_computation.19.clone.1 | convolution fusion | flops 545255424 | bytes 35143684 | tf_op jit(solution)/shard_map/while/body/eval_jaxpr/while/body/eval_jaxpr/qhd,khd->hqk/dot_general | solution.py:111
  341.5 9.4 multiply_convert_fusion.5
  350.9 7.2 bitcast_add_fusion.4
  360.6 4.9 bitcast_add_fusion.5
  365.5 4.7 fusion.144
  377.4 5.0 copy.93
  382.4 54.9 %all_to_all.60 = bf16[1,1024,8,192]{3,2,0,1:T(8,128)(2,1)} all-to-all(bf16[1,1024,8,192]{3,2,0,1:T(8,128)(2,1)} %copy.93), channel_id=1, replica_groups=mesh['dp'=4,'fsdp'=4,'seq'=2] {'seq'}, dimensions={1} | all-to-all | bytes 6291456 | tf_op jit(solution)/shard_map/all_to_all | solution.py:251
  437.3 8.6 copy.99
  448.3 6.9 fusion.58
  455.8 17.3 %fusion.51 = f32[1024,4096]{1,0:T(8,128)} fusion(bf16[512,4096]{1,0:T(8,128)(2,1)} %copy-done.56, f32[512,1024]{1,0:T(8,128)} %copy-done.7, f32[1024]{0:T(1024)S(1)} %bitcast.231, f32[1024]{0:T(1024)S(1)} %bitcast.227, f32[512]{0:T(512)S(1)} %copy-done.38, f32[512]{0:T(512)S(1)} %copy-done.27), kind=kOutput, calls=%fused_computation.85 | convolution fusion | flops 4297588736 | bytes 23080960 | tf_op jit(solution)/shard_map/dot_general | solution.py:31
  473.8 16.1 %fusion.61 = f32[4096,1024]{1,0:T(8,128)} fusion(bf16[1,512,1024]{2,1,0:T(8,128)(2,1)} %param.33, f32[512,4096]{1,0:T(8,128)} %fusion.81, f32[4096]{0:T(1024)S(1)} %copy-done.34), kind=kOutput, calls=%fused_computation.100 | convolution fusion | flops 4315938816 | bytes 26230784 | tf_op jit(solution)/shard_map/dot_general | solution.py:31
  491.8 55.3 %reduce-scatter.5.cloned.1.call-done = f32[128,3072]{1,0:T(8,128)} async-done(((f32[1024,3072]{1,0:T(8,128)}), f32[128,3072]{1,0:T(8,128)}) %reduce-scatter.5.cloned.1.call-update) | async-done | bytes 1572880 | tf_op jit(solution)/shard_map/reduce_scatter | solution.py:268
  549.6 117.6 %reduce-scatter.9.cloned.1.call-done = f32[128,4096]{1,0:T(8,128)} async-done(((f32[1024,4096]{1,0:T(8,128)}), f32[128,4096]{1,0:T(8,128)}) %reduce-scatter.9.cloned.1.call-update) | async-done | bytes 2097168 | tf_op jit(solution)/shard_map/reduce_scatter | solution.py:234
  669.8 117.3 %reduce-scatter.11.cloned.1.call-done = f32[512,1024]{1,0:T(8,128)} async-done(((f32[4096,1024]{1,0:T(8,128)}), f32[512,1024]{1,0:T(8,128)}) %reduce-scatter.11.cloned.1.call-update) | async-done | bytes 2097168 | tf_op jit(solution)/shard_map/reduce_scatter | solution.py:236
  789.9 123.3 %all-reduce.13.cloned.1.call-done = (bf16[128,3072]{1,0:T(8,128)(2,1)}, bf16[128,1024]{1,0:T(8,128)(2,1)}, bf16[128,4096]{1,0:T(8,128)(2,1)}, bf16[512,1024]{1,0:T(8,128)(2,1)}) async-done(((bf16[128,3072]{1,0:T(8,128)(2,1)}, bf16[128,1024]{1,0:T(8,128)(2,1)}, bf16[128,4096]{1,0:T(8,128)(2,1)}, bf16[512,1024]{1,0:T(8,128)(2,1)}), (bf16[128,3072]{1,0:T(8,128)(2,1)}, bf16[128,1024]{1,0:T(8,128)(2,1)}, ...) | async-done | bytes 3145744 | tf_op jit(solution)/shard_map/psum | solution.py:276
  913.3 5.1 all-gather.6
  921.2 13.0 %fusion.55 = bf16[1,512,1024]{2,1,0:T(8,128)(2,1)} fusion(f32[512,1024]{1,0:T(8,128)} %copy-done.7, bf16[4096,1024]{1,0:T(8,128)(2,1)} %all-gather.29.cloned.1.call-done, f32[1024]{0:T(1024)S(1)} %bitcast.233, f32[512,4096]{1,0:T(8,128)} %fusion.81, f32[4096]{0:T(1024)S(1)} %copy-done.34), kind=kOutput, calls=%fused_computation.93 | convolution fusion | flops 4317511680 | bytes 19943424 | tf_op jit(solution)/shard_map/dot_general | solution.py:216
  939.3 7.8 fusion.83
  951.4 26.8 %all-reduce.8 = (bf16[1024]{0:T(1024)(128)(2,1)S(1)}, bf16[1024]{0:T(1024)(128)(2,1)S(1)}, bf16[2048]{0:T(1024)(128)(2,1)S(1)}, bf16[1024]{0:T(1024)(128)(2,1)S(...) all-reduce(f32[1024]{0:T(1024)S(1)} %get-tuple-element.235, ...), channel_id=2, replica_groups=mesh['dp'=4,'fsdp'=4,'seq'=2] {'fsdp','seq'}, use_global_device_ids=true, to_apply=%region_18.19.clone | all-reduce | flops 12288 | bytes 73728
  978.8 10.1 all-reduce.9
  988.9 4.2 all-gather.7
  993.6 4.2 all-gather.8
  998.4 4.2 all-gather.9
  1003.2 4.2 all-gather.10
  1008.0 4.2 all-gather.11
  1012.8 4.2 all-gather.12
  1017.6 4.3 all-gather.13
  1022.5 4.2 all-gather.14
  1027.3 7.0 all_gather.88
  1038.8 4.1 convert_element_type.256
  1042.9 4.1 convert_element_type.260
  (285 shorter events, 101.1 us)
Async XLA Ops:
  7.2 2.3 copy-start.46
  7.2 8.8 copy-start.48
  7.2 14.1 %copy-start.49 = (bf16[256]{0:T(256)(128)(2,1)S(1)}, bf16[256]{0:T(256)(128)(2,1)}, u32[]{:S(2)}) copy-start(bf16[256]{0:T(256)(128)(2,1)} %param.21) | copy-start | bytes 1540
  7.2 19.2 %copy-start.3 = (bf16[1,512,1024]{2,1,0:T(8,128)(2,1)S(1)}, bf16[1,512,1024]{2,1,0:T(8,128)(2,1)}, u32[]{:S(2)}) copy-start(bf16[1,512,1024]{2,1,0:T(8,128)(2,1)} %param.19) | copy-start | bytes 3145732
  7.2 51.5 %all-gather.23.cloned.1.call-start = ((), (), s32[]{:S(2)}) async-start(), calls=%async_computation.8 | async-start | bytes 7864320 | tf_op jit(solution)/shard_map/all_gather | solution.py:167
  8.0 190.2 %all-gather.25.cloned.1.call-start = ((), (), s32[]{:S(2)}) async-start(), calls=%async_computation.9 | async-start | bytes 2621440 | tf_op jit(solution)/shard_map/all_gather | solution.py:169
  8.7 193.2 %all-gather.27.cloned.1.call-start = ((), (), s32[]{:S(2)}) async-start(), calls=%async_computation.10 | async-start | bytes 10485760 | tf_op jit(solution)/shard_map/all_gather | solution.py:175
  21.3 45.3 %copy-start.41 = (f32[4,1,256]{2,1,0:T(1,128)}, f32[4,1,256]{2,1,0:T(1,128)S(1)}, u32[]{:S(2)}) copy-start(f32[4,1,256]{2,1,0:T(1,128)S(1)} %convert_element_type.264) | copy-start | bytes 12292
  26.4 40.2 %copy-start.20 = (f32[4,1,256]{2,1,0:T(1,128)}, f32[4,1,256]{2,1,0:T(1,128)S(1)}, u32[]{:S(2)}) copy-start(f32[4,1,256]{2,1,0:T(1,128)S(1)} %convert_element_type.263) | copy-start | bytes 12292
  26.6 39.9 %copy-start.22 = (f32[512]{0:T(512)}, f32[512]{0:T(512)S(1)}, u32[]{:S(2)}) copy-start(f32[512]{0:T(512)S(1)} %broadcast_multiply_fusion.1) | copy-start | bytes 6148
  27.6 39.0 %copy-start.28 = (f32[512]{0:T(512)}, f32[512]{0:T(512)S(1)}, u32[]{:S(2)}) copy-start(f32[512]{0:T(512)S(1)} %fusion.78) | copy-start | bytes 6148
  71.3 4.7 copy-start.50
  71.3 40.8 %all-to-all-start = ((bf16[1,512,16,192]{1,3,0,2:T(8,128)(2,1)}), bf16[1,512,16,192]{1,3,0,2:T(8,128)(2,1)S(1)}, u32[]{:S(2)}, u32[]{:S(2)}) async-start(bf16[1,512,16,192]{1,3,0,2:T(8,128)(2,1)} %bitcast.210), calls=%async_computation | async-start | bytes 6291456 | tf_op jit(solution)/shard_map/all_to_all | solution.py:190
  75.4 137.2 %all-gather.29.cloned.1.call-start = ((), (), s32[]{:S(2)}) async-start(), calls=%async_computation.11 | async-start | bytes 10485760 | tf_op jit(solution)/shard_map/all_gather | solution.py:177
  133.9 3.5 copy-start.17
  153.4 3.5 copy-start.17
  165.0 6.1 copy-start.51
  165.1 11.2 %copy-start.52 = (bf16[256]{0:T(256)(128)(2,1)S(1)}, bf16[256]{0:T(256)(128)(2,1)}, u32[]{:S(2)}) copy-start(bf16[256]{0:T(256)(128)(2,1)} %param.28) | copy-start | bytes 1540
  165.1 16.2 %copy-start.53 = (bf16[256]{0:T(256)(128)(2,1)S(1)}, bf16[256]{0:T(256)(128)(2,1)}, u32[]{:S(2)}) copy-start(bf16[256]{0:T(256)(128)(2,1)} %param.27) | copy-start | bytes 1540
  165.1 21.3 %copy-start.45 = (bf16[1024]{0:T(1024)(128)(2,1)S(1)}, bf16[1024]{0:T(1024)(128)(2,1)}, u32[]{:S(2)}) copy-start(bf16[1024]{0:T(1024)(128)(2,1)} %param.30) | copy-start | bytes 6148
  167.5 24.3 %all-to-all-start.1 = ((bf16[2,2,131072]{2,1,0:T(2,128)(2,1)}), bf16[2,2,131072]{2,1,0:T(2,128)(2,1)S(1)}, u32[]{:S(2)}, u32[]{:S(2)}) async-start(bf16[2,2,131072]{2,1,0:T(2,128)(2,1)} %reshape.462), calls=%async_computation.1 | async-start | bytes 2097152 | tf_op jit(solution)/shard_map/all_to_all | solution.py:198
  181.3 20.6 %copy-start.43 = (f32[4,1,256]{2,1,0:T(1,128)}, f32[4,1,256]{2,1,0:T(1,128)S(1)}, u32[]{:S(2)}) copy-start(f32[4,1,256]{2,1,0:T(1,128)S(1)} %convert_element_type.267) | copy-start | bytes 12292
  186.4 47.3 %copy-start.35 = (f32[4,1,256]{2,1,0:T(1,128)}, f32[4,1,256]{2,1,0:T(1,128)S(1)}, u32[]{:S(2)}) copy-start(f32[4,1,256]{2,1,0:T(1,128)S(1)} %convert_element_type.266) | copy-start | bytes 12292
  191.8 20.7 %copy-start.33 = (f32[4096]{0:T(1024)}, f32[4096]{0:T(1024)S(1)}, u32[]{:S(2)}) copy-start(f32[4096]{0:T(1024)S(1)} %convert_element_type.226) | copy-start | bytes 49156
  193.2 5.0 copy-start.4
  201.4 32.3 %copy-start.7 = (f32[512,1024]{1,0:T(8,128)}, f32[512,1024]{1,0:T(8,128)S(1)}, u32[]{:S(2)}) copy-start(f32[512,1024]{1,0:T(8,128)S(1)} %get-tuple-element.319) | copy-start | bytes 6291460
  201.5 32.3 %copy-start.26 = (f32[512]{0:T(512)}, f32[512]{0:T(512)S(1)}, u32[]{:S(2)}) copy-start(f32[512]{0:T(512)S(1)} %broadcast_multiply_fusion) | copy-start | bytes 6148
  201.8 31.9 %copy-start.37 = (f32[512]{0:T(512)}, f32[512]{0:T(512)S(1)}, u32[]{:S(2)}) copy-start(f32[512]{0:T(512)S(1)} %fusion.79) | copy-start | bytes 6148
  201.9 10.7 %copy-start.13 = (bf16[1,512,1024]{2,1,0:T(8,128)(2,1)S(1)}, bf16[1,512,1024]{2,1,0:T(8,128)(2,1)}, u32[]{:S(2)}) copy-start(bf16[1,512,1024]{2,1,0:T(8,128)(2,1)} %param.33) | copy-start | bytes 3145732
  212.6 15.6 %copy-start.47 = (bf16[1024,4096]{1,0:T(8,128)(2,1)S(1)}, bf16[1024,4096]{1,0:T(8,128)(2,1)}, u32[]{:S(2)}) copy-start(bf16[1024,4096]{1,0:T(8,128)(2,1)} %all-gather.27.cloned.1.call-done) | copy-start | bytes 25165828
  228.2 5.5 copy-start.56
  234.5 10.5 copy-start.30
  238.1 6.9 copy-start.9
  238.1 7.0 copy-start.11
  240.5 19.0 %all-to-all-start.2 = ((bf16[1,512,16,64]{1,3,0,2:T(8,128)(2,1)}), bf16[1,512,16,64]{1,3,0,2:T(8,128)(2,1)}, u32[]{:S(2)}, u32[]{:S(2)}) async-start(bf16[1,512,16,64]{1,3,0,2:T(8,128)(2,1)} %bitcast.215), calls=%async_computation.2 | async-start | bytes 2097152 | tf_op jit(solution)/shard_map/all_to_all | solution.py:245
  244.9 245.1 %reduce-scatter.7.cloned.1.call-start = ((), (), s32[]{:S(2)}) async-start(), calls=%async_computation.14 | async-start | bytes 4718592 | tf_op jit(solution)/shard_map/reduce_scatter | solution.py:270
  249.7 297.5 %reduce-scatter.5.cloned.1.call-start = ((), (), s32[]{:S(2)}) async-start(), calls=%async_computation.12 | async-start | bytes 14155776 | tf_op jit(solution)/shard_map/reduce_scatter | solution.py:268
  277.4 11.5 %copy-start = (f32[8,512,1024]{2,1,0:T(8,128)}, f32[8,512,1024]{2,1,0:T(8,128)S(1)}, u32[]{:S(2)}) copy-start(f32[8,512,1024]{2,1,0:T(8,128)S(1)} %subtract_exponential_fusion.3) | copy-start | bytes 50331652 | tf_op jit(solution)/shard_map/while/body/eval_jaxpr/while
  298.4 9.3 copy-start.1
  298.4 13.5 %slice-start = ((s8[8388608]{0:T(1024)(128)(4,1)}), s8[4194304]{0:T(1024)(128)(4,1)S(1)}, s32[]{:S(2)}) async-start(s8[8388608]{0:T(1024)(128)(4,1)} %bitcast.202), calls=%async_computation.20 | async-start | bytes 8388608 | tf_op jit(solution)/shard_map/while/body/eval_jaxpr/while
  307.7 4.2 slice-start.1
  330.3 11.2 %copy-start = (f32[8,512,1024]{2,1,0:T(8,128)}, f32[8,512,1024]{2,1,0:T(8,128)S(1)}, u32[]{:S(2)}) copy-start(f32[8,512,1024]{2,1,0:T(8,128)S(1)} %subtract_exponential_fusion.3) | copy-start | bytes 50331652 | tf_op jit(solution)/shard_map/while/body/eval_jaxpr/while
  350.9 9.7 copy-start.1
  350.9 14.6 %slice-start = ((s8[8388608]{0:T(1024)(128)(4,1)}), s8[4194304]{0:T(1024)(128)(4,1)S(1)}, s32[]{:S(2)}) async-start(s8[8388608]{0:T(1024)(128)(4,1)} %bitcast.202), calls=%async_computation.20 | async-start | bytes 8388608 | tf_op jit(solution)/shard_map/while/body/eval_jaxpr/while
  360.6 4.9 slice-start.1
  370.6 4.0 copy-start.2
  445.9 2.4 copy-start.5
  445.9 2.3 copy-start.21
  445.9 2.3 copy-start.23
  445.9 2.3 copy-start.29
  445.9 2.3 copy-start.42
  455.2 212.0 %reduce-scatter.9.cloned.1.call-start = ((), (), s32[]{:S(2)}) async-start(), calls=%async_computation.15 | async-start | bytes 18874368 | tf_op jit(solution)/shard_map/reduce_scatter | solution.py:234
  473.1 314.0 %reduce-scatter.11.cloned.1.call-start = ((), (), s32[]{:S(2)}) async-start(), calls=%async_computation.17 | async-start | bytes 18874368 | tf_op jit(solution)/shard_map/reduce_scatter | solution.py:236
  490.0 423.2 %all-reduce.13.cloned.1.call-start = ((), (), s32[]{:S(2)}) async-start(), calls=%async_computation.19 | async-start | bytes 6291456 | tf_op jit(solution)/shard_map/psum | solution.py:276
  669.8 243.5 %copy-start.54 = (bf16[256]{0:T(256)(128)(2,1)S(1)}, bf16[256]{0:T(256)(128)(2,1)}, u32[]{:S(2)}) copy-start(bf16[256]{0:T(256)(128)(2,1)} %param.32) | copy-start | bytes 1540
  669.8 248.6 %copy-start.55 = (u32[32]{0:T(128)S(1)}, u32[32]{0:T(128)}, u32[]{:S(2)}) copy-start(u32[32]{0:T(128)} %constant.132) | copy-start | bytes 388
  789.9 245.5 %all-gather.31.cloned.1.call-start = ((), (), s32[]{:S(2)}) async-start(), calls=%async_computation.13 | async-start | bytes 2359296 | tf_op jit(solution)/shard_map/all_gather | solution.py:294
  913.2 125.6 %all-gather.33.cloned.1.call-start = ((), (), s32[]{:S(2)}) async-start(), calls=%async_computation.16 | async-start | bytes 3145728 | tf_op jit(solution)/shard_map/all_gather | solution.py:312
  921.0 122.0 %all-gather.35.cloned.1.call-start = ((), (), s32[]{:S(2)}) async-start(), calls=%async_computation.18 | async-start | bytes 3145728 | tf_op jit(solution)/shard_map/all_gather | solution.py:318
  939.3 7.9 copy-start.25
  939.3 7.9 copy-start.6
  949.3 2.1 copy-start.39
  949.3 2.1 copy-start.40
  949.3 78.0 %copy-start.19 = (bf16[128,1024]{1,0:T(8,128)(2,1)S(1)}, bf16[128,1024]{1,0:T(8,128)(2,1)}, u32[]{:S(2)}) copy-start(bf16[128,1024]{1,0:T(8,128)(2,1)} %get-tuple-element.301) | copy-start | bytes 786436
  (16 other events, 21.0 us)
Sparse Core Ops, SparseCore 0:
  9.6 49.0 all-gather.22
  60.3 22.5 all-gather.24
  84.5 58.2 all-gather.26
  144.2 58.3 all-gather.28
  249.8 51.9 reduce-scatter.6
  455.3 91.8 reduce-scatter.4
  551.2 115.9 reduce-scatter.8
  671.1 115.9 reduce-scatter.10
  791.1 122.0 all-reduce.12
  914.7 26.1 all-gather.30
  942.5 35.4 all-gather.32
  979.4 33.3 all-gather.34
where the time goes:
time: 1060 us; the launch traced here: 1050 us
  waiting for transfers between devices  493 us (47%)
  matrix products  204 us (19%)
  blocking collectives  175 us (17%)
  other arithmetic  72.2 us (7%)
  local copies, waits for them, and re-layouts  71.2 us (7%)
  between operations  17.1 us (2%)
  starting transfers between devices  13 us (1%)
    psum x1, waiting for transfers between devices, per_device(): lax.psum(attn_part[2].astype(jnp.bfloat16), 'dp').astype(jnp.float32)  123 us
    reduce_scatter x1, waiting for transfers between devices, per_device(): lax.psum_scatter(g_w_up, ('fsdp', 'seq'), scatter_dimension=0, tiled=True)  118 us
    reduce_scatter x1, waiting for transfers between devices, per_device(): lax.psum_scatter(g_w_down, ('fsdp', 'seq'), scatter_dimension=0, tiled=True)  117 us
    reduce_scatter x1, waiting for transfers between devices, per_device(): lax.psum_scatter(g_w_mixed, ('fsdp', 'seq'), scatter_dimension=0, tiled=T...  55.3 us
    all_to_all x1, blocking collectives, per_device(): lax.all_to_all(grad_mixed_heads, 'seq', split_axis=1, concat_axis=2, tile...  54.9 us
    dot_general x4, matrix products, contract_rows(): lax.dot_general(left_side, right_side, (((0,), (0,)), ((), ())), preferre...  44.9 us
    all_to_all x1, waiting for transfers between devices, per_device(): lax.all_to_all(mixed_cols, 'seq', split_axis=2, concat_axis=1, tiled=True)  35.8 us
    dot_general x4, matrix products, contract_cols(): lax.dot_general(left_side, right_side, (((1,), (1,)), ((), ())), preferre...  31.2 us
  transfers between devices with their start and end apart: 15, of which 7 were waited for; matrix products, arithmetic and copies ran while one was open for 29% of the time, Pallas kernels for 0%

commit v1 on v0

v1 whole, which is shorter than its diff:
```python
import functools
import math

import jax
import jax.numpy as jnp
from jax import lax
from jax.experimental import pallas as pl
from jax.experimental.pallas import tpu as pltpu
from jax.sharding import PartitionSpec as P

H = 16
HD = 64
ROWS = 256
VMEM = 48 * 1024 * 1024


EPSILON = 1e-05
GELU_COEF = 0.7978845608028654


def norm_layer(values, gain_vec, shift_vec):
    row_mean = jnp.mean(values, axis=-1, keepdims=True)
    centered = values - row_mean
    variance = jnp.mean(centered * centered, axis=-1, keepdims=True)
    return centered * lax.rsqrt(variance + EPSILON) * gain_vec + shift_vec


def gelu_tanh(values):
    return (
        0.5 * values * (1.0 + jnp.tanh(GELU_COEF * (values + 0.044715 * values * values * values)))
    )


def contract_rows(left_side, right_side):
    return lax.dot_general(
        left_side, right_side, (((0,), (0,)), ((), ())), preferred_element_type=jnp.float32
    )


def contract_cols(left_side, right_side):
    return lax.dot_general(
        left_side, right_side, (((1,), (1,)), ((), ())), preferred_element_type=jnp.float32
    )


def steps_of(axis):
    size = lax.axis_size(axis)
    return [2**k for k in range(size.bit_length() - 1)]


def bit_of(axis, step):
    return lax.rem(lax.axis_index(axis) // step, 2)


def swap(value, axis, step):
    pairs = [(i, i ^ step) for i in range(lax.axis_size(axis))]
    return lax.ppermute(value, axis, pairs)


def pick(value, dim, index):
    return lax.dynamic_index_in_dim(value, index, dim, keepdims=False)


def halve(value, axis, step, dim):
    bit = bit_of(axis, step)
    received = swap(pick(value, dim, 1 - bit), axis, step)
    kept = pick(value, dim, bit).astype(jnp.float32)
    return (kept + received.astype(jnp.float32)).astype(jnp.bfloat16)


def double(value, axis, step, dim):
    other = swap(value, axis, step)
    first = jnp.stack([value, other], axis=dim)
    second = jnp.stack([other, value], axis=dim)
    return jnp.where(bit_of(axis, step) == 0, first, second)


def gather(value, axis):
    shape = value.shape
    value = value[None]
    for step in steps_of(axis):
        value = double(value, axis, step, 0).reshape((-1,) + shape)
    return value


def reduce_rows(grad, order, axes):
    labels = [(axis, step) for axis in axes for step in reversed(steps_of(axis))]
    columns = grad.shape[1]
    value = grad.reshape((2,) * len(labels) + (-1, columns))
    for label in order:
        value = halve(value, label[0], label[1], labels.index(label))
        labels.remove(label)
    return value


def labels_of(*axes):
    return [(axis, step) for axis in axes for step in steps_of(axis)]


def spread_rows(value, axes):
    columns = value.shape[-1]
    for axis in reversed(axes):
        for place, step in enumerate(reversed(steps_of(axis))):
            value = double(value, axis, step, place)
        value = value.reshape(-1, columns)
    return value


def sum_all(value, axes):
    for axis in axes:
        for step in steps_of(axis):
            value = value + swap(value, axis, step)
    return value


def doc_starts_of(lengths, seq_length):
    ends = jnp.cumsum(lengths, axis=1)
    positions = jnp.arange(seq_length, dtype=jnp.int32)
    passed = ends[:, :, None] <= positions[None, None, :]
    return jnp.max(jnp.where(passed, ends[:, :, None], 0), axis=1, keepdims=True)


def local_columns(pair_bias, heads_here):
    first = lax.axis_index("seq") * heads_here
    grouped = lax.dynamic_slice_in_dim(pair_bias.reshape(H, 2, HD), first, heads_here, 0)
    zeros = jnp.zeros((heads_here, 1, HD), grouped.dtype)
    stacked = jnp.concatenate([grouped[:, :1], zeros, grouped[:, 1:]], axis=1)
    return stacked.reshape(heads_here * 3 * HD)


def pack(parts):
    return jnp.concatenate(parts).reshape(-1, 128)


def attend_forward_kernel(starts_ref, slopes_ref, mixed_ref, out_ref, sums_ref, *, block, heads):
    length = mixed_ref.shape[1]
    pair = pl.program_id(1)
    for head in range(heads):
        slope = slopes_ref[pair * heads + head]
        base = head * 3 * HD
        keys = mixed_ref[0, :, base + HD : base + 2 * HD]
        values_t = mixed_ref[0, :, base + 2 * HD : base + 3 * HD].T
        for start in range(0, length, block):
            stop = start + block
            query = mixed_ref[0, start:stop, base : base + HD] * jnp.bfloat16(1 / math.sqrt(HD))
            offsets = masked_offsets(starts_ref[0, :, start:stop], start, stop, block)
            scores = contract_cols(keys[:stop], query) + slope * offsets
            row_max = jnp.max(scores, axis=0, keepdims=True)
            terms = jnp.exp(scores - row_max)
            total = jnp.sum(terms, axis=0, keepdims=True)
            probs = (terms * (1.0 / total)).astype(jnp.bfloat16)
            attended = jnp.dot(
                values_t[:, :stop], probs, preferred_element_type=jnp.float32
            )
            out_ref[0, start:stop, head * HD : (head + 1) * HD] = attended.T.astype(jnp.bfloat16)
            sums_ref[0, 0, head : head + 1, start:stop] = row_max + jnp.log(total)


def masked_offsets(doc_starts, start, stop, block):
    key_pos = lax.broadcasted_iota(jnp.int32, (stop, block), 0)
    query_pos = lax.broadcasted_iota(jnp.int32, (stop, block), 1) + start
    allowed = (key_pos <= query_pos) & (key_pos >= doc_starts)
    return jnp.where(allowed, (key_pos - query_pos).astype(jnp.float32), -1e32)


def attend_backward_kernel(
    starts_ref, slopes_ref, mixed_ref, grad_ref, sums_ref, out_ref, keys_acc, values_acc, *, block, heads
):
    length = mixed_ref.shape[1]
    pair = pl.program_id(1)
    scale = 1 / math.sqrt(HD)
    for head in range(heads):
        slope = slopes_ref[pair * heads + head]
        base = head * 3 * HD
        keys = mixed_ref[0, :, base + HD : base + 2 * HD]
        keys_t = keys.T
        values = mixed_ref[0, :, base + 2 * HD : base + 3 * HD]
        for start in reversed(range(0, length, block)):
            stop = start + block
            query = mixed_ref[0, start:stop, base : base + HD] * jnp.bfloat16(scale)
            grad = grad_ref[0, start:stop, head * HD : (head + 1) * HD]
            offsets = masked_offsets(starts_ref[0, :, start:stop], start, stop, block)
            scores = contract_cols(keys[:stop], query) + slope * offsets
            probs = jnp.exp(scores - sums_ref[0, 0, head : head + 1, start:stop])
            grad_probs = contract_cols(values[:stop], grad)
            inner = jnp.sum(grad_probs * probs, axis=0, keepdims=True)
            grad_scores = (probs * (grad_probs - inner)).astype(jnp.bfloat16)
            grad_query = jnp.dot(
                keys_t[:, :stop], grad_scores, preferred_element_type=jnp.float32
            )
            out_ref[0, start:stop, base : base + HD] = (grad_query.T * scale).astype(jnp.bfloat16)
            grad_keys = jnp.dot(grad_scores, query, preferred_element_type=jnp.float32)
            grad_values = jnp.dot(
                probs.astype(jnp.bfloat16), grad, preferred_element_type=jnp.float32
            )
            if stop == length:
                keys_acc[...] = grad_keys
                values_acc[...] = grad_values
            else:
                keys_acc[:stop] += grad_keys
                values_acc[:stop] += grad_values
        out_ref[0, :, base + HD : base + 2 * HD] = keys_acc[...].astype(jnp.bfloat16)
        out_ref[0, :, base + 2 * HD : base + 3 * HD] = values_acc[...].astype(jnp.bfloat16)


def attention_specs(length, heads):
    return [
        pl.BlockSpec((1, 1, length), lambda s, p: (s, 0, 0)),
        pl.BlockSpec(memory_space=pltpu.SMEM),
        pl.BlockSpec((1, length, heads * 3 * HD), lambda s, p: (s, 0, p)),
    ]


def attend_forward(mixed, doc_starts, slopes):
    seqs, length, columns = mixed.shape
    heads_here = columns // (3 * HD)
    heads = min(2, heads_here)
    pairs = heads_here // heads
    return pl.pallas_call(
        functools.partial(attend_forward_kernel, block=min(ROWS, length), heads=heads),
        grid=(seqs, pairs),
        in_specs=attention_specs(length, heads),
        out_specs=[
            pl.BlockSpec((1, length, heads * HD), lambda s, p: (s, 0, p)),
            pl.BlockSpec((1, 1, heads, length), lambda s, p: (s, p, 0, 0)),
        ],
        out_shape=[
            jax.ShapeDtypeStruct((seqs, length, heads_here * HD), jnp.bfloat16),
            jax.ShapeDtypeStruct((seqs, pairs, heads, length), jnp.float32),
        ],
        compiler_params=pltpu.CompilerParams(vmem_limit_bytes=VMEM),
        cost_estimate=pl.CostEstimate(
            flops=seqs * heads_here * length * length * HD * 8,
            bytes_accessed=seqs * length * columns * 4,
            transcendentals=seqs * heads_here * length * length,
        ),
    )(doc_starts, slopes, mixed)


def attend_backward(mixed, grad, sums, doc_starts, slopes):
    seqs, length, columns = mixed.shape
    heads_here = columns // (3 * HD)
    heads = min(2, heads_here)
    pairs = heads_here // heads
    return pl.pallas_call(
        functools.partial(attend_backward_kernel, block=min(ROWS, length), heads=heads),
        grid=(seqs, pairs),
        in_specs=attention_specs(length, heads)
        + [
            pl.BlockSpec((1, length, heads * HD), lambda s, p: (s, 0, p)),
            pl.BlockSpec((1, 1, heads, length), lambda s, p: (s, p, 0, 0)),
        ],
        out_specs=pl.BlockSpec((1, length, heads * 3 * HD), lambda s, p: (s, 0, p)),
        out_shape=jax.ShapeDtypeStruct((seqs, length, columns), jnp.bfloat16),
        scratch_shapes=[
            pltpu.VMEM((length, HD), jnp.float32),
            pltpu.VMEM((length, HD), jnp.float32),
        ],
        compiler_params=pltpu.CompilerParams(vmem_limit_bytes=VMEM),
        cost_estimate=pl.CostEstimate(
            flops=seqs * heads_here * length * length * HD * 20,
            bytes_accessed=seqs * length * columns * 6,
            transcendentals=seqs * heads_here * length * length,
        ),
    )(doc_starts, slopes, mixed, grad, sums)


def per_device(
    hidden_in,
    lengths,
    ln1_gain,
    ln1_bias,
    qkv_weight,
    qv_bias,
    dense_weight,
    dense_bias,
    ln2_gain,
    ln2_bias,
    fc1_weight,
    fc1_bias,
    fc2_weight,
    fc2_bias,
    cotangent,
):
    seqs_here, local_len, width = hidden_in.shape
    token_rows = seqs_here * local_len
    seq_ranks = lax.axis_size("seq")
    seq_length = local_len * seq_ranks
    heads_here = H // seq_ranks
    columns = heads_here * 3 * HD
    fsdp_ranks = lax.axis_size("fsdp")
    fsdp_rank = lax.axis_index("fsdp")

    small = [ln1_gain, ln1_bias, qv_bias, dense_bias, ln2_gain, ln2_bias, fc1_bias, fc2_bias]
    gathered = lax.all_gather(jnp.concatenate(small), "fsdp", axis=0).astype(jnp.float32)
    vectors, place = [], 0
    for part in small:
        size = part.shape[0]
        vectors.append(gathered[:, place : place + size].reshape(-1))
        place += size
    gain_one, shift_one, pair_bias, bias_dense, gain_two, shift_two, bias_up, bias_down = vectors

    head_columns = lax.dynamic_slice_in_dim(
        qkv_weight, lax.axis_index("seq") * columns, columns, 1
    )
    w_mixed = lax.all_gather(head_columns, "fsdp", axis=0, tiled=True)
    w_dense = lax.all_gather(dense_weight, "fsdp", axis=0, tiled=True)
    w_up = lax.all_gather(fc1_weight, "fsdp", axis=0, tiled=True)
    w_down = lax.all_gather(fc2_weight, "fsdp", axis=0, tiled=True)

    hidden_all = jnp.moveaxis(gather(hidden_in, "seq"), 0, 1).reshape(-1, width)
    normed = norm_layer(hidden_all.astype(jnp.float32), gain_one, shift_one).astype(jnp.bfloat16)
    mixed = (
        jnp.dot(normed, w_mixed, preferred_element_type=jnp.float32)
        + local_columns(pair_bias, heads_here)
    ).astype(jnp.bfloat16)
    mixed = mixed.reshape(seqs_here, seq_length, columns)
    head_ids = lax.axis_index("seq") * heads_here + jnp.arange(heads_here, dtype=jnp.int32)
    slopes = 2.0 ** (-8.0 * (head_ids + 1).astype(jnp.float32) / H)
    doc_starts = doc_starts_of(lengths, seq_length)
    attended_heads, log_sums = attend_forward(mixed, doc_starts, slopes)
    attended = lax.all_to_all(
        attended_heads, "seq", split_axis=1, concat_axis=2, tiled=True
    ).reshape(token_rows, width)

    tokens = hidden_in.reshape(token_rows, width).astype(jnp.float32)
    hidden = tokens + jnp.dot(attended, w_dense, preferred_element_type=jnp.float32) + bias_dense
    normed_two_f, norm_pull_two = jax.vjp(norm_layer, hidden, gain_two, shift_two)
    normed_two = normed_two_f.astype(jnp.bfloat16)
    activation = jnp.dot(normed_two, w_up, preferred_element_type=jnp.float32) + bias_up
    gelu_f, gelu_pull = jax.vjp(gelu_tanh, activation)
    gelu_out = gelu_f.astype(jnp.bfloat16)
    grad_out = cotangent.reshape(token_rows, width)
    grad_out_f = grad_out.astype(jnp.float32)

    core_first = labels_of("fsdp")[:1]
    far = labels_of("fsdp")[1:]
    g_w_down = contract_rows(gelu_out, grad_out).astype(jnp.bfloat16)
    g_w_down = reduce_rows(
        g_w_down, core_first + far + labels_of("seq", "dp"), ("fsdp", "seq", "dp")
    )
    result = hidden + jnp.dot(gelu_out, w_down, preferred_element_type=jnp.float32) + bias_down
    output = result.astype(jnp.bfloat16).reshape(seqs_here, local_len, width)

    g_bias_down = jnp.sum(grad_out_f, axis=0)
    grad_gelu = contract_cols(grad_out, w_down)
    grad_act = gelu_pull(grad_gelu)[0]
    g_bias_up = jnp.sum(grad_act, axis=0)
    grad_act_low = grad_act.astype(jnp.bfloat16)
    g_w_up = contract_rows(normed_two, grad_act_low).astype(jnp.bfloat16)
    g_w_up = reduce_rows(
        g_w_up, core_first + labels_of("seq") + far + labels_of("dp"), ("fsdp", "seq", "dp")
    )
    grad_normed_two = contract_cols(grad_act_low, w_up)
    grad_hidden_norm, g_gain_two, g_shift_two = norm_pull_two(grad_normed_two)
    grad_hidden = grad_out_f + grad_hidden_norm
    g_bias_dense = jnp.sum(grad_hidden, axis=0)
    grad_hidden_low = grad_hidden.astype(jnp.bfloat16)
    grad_attended = contract_cols(grad_hidden_low, w_dense).astype(jnp.bfloat16)
    grad_heads = lax.all_to_all(
        grad_attended.reshape(seqs_here, local_len, width),
        "seq",
        split_axis=2,
        concat_axis=1,
        tiled=True,
    )
    g_w_dense = contract_rows(attended, grad_hidden_low).astype(jnp.bfloat16)
    g_w_dense = reduce_rows(
        g_w_dense, core_first + far + labels_of("seq", "dp"), ("fsdp", "seq", "dp")
    )
    early = sum_all(
        pack([g_gain_two, g_shift_two, g_bias_up, g_bias_down, g_bias_dense]),
        ("fsdp", "seq", "dp"),
    ).reshape(-1)

    grad_mixed = attend_backward(mixed, grad_heads, log_sums, doc_starts, slopes)
    grad_mixed = grad_mixed.reshape(-1, columns)
    partial = contract_cols(grad_mixed, w_mixed).astype(jnp.bfloat16)
    seq_labels = [("seq", step) for step in reversed(steps_of("seq"))]
    partial = partial.reshape((seqs_here,) + (2,) * len(seq_labels) + (local_len, width))
    for label in list(seq_labels):
        partial = halve(partial, label[0], label[1], 1)
    g_w_mixed = contract_rows(normed, grad_mixed).astype(jnp.bfloat16)
    g_w_mixed = reduce_rows(g_w_mixed, core_first + far + labels_of("dp"), ("fsdp", "dp"))
    grad_normed = partial.reshape(token_rows, width).astype(jnp.float32)
    norm_pull_one = jax.vjp(norm_layer, tokens, gain_one, shift_one)[1]
    grad_token_norm, g_gain_one, g_shift_one = norm_pull_one(grad_normed)
    grad_input = (
        (grad_hidden + grad_token_norm)
        .astype(jnp.bfloat16)
        .reshape(seqs_here, local_len, width)
    )
    bias_total = jnp.sum(grad_mixed, axis=0, dtype=jnp.float32).reshape(heads_here, 3, HD)
    pair_total = jnp.concatenate([bias_total[:, :1], bias_total[:, 2:]], axis=1)
    g_pair_bias = lax.dynamic_update_slice_in_dim(
        jnp.zeros((H, 2, HD), jnp.float32), pair_total, lax.axis_index("seq") * heads_here, 0
    ).reshape(2 * H * HD)
    late = sum_all(pack([g_gain_one, g_shift_one, g_pair_bias]), ("fsdp", "seq", "dp"))
    late = late.reshape(-1)

    def own(packed, start, size):
        here = size // fsdp_ranks
        return lax.dynamic_slice_in_dim(packed, start + fsdp_rank * here, here, 0)

    hidden_units = bias_up.shape[0]
    g_gain_two = own(early, 0, width)
    g_shift_two = own(early, width, width)
    g_bias_up = own(early, 2 * width, hidden_units)
    g_bias_down = own(early, 2 * width + hidden_units, width)
    g_bias_dense = own(early, 3 * width + hidden_units, width)
    g_gain_one = own(late, 0, width)
    g_shift_one = own(late, width, width)
    g_pair_bias = own(late, 2 * width, 2 * H * HD)

    g_w_down = spread_rows(g_w_down, ("seq", "dp")).astype(jnp.float32)
    g_w_up = spread_rows(g_w_up, ("seq", "dp")).astype(jnp.float32)
    g_w_dense = spread_rows(g_w_dense, ("seq", "dp")).astype(jnp.float32)
    g_w_mixed = spread_rows(g_w_mixed, ("dp",))
    g_w_mixed = jnp.moveaxis(gather(g_w_mixed, "seq"), 0, 1).astype(jnp.float32)
    g_w_mixed = g_w_mixed.reshape(-1, seq_ranks * columns)
    return (
        output,
        grad_input,
        g_gain_one,
        g_shift_one,
        g_w_mixed,
        g_pair_bias,
        g_w_dense,
        g_bias_dense,
        g_gain_two,
        g_shift_two,
        g_w_up,
        g_bias_up,
        g_w_down,
        g_bias_down,
    )


def solution(mesh):
    placed = (
        P(("dp", "fsdp"), "seq", None),
        P(("dp", "fsdp"), None),
        P("fsdp"),
        P("fsdp"),
        P("fsdp", None),
        P("fsdp"),
        P("fsdp", None),
        P("fsdp"),
        P("fsdp"),
        P("fsdp"),
        P("fsdp", None),
        P("fsdp"),
        P("fsdp", None),
        P("fsdp"),
        P(("dp", "fsdp"), "seq", None),
    )
    return jax.shard_map(
        per_device,
        mesh=mesh,
        in_specs=placed,
        out_specs=(
            P(("dp", "fsdp"), "seq", None),
            P(("dp", "fsdp"), "seq", None),
            P("fsdp"),
            P("fsdp"),
            P("fsdp", None),
            P("fsdp"),
            P("fsdp", None),
            P("fsdp"),
            P("fsdp"),
            P("fsdp"),
            P("fsdp", None),
            P("fsdp"),
            P("fsdp", None),
            P("fsdp"),
        ),
        check_vma=False,
    )
```

time: 1060 us -> 597 us (0.56)
  waiting for transfers between devices: 493 us -> 251 us
  blocking collectives: 175 us -> 5.7 us
  matrix products: 204 us -> 82.1 us
  starting transfers between devices: 13 us -> 61.8 us
  Pallas kernels: 0 us -> 47.2 us
  other arithmetic: 72.2 us -> 57.7 us
    reduce_scatter x4 -> x0, waiting for transfers between devices: 290 us -> none  [the longest x1 118 us: per_device(): lax.psum_scatter(g_w_up, ('fsdp', 'seq'), scatter_dimension=0, tiled=True)]
    ppermute x0 -> x43, waiting for transfers between devices: none -> 188 us  [swap(): return lax.ppermute(value, axis, pairs)]
    psum x1 -> x0, waiting for transfers between devices: 123 us -> none  [per_device(): lax.psum(attn_part[2].astype(jnp.bfloat16), 'dp').astype(jnp.float32)]
    dot_general x16 -> x2, matrix products: 107 us -> 11.1 us  [the longest x1 7.85 us: per_device(): jnp.dot(normed_two, w_up, preferred_element_type=jnp.float32) + bias_up]
    all_gather x17 -> x1, blocking collectives: 83.1 us -> 5.7 us  [per_device(): lax.all_gather(jnp.concatenate(small), 'fsdp', axis=0).astype(jnp.float32)]
    all_to_all x1 -> x0, blocking collectives: 54.9 us -> none  [per_device(): lax.all_to_all(grad_mixed_heads, 'seq', split_axis=1, concat_axis=2, tile...]
    ppermute x0 -> x43, starting transfers between devices: none -> 52.6 us  [swap(): return lax.ppermute(value, axis, pairs)]
    pallas_call x0 -> x2, Pallas kernels: none -> 47.2 us  [the longest x1 26.7 us: attend_backward(): pl.pallas_call(functools.partial(attend_backward_kernel, block=min(ROWS,...]
  transfers between devices with their start and end apart: 15 -> 49, of which waited for: 7 -> 27; matrix products, arithmetic and copies ran while one was open for 29% -> 25% of each run, Pallas kernels for 0% -> 8%
where the time goes in v1:
time: 597 us; the launch traced here: 593 us
  waiting for transfers between devices  251 us (42%)
  matrix products  82.1 us (14%)
  local copies, waits for them, and re-layouts  72.5 us (12%)
  starting transfers between devices  61.8 us (10%)
  other arithmetic  57.7 us (10%)
  Pallas kernels  47.2 us (8%)
  between operations  15 us (3%)
    ppermute x43, waiting for transfers between devices, swap(): return lax.ppermute(value, axis, pairs)  188 us
    ppermute x43, starting transfers between devices, swap(): return lax.ppermute(value, axis, pairs)  52.6 us
    all_gather x1, waiting for transfers between devices, per_device(): w_down = lax.all_gather(fc2_weight, 'fsdp', axis=0, tiled=True)  39 us
    unnamed x94, local copies, waits for them, and re-layouts  31 us
    dot_general x4, matrix products, contract_cols(): lax.dot_general(left_side, right_side, (((1,), (1,)), ((), ())), preferre...  29.1 us
    pallas_call x1, Pallas kernels, attend_backward(): pl.pallas_call(functools.partial(attend_backward_kernel, block=min(ROWS,...  26.7 us
    dot_general x4, matrix products, contract_rows(): lax.dot_general(left_side, right_side, (((0,), (0,)), ((), ())), preferre...  23.8 us
    dynamic_slice x8, local copies, waits for them, and re-layouts, pick(): return lax.dynamic_index_in_dim(value, index, dim, keepdims=False)  21 us
  transfers between devices with their start and end apart: 49, of which 27 were waited for; matrix products, arithmetic and copies ran while one was open for 25% of the time, Pallas kernels for 8%

profile of v1, /device:TPU:0, one launch (start us, length us, event | category | flops | bytes accessed | tf_op | source)
XLA Modules:
  0.0 593.2 jit_solution(7566591584177022450)
XLA Ops:
  11.7 3.0 collective-permute-start
  16.5 5.7 all-gather
  23.1 14.9 %collective-permute-done = bf16[1,1,512,1024]{3,2,1,0:T(8,128)(2,1)S(1)} collective-permute-done((bf16[1,1,512,1024]{3,2,1,0:T(8,128)(2,1)S(1)}, bf16[1,1,512,1024]{3,2,1,0:T(8,128)(2,1)S(1)}, u32[]{:S(2)}, u32[]{:S(2)}) %collective-permute-start) | collective-permute-done | bytes 1048608 | tf_op jit(solution)/shard_map/ppermute | solution.py:57
  39.6 3.4 fusion.12
  43.0 5.9 fusion.13.mixed_ref
  49.0 20.5 %shard_map.254 = (bf16[1,1024,512]{2,1,0:T(8,128)(2,1)S(1)}, f32[1,4,2,1024]{3,2,1,0:T(2,128)S(1)}) custom-call(s32[1,1,1024]{2,1,0:T(1,128)S(1)} %bitcast.341, f32[8]{0:T(128)S(1)} %multiply_power_fusion.slopes_ref, bf16[1,1024,1536]{2,1,0:T(8,128)(2,1)S(1)} %fusion.13.mixed_ref), custom_call_target="tpu_custom_call" | custom-call | flops 4294967296 | bytes 6291456 | tf_op jit(solution)/shard_map/pallas_call | solution.py:219
  69.5 2.9 copy.131
  72.9 9.3 %reduce.7 = bf16[1024,512]{1,0:T(8,128)(2,1)} reduce(bf16[1024,1,512]{2,1,0:T(2,128)(2,1)} %bitcast.359, bf16[]{:T(256)} %broadcast.454), dimensions={1}, to_apply=%bitcast.339.reduce_sub_computation | reduce | bytes 2097154
  82.2 2.6 reshape.1010
  84.9 4.4 all-to-all-start
  91.8 11.0 %all-to-all-done = bf16[2,2,131072]{2,1,0:T(2,128)(2,1)} async-done(((bf16[2,2,131072]{2,1,0:T(2,128)(2,1)}), bf16[2,2,131072]{2,1,0:T(2,128)(2,1)}, u32[]{:S(2)}, u32[]{:S(2)}) %all-to-all-start) | async-done | bytes 1048608 | tf_op jit(solution)/shard_map/all_to_all | solution.py:322
  102.8 2.9 reshape.1011
  108.9 3.3 fusion.75
  113.8 11.7 %all-gather.10.cloned.1.call-done = bf16[1024,4096]{1,0:T(8,128)(2,1)} async-done(((bf16[256,4096]{1,0:T(8,128)(2,1)}), bf16[1024,4096]{1,0:T(8,128)(2,1)}) %all-gather.10.cloned.1.call-update) | async-done | bytes 8388624 | tf_op jit(solution)/shard_map/all_gather | solution.py:308
  125.5 7.9 %fusion.68 = f32[512,4096]{1,0:T(8,128)S(1)} fusion(bf16[1024,4096]{1,0:T(8,128)(2,1)} %all-gather.10.cloned.1.call-done, f32[512,1024]{1,0:T(8,128)} %copy-done.4, f32[1024]{0:T(1024)S(1)} %bitcast.421, f32[1024]{0:T(1024)S(1)} %bitcast.414, f32[512]{0:T(512)S(1)} %fusion.63, f32[512]{0:T(512)S(1)} %broadcast_multiply_fusion.2), kind=kOutput, calls=%fused_computation.202 | convolution fusion | flops 4297588736 | bytes 18886656 | tf_op jit(solution)/shard_map/dot_general | solution.py:330
  133.4 4.2 copy-done.29
  137.5 8.7 %convolution_convert_fusion = bf16[4096,1024]{1,0:T(8,128)(2,1)} fusion(bf16[1,512,1024]{2,1,0:T(8,128)(2,1)S(1)} %copy-done.17, f32[512,4096]{1,0:T(8,128)S(1)} %fusion.68, f32[4096]{0:T(1024)S(1)} %bitcast.411), kind=kOutput, calls=%fused_computation.14 | convolution fusion | flops 4320133120 | bytes 17842176 | tf_op jit(solution)/shard_map/dot_general | solution.py:35
  146.2 39.0 %all-gather.12.cloned.1.call-done = bf16[4096,1024]{1,0:T(8,128)(2,1)} async-done(((bf16[1024,1024]{1,0:T(8,128)(2,1)}), bf16[4096,1024]{1,0:T(8,128)(2,1)}) %all-gather.12.cloned.1.call-update) | async-done | bytes 8388624 | tf_op jit(solution)/shard_map/all_gather | solution.py:309
  185.2 14.8 %fusion.76 = (f32[4096]{0:T(1024)S(1)}, bf16[512,4096]{1,0:T(8,128)(2,1)S(1)}) fusion(bf16[4096,1024]{1,0:T(8,128)(2,1)} %all-gather.12.cloned.1.call-done, bf16[1,512,1024]{2,1,0:T(8,128)(2,1)S(1)} %copy-done.17, f32[512,4096]{1,0:T(8,128)} %copy-done.29, f32[4096]{0:T(1024)S(1)} %bitcast.412), kind=kOutput, calls=%fused_computation.209 | convolution fusion | flops 4349489152 | bytes 22052864 | tf_op jit(solution)/shard_map/dot_general | solution.py:41
  200.0 7.4 %convolution_convert_fusion.1 = bf16[1024,4096]{1,0:T(8,128)(2,1)} fusion(bf16[512,4096]{1,0:T(8,128)(2,1)S(1)} %get-tuple-element.122, f32[512,1024]{1,0:T(8,128)S(1)} %copy-done.5, f32[1024]{0:T(1024)S(1)} %bitcast.422, f32[1024]{0:T(1024)S(1)} %bitcast.415, f32[512]{0:T(512)S(1)} %fusion.63, f32[512]{0:T(512)S(1)} %broadcast_multiply_fusion.2), kind=kOutput, calls=%fused_computation.15 | convolution fusion | flops 4301783040 | bytes 14692352 | tf_op jit(solution)/shard_map/dot_general | solution.py:35
  207.4 8.4 %multiply_reduce_fusion.1 = (f32[1024]{0:T(1024)S(1)}, f32[512]{0:T(512)S(1)}, f32[1024]{0:T(1024)S(1)}, f32[512,1024]{1,0:T(8,128)S(1)}) fusion(f32[512,1024]{1,0:T(8,128)S(1)} %copy-done.5, f32[512]{0:T(512)S(1)} %fusion.63, f32[512]{0:T(512)S(1)} %broadcast_multiply_fusion.2, f32[1024]{0:T(1024)S(1)} %bitcast.416, ...), kind=kOutput, calls=%fused_computation.78 | convolution fusion | flops 4299159040 | bytes 16795648 | tf_op jit(solution)/shard_map/dot_general | solution.py:41
  217.1 2.7 convolution_convert_fusion.3
  222.1 6.0 %copy.81 = bf16[1,512,1024]{1,0,2:T(2,128)(2,1)} copy(bf16[1,512,1024]{2,1,0:T(8,128)(2,1)} %fusion.42) | data formatting | bytes 2097152 | tf_op jit(solution)/shard_map/reshape | solution.py:361
  228.1 8.0 %reduce.8 = bf16[1024,512]{1,0:T(8,128)(2,1)S(1)} reduce(bf16[1024,1,512]{2,1,0:T(2,128)(2,1)} %bitcast.360, bf16[]{:T(256)} %broadcast.454), dimensions={1}, to_apply=%bitcast.310.reduce_sub_computation | reduce | bytes 2097154
  237.7 4.6 all-to-all-start.1
  242.3 2.7 constant_dynamic-slice_fusion.6
  246.3 6.7 %constant_dynamic-slice_fusion.4 = (bf16[2,1,2,2,2,32,4096]{6,5,4,3,2,1,0:T(8,128)(2,1)}, bf16[2,1,2,2,2,32,4096]{6,5,4,3,2,1,0:T(8,128)(2,1)S(1)}) fusion(bf16[2,2,2,2,2,32,4096]{6,5,4,3,2,1,0:T(8,128)(2,1)} %bitcast.358, s32[]{:T(128)S(6)} %select_n.410, s32[]{:T(128)S(6)} %select_n.411), kind=kLoop, calls=%fused_computation.166 | loop fusion | bytes 16777224 | tf_op jit(solution)/shard_map/jit(dynamic_index_in_dim)/dynamic_slice | solution.py:61
  255.6 3.4 constant_dynamic-slice_fusion.2
  259.0 2.7 copy.126
  261.9 12.2 %fusion.43 = bf16[1,512,1024]{2,1,0:T(8,128)(2,1)} fusion(f32[512,1024]{1,0:T(8,128)S(1)} %copy-done.6, bf16[4096,1024]{1,0:T(8,128)(2,1)} %all-gather.12.cloned.1.call-done, f32[1024]{0:T(1024)S(1)} %bitcast.420, f32[512,4096]{1,0:T(8,128)} %copy-done.29, f32[4096]{0:T(1024)S(1)} %bitcast.413), kind=kOutput, calls=%fused_computation.96 | convolution fusion | flops 4317511680 | bytes 19943424 | tf_op jit(solution)/shard_map/dot_general | solution.py:342
  274.1 3.1 reshape.1013
  277.2 2.8 copy.94
  281.6 26.7 %shard_map.255 = bf16[1,1024,1536]{2,1,0:T(8,128)(2,1)S(1)} custom-call(s32[1,1,1024]{2,1,0:T(1,128)S(1)} %bitcast.342, f32[8]{0:T(128)S(1)} %multiply_power_fusion.slopes_ref, bf16[1,1024,1536]{2,1,0:T(8,128)(2,1)} %copy-done.2, bf16[1,1024,512]{2,1,0:T(8,128)(2,1)S(1)} %bitcast.340, f32[1,4,2,1024]{3,2,1,0:T(2,128)S(1)} %get-tuple-element.17.sums_ref), custom_call_target="tpu_custom_call" | custom-call | flops 10737418240 | bytes 9437184 | tf_op jit(solution)/shard_map/pallas_call | solution.py:245
  308.3 3.7 fusion.38
  314.3 4.9 convolution_convert_fusion.2
  325.5 12.1 %collective-permute-done.1 = bf16[1,512,1024]{2,1,0:T(8,128)(2,1)} collective-permute-done((bf16[1,512,1024]{2,1,0:T(8,128)(2,1)S(1)}, bf16[1,512,1024]{2,1,0:T(8,128)(2,1)}, u32[]{:S(2)}, u32[]{:S(2)}) %collective-permute-start.1) | collective-permute-done | bytes 1048608 | tf_op jit(solution)/shard_map/ppermute | solution.py:57
  341.3 2.5 fusion.69
  345.9 3.2 collective-permute-done.3
  358.3 2.5 collective-permute-start.6
  363.3 3.6 collective-permute-done.24
  381.6 3.7 fusion.6
  385.7 6.3 %collective-permute-done.8 = bf16[2,2,64,1536]{3,2,0,1:T(8,128)(2,1)S(1)} collective-permute-done((bf16[2,2,64,1536]{3,2,0,1:T(8,128)(2,1)S(1)}, bf16[2,2,64,1536]{3,2,0,1:T(8,128)(2,1)S(1)}, u32[]{:S(2)}, u32[]{:S(2)}) %collective-permute-start.8) | collective-permute-done | bytes 786464 | tf_op jit(solution)/shard_map/ppermute | solution.py:57
  396.7 5.1 collective-permute-done.19
  401.8 2.8 collective-permute-start.20
  405.5 4.6 collective-permute-done.20
  410.1 3.3 collective-permute-done.10
  413.6 14.5 %collective-permute-done.28 = bf16[2,2,2,32,4096]{4,3,1,2,0:T(8,128)(2,1)S(1)} collective-permute-done((bf16[2,2,2,32,4096]{4,3,1,2,0:T(8,128)(2,1)S(1)}, bf16[2,2,2,32,4096]{4,3,1,2,0:T(8,128)(2,1)S(1)}, u32[]{:S(2)}, u32[]{:S(2)}) %collective-permute-start.28) | collective-permute-done | bytes 2097184 | tf_op jit(solution)/shard_map/ppermute | solution.py:57
  430.2 4.3 fusion.5
  437.5 17.6 %collective-permute-done.29 = bf16[2,2,32,4096]{3,2,0,1:T(8,128)(2,1)S(1)} collective-permute-done((bf16[2,2,32,4096]{3,2,0,1:T(8,128)(2,1)S(1)}, bf16[2,2,32,4096]{3,2,0,1:T(8,128)(2,1)S(1)}, u32[]{:S(2)}, u32[]{:S(2)}) %collective-permute-start.29) | collective-permute-done | bytes 1048608 | tf_op jit(solution)/shard_map/ppermute | solution.py:57
  457.6 29.8 %collective-permute-done.36 = bf16[2,2,2,128,1024]{4,3,1,2,0:T(8,128)(2,1)S(1)} collective-permute-done((bf16[2,2,2,128,1024]{4,3,1,2,0:T(8,128)(2,1)S(1)}, bf16[2,2,2,128,1024]{4,3,1,2,0:T(8,128)(2,1)S(1)}, u32[]{:S(2)}, u32[]{:S(2)}) %collective-permute-start.36) | collective-permute-done | bytes 2097184 | tf_op jit(solution)/shard_map/ppermute | solution.py:57
  489.1 3.0 collective-permute-start.31
  492.2 11.1 %collective-permute-done.37 = bf16[2,2,128,1024]{3,2,0,1:T(8,128)(2,1)S(1)} collective-permute-done((bf16[2,2,128,1024]{3,2,0,1:T(8,128)(2,1)S(1)}, bf16[2,2,128,1024]{3,2,0,1:T(8,128)(2,1)S(1)}, u32[]{:S(2)}, u32[]{:S(2)}) %collective-permute-start.37) | collective-permute-done | bytes 1048608 | tf_op jit(solution)/shard_map/ppermute | solution.py:57
  505.4 3.0 collective-permute-start.32
  508.5 18.1 %collective-permute-done.38 = bf16[2,128,1024]{2,1,0:T(8,128)(2,1)S(1)} collective-permute-done((bf16[2,128,1024]{2,1,0:T(8,128)(2,1)S(1)}, bf16[2,128,1024]{2,1,0:T(8,128)(2,1)S(1)}, u32[]{:S(2)}, u32[]{:S(2)}) %collective-permute-start.38) | collective-permute-done | bytes 524320 | tf_op jit(solution)/shard_map/ppermute | solution.py:57
  529.1 2.5 collective-permute-start.33
  531.6 4.7 collective-permute-done.39
  536.5 2.7 collective-permute-start.40
  539.3 8.6 %collective-permute-done.33 = bf16[2,32,4096]{2,1,0:T(8,128)(2,1)S(1)} collective-permute-done((bf16[2,32,4096]{2,1,0:T(8,128)(2,1)S(1)}, bf16[2,32,4096]{2,1,0:T(8,128)(2,1)S(1)}, u32[]{:S(2)}, u32[]{:S(2)}) %collective-permute-start.33) | collective-permute-done | bytes 524320 | tf_op jit(solution)/shard_map/ppermute | solution.py:57
  553.9 3.5 copy.85
  557.4 3.5 copy.92
  561.8 10.5 %collective-permute-done.34 = bf16[128,4096]{1,0:T(8,128)(2,1)S(1)} collective-permute-done((bf16[128,4096]{1,0:T(8,128)(2,1)S(1)}, bf16[128,4096]{1,0:T(8,128)(2,1)S(1)}, u32[]{:S(2)}, u32[]{:S(2)}) %collective-permute-start.34) | collective-permute-done | bytes 1048608 | tf_op jit(solution)/shard_map/ppermute | solution.py:57
  572.6 2.6 bitcast_convert_fusion.1
  575.3 8.2 %collective-permute-done.42 = bf16[512,1024]{1,0:T(8,128)(2,1)S(1)} collective-permute-done((bf16[512,1024]{1,0:T(8,128)(2,1)S(1)}, bf16[512,1024]{1,0:T(8,128)(2,1)S(1)}, u32[]{:S(2)}, u32[]{:S(2)}) %collective-permute-start.42) | collective-permute-done | bytes 1048608 | tf_op jit(solution)/shard_map/ppermute | solution.py:57
  583.9 2.6 bitcast_convert_fusion
  (272 shorter events, 95.4 us)
Async XLA Ops:
  7.2 35.8 %all-gather.6.cloned.1.call-start = ((), (), s32[]{:S(2)}) async-start(), calls=%async_computation.2 | async-start | bytes 3932160 | tf_op jit(solution)/shard_map/all_gather | solution.py:306
  9.5 99.3 %all-gather.8.cloned.1.call-start = ((), (), s32[]{:S(2)}) async-start(), calls=%async_computation.3 | async-start | bytes 2621440 | tf_op jit(solution)/shard_map/all_gather | solution.py:307
  10.3 4.8 copy-start.20
  10.3 5.1 copy-start.23
  10.4 5.3 copy-start.24
  10.4 5.5 copy-start.25
  10.4 5.7 copy-start.19
  10.4 5.9 copy-start.26
  10.4 11.8 %copy-start.28 = (s32[1,4]{1,0:T(1,128)S(1)}, s32[1,4]{1,0:T(1,128)}, u32[]{:S(2)}) copy-start(s32[1,4]{1,0:T(1,128)} %param.16) | copy-start | bytes 52
  10.4 115.1 %all-gather.10.cloned.1.call-start = ((), (), s32[]{:S(2)}) async-start(), calls=%async_computation.4 | async-start | bytes 10485760 | tf_op jit(solution)/shard_map/all_gather | solution.py:308
  11.2 174.1 %all-gather.12.cloned.1.call-start = ((), (), s32[]{:S(2)}) async-start(), calls=%async_computation.5 | async-start | bytes 10485760 | tf_op jit(solution)/shard_map/all_gather | solution.py:309
  11.7 26.2 %collective-permute-start = (bf16[1,1,512,1024]{3,2,1,0:T(8,128)(2,1)S(1)}, bf16[1,1,512,1024]{3,2,1,0:T(8,128)(2,1)S(1)}, u32[]{:S(2)}, u32[]{:S(2)}) collective-permute-start(bf16[1,1,512,1024]{3,2,1,0:T(8,128)(2,1)S(1)} %bitcast.343), channel_id=1, source_target_pairs={{0,1},{1,0},{2,3},{3,2},{4,5},{5,4},{6,7},{7,6},{8,9},{9,8},{10,11... | collective-permute-start | bytes 3145736 | tf_op jit(solution)/shard_map/ppermute | solution.py:57
  49.0 20.5 %copy-start.2 = (bf16[1,1024,1536]{2,1,0:T(8,128)(2,1)}, bf16[1,1024,1536]{2,1,0:T(8,128)(2,1)S(1)}, u32[]{:S(2)}) copy-start(bf16[1,1024,1536]{2,1,0:T(8,128)(2,1)S(1)} %fusion.13.mixed_ref) | copy-start | bytes 9437188
  84.9 17.9 %all-to-all-start = ((bf16[2,2,131072]{2,1,0:T(2,128)(2,1)}), bf16[2,2,131072]{2,1,0:T(2,128)(2,1)}, u32[]{:S(2)}, u32[]{:S(2)}) async-start(bf16[2,2,131072]{2,1,0:T(2,128)(2,1)} %reshape.1010), calls=%async_computation | async-start | bytes 2097152 | tf_op jit(solution)/shard_map/all_to_all | solution.py:322
  125.5 12.0 %copy-start.17 = (bf16[1,512,1024]{2,1,0:T(8,128)(2,1)S(1)}, bf16[1,512,1024]{2,1,0:T(8,128)(2,1)}, u32[]{:S(2)}) copy-start(bf16[1,512,1024]{2,1,0:T(8,128)(2,1)} %param.29) | copy-start | bytes 3145732
  185.2 14.8 %copy-start.5 = (f32[512,1024]{1,0:T(8,128)S(1)}, f32[512,1024]{1,0:T(8,128)}, u32[]{:S(2)}) copy-start(f32[512,1024]{1,0:T(8,128)} %copy-done.4) | copy-start | bytes 6291460
  237.7 36.4 %all-to-all-start.1 = ((bf16[2,2,131072]{2,1,0:T(2,128)(2,1)}), bf16[2,2,131072]{2,1,0:T(2,128)(2,1)}, u32[]{:S(2)}, u32[]{:S(2)}) async-start(bf16[2,2,131072]{2,1,0:T(2,128)(2,1)} %reshape.1012), calls=%async_computation.1 | async-start | bytes 2097152 | tf_op jit(solution)/shard_map/all_to_all | solution.py:360
  245.0 10.5 %slice-start = ((s8[8388608]{0:T(1024)(128)(4,1)}), s8[4194304]{0:T(1024)(128)(4,1)S(1)}, s32[]{:S(2)}) async-start(s8[8388608]{0:T(1024)(128)(4,1)} %bitcast.355), calls=%async_computation.6 | async-start | bytes 8388608
  246.1 76.4 %collective-permute-start.14 = (bf16[2,2,2,2,32,1024]{5,4,2,3,1,0:T(8,128)(2,1)}, bf16[2,2,2,2,32,1024]{5,4,2,3,1,0:T(8,128)(2,1)}, u32[]{:S(2)}, u32[]{:S(2)}) collective-permute-start(bf16[2,2,2,2,32,1024]{5,4,2,3,1,0:T(8,128)(2,1)} %bitcast.337), channel_id=1, source_target_pairs={{0,2},{2,0},{4,6},{6,4},{1,3},{3,1},{5,7},{7,5},{8,10},{10,8},{12,... | collective-permute-start | bytes 3145736 | tf_op jit(solution)/shard_map/ppermute | solution.py:57
  246.3 9.2 %slice-start.1 = ((s8[8388608]{0:T(1024)(128)(4,1)}), s8[4194304]{0:T(1024)(128)(4,1)S(1)}, s32[]{:S(2)}) async-start(s8[8388608]{0:T(1024)(128)(4,1)} %bitcast.355), calls=%async_computation.7 | async-start | bytes 8388608
  255.3 124.9 %collective-permute-start.27 = (bf16[2,2,2,2,32,4096]{5,4,2,3,0,1:T(8,128)(2,1)}, bf16[2,2,2,2,32,4096]{5,4,2,3,0,1:T(8,128)(2,1)}, u32[]{:S(2)}, u32[]{:S(2)}) collective-permute-start(bf16[2,2,2,2,32,4096]{5,4,2,3,0,1:T(8,128)(2,1)} %bitcast.335), channel_id=1, source_target_pairs={{0,2},{2,0},{4,6},{6,4},{1,3},{3,1},{5,7},{7,5},{8,10},{10,8},{12,... | collective-permute-start | bytes 12582920 | tf_op jit(solution)/shard_map/ppermute | solution.py:57
  261.6 167.8 %collective-permute-start.35 = (bf16[2,2,2,2,128,1024]{5,4,2,3,1,0:T(8,128)(2,1)}, bf16[2,2,2,2,128,1024]{5,4,2,3,1,0:T(8,128)(2,1)}, u32[]{:S(2)}, u32[]{:S(2)}) collective-permute-start(bf16[2,2,2,2,128,1024]{5,4,2,3,1,0:T(8,128)(2,1)} %bitcast.334), channel_id=1, source_target_pairs={{0,2},{2,0},{4,6},{6,4},{1,3},{3,1},{5,7},{7,5},{8,10},{10,8},{12,... | collective-permute-start | bytes 12582920 | tf_op jit(solution)/shard_map/ppermute | solution.py:57
  281.6 26.7 %copy-start.27 = (bf16[1024,1536]{1,0:T(8,128)(2,1)S(1)}, bf16[1024,1536]{1,0:T(8,128)(2,1)}, u32[]{:S(2)}) copy-start(bf16[1024,1536]{1,0:T(8,128)(2,1)} %all-gather.6.cloned.1.call-done) | copy-start | bytes 9437188
  312.0 7.3 %copy-start.15 = (bf16[1024,1024]{1,0:T(8,128)(2,1)}, bf16[1024,1024]{1,0:T(8,128)(2,1)S(1)}, u32[]{:S(2)}) copy-start(bf16[1024,1024]{1,0:T(8,128)(2,1)S(1)} %fusion.38) | copy-start | bytes 6291460
  312.1 25.5 %collective-permute-start.1 = (bf16[1,512,1024]{2,1,0:T(8,128)(2,1)S(1)}, bf16[1,512,1024]{2,1,0:T(8,128)(2,1)}, u32[]{:S(2)}, u32[]{:S(2)}) collective-permute-start(bf16[1,512,1024]{2,1,0:T(8,128)(2,1)S(1)} %dynamic-slice_bitcast_fusion.4), channel_id=1, source_target_pairs={{0,1},{1,0},{2,3},{3,2},{4,5},{5,4},{6,7},{7,6},{8,9},{9,8},{10,11... | collective-permute-start | bytes 3145736 | tf_op jit(solution)/shard_map/ppermute | solution.py:57
  322.2 57.2 %collective-permute-start.7 = (bf16[2,2,2,64,1536]{4,3,1,2,0:T(8,128)(2,1)S(1)}, bf16[2,2,2,64,1536]{4,3,1,2,0:T(8,128)(2,1)S(1)}, u32[]{:S(2)}, u32[]{:S(2)}) collective-permute-start(bf16[2,2,2,64,1536]{4,3,1,2,0:T(8,128)(2,1)S(1)} %bitcast.382), channel_id=1, source_target_pairs={{0,2},{2,0},{4,6},{6,4},{1,3},{3,1},{5,7},{7,5},{8,10},{10,8},{12,... | collective-permute-start | bytes 4718600 | tf_op jit(solution)/shard_map/ppermute | solution.py:57
  323.3 14.3 %copy-start.16 = (bf16[1024,1024]{1,0:T(8,128)(2,1)S(1)}, bf16[1024,1024]{1,0:T(8,128)(2,1)}, u32[]{:S(2)}) copy-start(bf16[1024,1024]{1,0:T(8,128)(2,1)} %copy-done.15) | copy-start | bytes 6291460
  325.1 20.2 %collective-permute-start.15 = (bf16[2,2,2,32,1024]{4,3,1,2,0:T(8,128)(2,1)S(1)}, bf16[2,2,2,32,1024]{4,3,1,2,0:T(8,128)(2,1)S(1)}, u32[]{:S(2)}, u32[]{:S(2)}) collective-permute-start(bf16[2,2,2,32,1024]{4,3,1,2,0:T(8,128)(2,1)S(1)} %dynamic-slice_bitcast_fusion.8), channel_id=1, source_target_pairs={{0,4},{2,6},{4,0},{6,2},{1,5},{3,7},{5,1},{7,3},{8,12},{10,14},{12... | collective-permute-start | bytes 1572872 | tf_op jit(solution)/shard_map/ppermute | solution.py:57
  343.9 1.2 collective-permute-start.2
  345.1 5.7 collective-permute-start.22
  345.3 3.8 collective-permute-start.3
  349.1 3.7 collective-permute-start.4
  350.9 7.5 %collective-permute-start.23 = (f32[64,128]{1,0:T(8,128)S(1)}, f32[64,128]{1,0:T(8,128)S(1)}, u32[]{:S(2)}, u32[]{:S(2)}) collective-permute-start(f32[64,128]{1,0:T(8,128)S(1)} %bitcast_add_fusion), channel_id=1, source_target_pairs={{0,4},{2,6},{4,0},{6,2},{1,5},{3,7},{5,1},{7,3},{8,12},{10,14},{12... | collective-permute-start | bytes 98312 | tf_op jit(solution)/shard_map/ppermute | solution.py:57
  352.8 3.7 collective-permute-start.5
  356.6 16.7 %collective-permute-start.16 = (bf16[2,2,32,1024]{3,2,0,1:T(8,128)(2,1)S(1)}, bf16[2,2,32,1024]{3,2,0,1:T(8,128)(2,1)S(1)}, u32[]{:S(2)}, u32[]{:S(2)}) collective-permute-start(bf16[2,2,32,1024]{3,2,0,1:T(8,128)(2,1)S(1)} %dynamic-slice_bitcast_fusion.12), channel_id=1, source_target_pairs={{0,1},{1,0},{2,3},{3,2},{4,5},{5,4},{6,7},{7,6},{8,9},{9,8},{10,11... | collective-permute-start | bytes 786440 | tf_op jit(solution)/shard_map/ppermute | solution.py:57
  358.3 4.7 collective-permute-start.6
  363.0 3.9 collective-permute-start.24
  367.0 4.3 collective-permute-start.25
  371.2 6.0 %collective-permute-start.26 = (f32[64,128]{1,0:T(8,128)S(1)}, f32[64,128]{1,0:T(8,128)S(1)}, u32[]{:S(2)}, u32[]{:S(2)}) collective-permute-start(f32[64,128]{1,0:T(8,128)S(1)} %add.439), channel_id=1, source_target_pairs={{0,16},{8,24},{16,0},{24,8},{1,17},{9,25},{17,1},{25,9},{2,18},{10... | collective-permute-start | bytes 98312 | tf_op jit(solution)/shard_map/ppermute | solution.py:57
  373.4 5.1 collective-permute-start.17
  378.5 15.5 %collective-permute-start.18 = (bf16[32,1024]{1,0:T(8,128)(2,1)S(1)}, bf16[32,1024]{1,0:T(8,128)(2,1)S(1)}, u32[]{:S(2)}, u32[]{:S(2)}) collective-permute-start(bf16[32,1024]{1,0:T(8,128)(2,1)S(1)} %dynamic-slice_bitcast_fusion.15), channel_id=1, source_target_pairs={{0,16},{8,24},{16,0},{24,8},{1,17},{9,25},{17,1},{25,9},{2,18},{10... | collective-permute-start | bytes 196616 | tf_op jit(solution)/shard_map/ppermute | solution.py:57
  379.9 12.1 %collective-permute-start.8 = (bf16[2,2,64,1536]{3,2,0,1:T(8,128)(2,1)S(1)}, bf16[2,2,64,1536]{3,2,0,1:T(8,128)(2,1)S(1)}, u32[]{:S(2)}, u32[]{:S(2)}) collective-permute-start(bf16[2,2,64,1536]{3,2,0,1:T(8,128)(2,1)S(1)} %dynamic-slice_bitcast_fusion.5), channel_id=1, source_target_pairs={{0,4},{2,6},{4,0},{6,2},{1,5},{3,7},{5,1},{7,3},{8,12},{10,14},{12... | collective-permute-start | bytes 2359304 | tf_op jit(solution)/shard_map/ppermute | solution.py:57
  385.6 42.5 %collective-permute-start.28 = (bf16[2,2,2,32,4096]{4,3,1,2,0:T(8,128)(2,1)S(1)}, bf16[2,2,2,32,4096]{4,3,1,2,0:T(8,128)(2,1)S(1)}, u32[]{:S(2)}, u32[]{:S(2)}) collective-permute-start(bf16[2,2,2,32,4096]{4,3,1,2,0:T(8,128)(2,1)S(1)} %dynamic-slice_bitcast_fusion.1), channel_id=1, source_target_pairs={{0,1},{1,0},{2,3},{3,2},{4,5},{5,4},{6,7},{7,6},{8,9},{9,8},{10,11... | collective-permute-start | bytes 6291464 | tf_op jit(solution)/shard_map/ppermute | solution.py:57
  392.2 12.4 %collective-permute-start.9 = (bf16[2,64,1536]{2,1,0:T(8,128)(2,1)S(1)}, bf16[2,64,1536]{2,1,0:T(8,128)(2,1)S(1)}, u32[]{:S(2)}, u32[]{:S(2)}) collective-permute-start(bf16[2,64,1536]{2,1,0:T(8,128)(2,1)S(1)} %dynamic-slice_bitcast_fusion.9), channel_id=1, source_target_pairs={{0,8},{8,0},{16,24},{24,16},{1,9},{9,1},{17,25},{25,17},{2,10},{10... | collective-permute-start | bytes 1179656 | tf_op jit(solution)/shard_map/ppermute | solution.py:57
  394.1 7.7 %collective-permute-start.19 = (bf16[32,1024]{1,0:T(8,128)(2,1)S(1)}, bf16[32,1024]{1,0:T(8,128)(2,1)S(1)}, u32[]{:S(2)}, u32[]{:S(2)}) collective-permute-start(bf16[32,1024]{1,0:T(8,128)(2,1)S(1)} %fusion.62), channel_id=1, source_target_pairs={{0,16},{8,24},{16,0},{24,8},{1,17},{9,25},{17,1},{25,9},{2,18},{10... | collective-permute-start | bytes 196616 | tf_op jit(solution)/shard_map/ppermute | solution.py:57
  401.8 8.2 %collective-permute-start.20 = (bf16[2,32,1024]{2,1,0:T(8,128)(2,1)S(1)}, bf16[2,32,1024]{2,1,0:T(8,128)(2,1)S(1)}, u32[]{:S(2)}, u32[]{:S(2)}) collective-permute-start(bf16[2,32,1024]{2,1,0:T(8,128)(2,1)S(1)} %maximum_select_fusion.16), channel_id=1, source_target_pairs={{0,8},{8,0},{16,24},{24,16},{1,9},{9,1},{17,25},{25,17},{2,10},{10... | collective-permute-start | bytes 393224 | tf_op jit(solution)/shard_map/ppermute | solution.py:57
  404.7 8.7 %collective-permute-start.10 = (bf16[64,1536]{1,0:T(8,128)(2,1)S(1)}, bf16[64,1536]{1,0:T(8,128)(2,1)S(1)}, u32[]{:S(2)}, u32[]{:S(2)}) collective-permute-start(bf16[64,1536]{1,0:T(8,128)(2,1)S(1)} %dynamic-slice_bitcast_fusion.13), channel_id=1, source_target_pairs={{0,16},{8,24},{16,0},{24,8},{1,17},{9,25},{17,1},{25,9},{2,18},{10... | collective-permute-start | bytes 589832 | tf_op jit(solution)/shard_map/ppermute | solution.py:57
  410.1 138.2 %collective-permute-start.21 = (bf16[128,1024]{1,0:T(8,128)(2,1)S(1)}, bf16[128,1024]{1,0:T(8,128)(2,1)S(1)}, u32[]{:S(2)}, u32[]{:S(2)}) collective-permute-start(bf16[128,1024]{1,0:T(8,128)(2,1)S(1)} %bitcast.385), channel_id=1, source_target_pairs={{0,1},{1,0},{2,3},{3,2},{4,5},{5,4},{6,7},{7,6},{8,9},{9,8},{10,11... | collective-permute-start | bytes 786440 | tf_op jit(solution)/shard_map/ppermute | solution.py:57
  413.5 22.1 %collective-permute-start.11 = (bf16[64,1536]{1,0:T(8,128)(2,1)S(1)}, bf16[64,1536]{1,0:T(8,128)(2,1)S(1)}, u32[]{:S(2)}, u32[]{:S(2)}) collective-permute-start(bf16[64,1536]{1,0:T(8,128)(2,1)S(1)} %fusion.60), channel_id=1, source_target_pairs={{0,16},{8,24},{16,0},{24,8},{1,17},{9,25},{17,1},{25,9},{2,18},{10... | collective-permute-start | bytes 589832 | tf_op jit(solution)/shard_map/ppermute | solution.py:57
  428.9 26.2 %collective-permute-start.29 = (bf16[2,2,32,4096]{3,2,0,1:T(8,128)(2,1)S(1)}, bf16[2,2,32,4096]{3,2,0,1:T(8,128)(2,1)S(1)}, u32[]{:S(2)}, u32[]{:S(2)}) collective-permute-start(bf16[2,2,32,4096]{3,2,0,1:T(8,128)(2,1)S(1)} %dynamic-slice_bitcast_fusion.3), channel_id=1, source_target_pairs={{0,4},{2,6},{4,0},{6,2},{1,5},{3,7},{5,1},{7,3},{8,12},{10,14},{12... | collective-permute-start | bytes 3145736 | tf_op jit(solution)/shard_map/ppermute | solution.py:57
  434.7 52.6 %collective-permute-start.36 = (bf16[2,2,2,128,1024]{4,3,1,2,0:T(8,128)(2,1)S(1)}, bf16[2,2,2,128,1024]{4,3,1,2,0:T(8,128)(2,1)S(1)}, u32[]{:S(2)}, u32[]{:S(2)}) collective-permute-start(bf16[2,2,2,128,1024]{4,3,1,2,0:T(8,128)(2,1)S(1)} %dynamic-slice_bitcast_fusion), channel_id=1, source_target_pairs={{0,4},{2,6},{4,0},{6,2},{1,5},{3,7},{5,1},{7,3},{8,12},{10,14},{12... | collective-permute-start | bytes 6291464 | tf_op jit(solution)/shard_map/ppermute | solution.py:57
  435.7 21.5 %collective-permute-start.12 = (bf16[2,64,1536]{2,1,0:T(8,128)(2,1)S(1)}, bf16[2,64,1536]{2,1,0:T(8,128)(2,1)S(1)}, u32[]{:S(2)}, u32[]{:S(2)}) collective-permute-start(bf16[2,64,1536]{2,1,0:T(8,128)(2,1)S(1)} %maximum_select_fusion.13), channel_id=1, source_target_pairs={{0,8},{8,0},{16,24},{24,16},{1,9},{9,1},{17,25},{25,17},{2,10},{10... | collective-permute-start | bytes 1179656 | tf_op jit(solution)/shard_map/ppermute | solution.py:57
  455.4 33.6 %collective-permute-start.30 = (bf16[2,32,4096]{2,1,0:T(8,128)(2,1)S(1)}, bf16[2,32,4096]{2,1,0:T(8,128)(2,1)S(1)}, u32[]{:S(2)}, u32[]{:S(2)}) collective-permute-start(bf16[2,32,4096]{2,1,0:T(8,128)(2,1)S(1)} %dynamic-slice_bitcast_fusion.7), channel_id=1, source_target_pairs={{0,8},{8,0},{16,24},{24,16},{1,9},{9,1},{17,25},{25,17},{2,10},{10... | collective-permute-start | bytes 1572872 | tf_op jit(solution)/shard_map/ppermute | solution.py:57
  457.2 94.6 %collective-permute-start.13 = (bf16[1,256,1536]{2,1,0:T(8,128)(2,1)S(1)}, bf16[1,256,1536]{2,1,0:T(8,128)(2,1)S(1)}, u32[]{:S(2)}, u32[]{:S(2)}) collective-permute-start(bf16[1,256,1536]{2,1,0:T(8,128)(2,1)S(1)} %bitcast.369), channel_id=1, source_target_pairs={{0,1},{1,0},{2,3},{3,2},{4,5},{5,4},{6,7},{7,6},{8,9},{9,8},{10,11... | collective-permute-start | bytes 2359304 | tf_op jit(solution)/shard_map/ppermute | solution.py:57
  488.4 14.9 %collective-permute-start.37 = (bf16[2,2,128,1024]{3,2,0,1:T(8,128)(2,1)S(1)}, bf16[2,2,128,1024]{3,2,0,1:T(8,128)(2,1)S(1)}, u32[]{:S(2)}, u32[]{:S(2)}) collective-permute-start(bf16[2,2,128,1024]{3,2,0,1:T(8,128)(2,1)S(1)} %dynamic-slice_bitcast_fusion.2), channel_id=1, source_target_pairs={{0,1},{1,0},{2,3},{3,2},{4,5},{5,4},{6,7},{7,6},{8,9},{9,8},{10,11... | collective-permute-start | bytes 3145736 | tf_op jit(solution)/shard_map/ppermute | solution.py:57
  489.1 16.2 %collective-permute-start.31 = (bf16[32,4096]{1,0:T(8,128)(2,1)S(1)}, bf16[32,4096]{1,0:T(8,128)(2,1)S(1)}, u32[]{:S(2)}, u32[]{:S(2)}) collective-permute-start(bf16[32,4096]{1,0:T(8,128)(2,1)S(1)} %dynamic-slice_bitcast_fusion.11), channel_id=1, source_target_pairs={{0,16},{8,24},{16,0},{24,8},{1,17},{9,25},{17,1},{25,9},{2,18},{10... | collective-permute-start | bytes 786440 | tf_op jit(solution)/shard_map/ppermute | solution.py:57
  503.7 22.8 %collective-permute-start.38 = (bf16[2,128,1024]{2,1,0:T(8,128)(2,1)S(1)}, bf16[2,128,1024]{2,1,0:T(8,128)(2,1)S(1)}, u32[]{:S(2)}, u32[]{:S(2)}) collective-permute-start(bf16[2,128,1024]{2,1,0:T(8,128)(2,1)S(1)} %dynamic-slice_bitcast_fusion.6), channel_id=1, source_target_pairs={{0,8},{8,0},{16,24},{24,16},{1,9},{9,1},{17,25},{25,17},{2,10},{10... | collective-permute-start | bytes 1572872 | tf_op jit(solution)/shard_map/ppermute | solution.py:57
  505.4 23.6 %collective-permute-start.32 = (bf16[32,4096]{1,0:T(8,128)(2,1)S(1)}, bf16[32,4096]{1,0:T(8,128)(2,1)S(1)}, u32[]{:S(2)}, u32[]{:S(2)}) collective-permute-start(bf16[32,4096]{1,0:T(8,128)(2,1)S(1)} %fusion.56), channel_id=1, source_target_pairs={{0,16},{8,24},{16,0},{24,8},{1,17},{9,25},{17,1},{25,9},{2,18},{10... | collective-permute-start | bytes 786440 | tf_op jit(solution)/shard_map/ppermute | solution.py:57
  526.8 9.6 %collective-permute-start.39 = (bf16[128,1024]{1,0:T(8,128)(2,1)S(1)}, bf16[128,1024]{1,0:T(8,128)(2,1)S(1)}, u32[]{:S(2)}, u32[]{:S(2)}) collective-permute-start(bf16[128,1024]{1,0:T(8,128)(2,1)S(1)} %dynamic-slice_bitcast_fusion.10), channel_id=1, source_target_pairs={{0,16},{8,24},{16,0},{24,8},{1,17},{9,25},{17,1},{25,9},{2,18},{10... | collective-permute-start | bytes 786440 | tf_op jit(solution)/shard_map/ppermute | solution.py:57
  529.1 18.8 %collective-permute-start.33 = (bf16[2,32,4096]{2,1,0:T(8,128)(2,1)S(1)}, bf16[2,32,4096]{2,1,0:T(8,128)(2,1)S(1)}, u32[]{:S(2)}, u32[]{:S(2)}) collective-permute-start(bf16[2,32,4096]{2,1,0:T(8,128)(2,1)S(1)} %maximum_select_fusion.9), channel_id=1, source_target_pairs={{0,8},{8,0},{16,24},{24,16},{1,9},{9,1},{17,25},{25,17},{2,10},{10... | collective-permute-start | bytes 1572872 | tf_op jit(solution)/shard_map/ppermute | solution.py:57
  536.5 11.9 %collective-permute-start.40 = (bf16[128,1024]{1,0:T(8,128)(2,1)S(1)}, bf16[128,1024]{1,0:T(8,128)(2,1)S(1)}, u32[]{:S(2)}, u32[]{:S(2)}) collective-permute-start(bf16[128,1024]{1,0:T(8,128)(2,1)S(1)} %fusion.55), channel_id=1, source_target_pairs={{0,16},{8,24},{16,0},{24,8},{1,17},{9,25},{17,1},{25,9},{2,18},{10... | collective-permute-start | bytes 786440 | tf_op jit(solution)/shard_map/ppermute | solution.py:57
  548.0 24.3 %collective-permute-start.34 = (bf16[128,4096]{1,0:T(8,128)(2,1)S(1)}, bf16[128,4096]{1,0:T(8,128)(2,1)S(1)}, u32[]{:S(2)}, u32[]{:S(2)}) collective-permute-start(bf16[128,4096]{1,0:T(8,128)(2,1)S(1)} %bitcast.361), channel_id=1, source_target_pairs={{0,1},{1,0},{2,3},{3,2},{4,5},{5,4},{6,7},{7,6},{8,9},{9,8},{10,11... | collective-permute-start | bytes 3145736 | tf_op jit(solution)/shard_map/ppermute | solution.py:57
  549.3 11.8 %collective-permute-start.41 = (bf16[2,128,1024]{2,1,0:T(8,128)(2,1)}, bf16[2,128,1024]{2,1,0:T(8,128)(2,1)S(1)}, u32[]{:S(2)}, u32[]{:S(2)}) collective-permute-start(bf16[2,128,1024]{2,1,0:T(8,128)(2,1)} %maximum_select_fusion.11), channel_id=1, source_target_pairs={{0,8},{8,0},{16,24},{24,16},{1,9},{9,1},{17,25},{25,17},{2,10},{10... | collective-permute-start | bytes 1572872 | tf_op jit(solution)/shard_map/ppermute | solution.py:57
  561.2 22.3 %collective-permute-start.42 = (bf16[512,1024]{1,0:T(8,128)(2,1)S(1)}, bf16[512,1024]{1,0:T(8,128)(2,1)S(1)}, u32[]{:S(2)}, u32[]{:S(2)}) collective-permute-start(bf16[512,1024]{1,0:T(8,128)(2,1)S(1)} %bitcast.363), channel_id=1, source_target_pairs={{0,1},{1,0},{2,3},{3,2},{4,5},{5,4},{6,7},{7,6},{8,9},{9,8},{10,11... | collective-permute-start | bytes 3145736 | tf_op jit(solution)/shard_map/ppermute | solution.py:57
  (17 other events, 42.6 us)
Sparse Core Ops, SparseCore 0:
  10.2 31.2 all-gather.5
  43.0 22.5 all-gather.7
  67.2 58.2 all-gather.9
  126.9 58.2 all-gather.11

commit v2 on v1

--- a/solution.py
+++ b/solution.py
@@ -61,11 +61,13 @@
     return lax.dynamic_index_in_dim(value, index, dim, keepdims=False)
 
 
-def halve(value, axis, step, dim):
-    bit = bit_of(axis, step)
-    received = swap(pick(value, dim, 1 - bit), axis, step)
-    kept = pick(value, dim, bit).astype(jnp.float32)
-    return (kept + received.astype(jnp.float32)).astype(jnp.bfloat16)
+class Order:
+    def __init__(self, first):
+        self.last = first
+
+    def __call__(self, value):
+        value, self.last = lax.optimization_barrier((value, self.last))
+        return value
 
 
 def double(value, axis, step, dim):
@@ -83,34 +85,62 @@
     return value
 
 
-def reduce_rows(grad, order, axes):
+def labels_of(*axes):
+    return [(axis, step) for axis in axes for step in steps_of(axis)]
+
+
+class Stage:
+    def __init__(self, value):
+        self.value = value
+
+
+def halves(value, order, labels, groups):
+    for group in groups:
+        for place, (axis, step) in enumerate(group):
+            dim = labels.index((axis, step))
+            bit = bit_of(axis, step)
+            received = swap(pick(value, dim, 1 - bit), axis, step)
+            if place == 0:
+                yield Stage(value)
+            received = order(received)
+            kept = pick(value, dim, bit).astype(jnp.float32)
+            value = order((kept + received.astype(jnp.float32)).astype(jnp.bfloat16))
+            labels.remove((axis, step))
+    yield value
+
+
+def sum_rows(grad, order, axes, groups, spread):
     labels = [(axis, step) for axis in axes for step in reversed(steps_of(axis))]
     columns = grad.shape[1]
     value = grad.reshape((2,) * len(labels) + (-1, columns))
-    for label in order:
-        value = halve(value, label[0], label[1], labels.index(label))
-        labels.remove(label)
-    return value
-
-
-def labels_of(*axes):
-    return [(axis, step) for axis in axes for step in steps_of(axis)]
-
-
-def spread_rows(value, axes):
-    columns = value.shape[-1]
-    for axis in reversed(axes):
+    for value in halves(value, order, labels, groups):
+        if isinstance(value, Stage):
+            yield value
+    for axis in reversed(spread):
         for place, step in enumerate(reversed(steps_of(axis))):
-            value = double(value, axis, step, place)
+            other = swap(value, axis, step)
+            if place == 0 or axis == "dp":
+                yield Stage(value)
+            other = order(other)
+            first = jnp.stack([value, other], axis=place)
+            second = jnp.stack([other, value], axis=place)
+            value = order(jnp.where(bit_of(axis, step) == 0, first, second))
         value = value.reshape(-1, columns)
-    return value
-
-
-def sum_all(value, axes):
-    for axis in axes:
-        for step in steps_of(axis):
-            value = value + swap(value, axis, step)
-    return value
+    yield value
+
+
+def sum_all(value, order, axes):
+    for axis, step in labels_of(*axes):
+        received = swap(value, axis, step)
+        yield Stage(value)
+        value = order(value + order(received))
+    yield value
+
+
+def finish(chain):
+    for value in chain:
+        if not isinstance(value, Stage):
+            return value
 
 
 def doc_starts_of(lengths, seq_length):
@@ -132,7 +162,9 @@
     return jnp.concatenate(parts).reshape(-1, 128)
 
 
-def attend_forward_kernel(starts_ref, slopes_ref, mixed_ref, out_ref, sums_ref, *, block, heads):
+def attend_forward_kernel(*refs, block, heads):
+    starts_ref, slopes_ref, mixed_ref = refs[:3]
+    out_ref, sums_ref = refs[-2:]
     length = mixed_ref.shape[1]
     pair = pl.program_id(1)
     for head in range(heads):
@@ -163,9 +195,9 @@
     return jnp.where(allowed, (key_pos - query_pos).astype(jnp.float32), -1e32)
 
 
-def attend_backward_kernel(
-    starts_ref, slopes_ref, mixed_ref, grad_ref, sums_ref, out_ref, keys_acc, values_acc, *, block, heads
-):
+def attend_backward_kernel(*refs, block, heads):
+    starts_ref, slopes_ref, mixed_ref, grad_ref, sums_ref = refs[:5]
+    out_ref, keys_acc, values_acc = refs[-3:]
     length = mixed_ref.shape[1]
     pair = pl.program_id(1)
     scale = 1 / math.sqrt(HD)
@@ -211,7 +243,7 @@
     ]
 
 
-def attend_forward(mixed, doc_starts, slopes):
+def attend_forward(mixed, doc_starts, slopes, ahead):
     seqs, length, columns = mixed.shape
     heads_here = columns // (3 * HD)
     heads = min(2, heads_here)
@@ -219,7 +251,8 @@
     return pl.pallas_call(
         functools.partial(attend_forward_kernel, block=min(ROWS, length), heads=heads),
         grid=(seqs, pairs),
-        in_specs=attention_specs(length, heads),
+        in_specs=attention_specs(length, heads)
+        + [pl.BlockSpec(memory_space=pl.ANY)] * len(ahead),
         out_specs=[
             pl.BlockSpec((1, length, heads * HD), lambda s, p: (s, 0, p)),
             pl.BlockSpec((1, 1, heads, length), lambda s, p: (s, p, 0, 0)),
@@ -234,10 +267,10 @@
             bytes_accessed=seqs * length * columns * 4,
             transcendentals=seqs * heads_here * length * length,
         ),
-    )(doc_starts, slopes, mixed)
-
-
-def attend_backward(mixed, grad, sums, doc_starts, slopes):
+    )(doc_starts, slopes, mixed, *ahead)
+
+
+def attend_backward(mixed, grad, sums, doc_starts, slopes, ahead):
     seqs, length, columns = mixed.shape
     heads_here = columns // (3 * HD)
     heads = min(2, heads_here)
@@ -249,7 +282,8 @@
         + [
             pl.BlockSpec((1, length, heads * HD), lambda s, p: (s, 0, p)),
             pl.BlockSpec((1, 1, heads, length), lambda s, p: (s, p, 0, 0)),
-        ],
+        ]
+        + [pl.BlockSpec(memory_space=pl.ANY)] * len(ahead),
         out_specs=pl.BlockSpec((1, length, heads * 3 * HD), lambda s, p: (s, 0, p)),
         out_shape=jax.ShapeDtypeStruct((seqs, length, columns), jnp.bfloat16),
         scratch_shapes=[
@@ -262,7 +296,7 @@
             bytes_accessed=seqs * length * columns * 6,
             transcendentals=seqs * heads_here * length * length,
         ),
-    )(doc_starts, slopes, mixed, grad, sums)
+    )(doc_starts, slopes, mixed, grad, sums, *ahead)
 
 
 def per_device(
@@ -306,7 +340,20 @@
     w_mixed = lax.all_gather(head_columns, "fsdp", axis=0, tiled=True)
     w_dense = lax.all_gather(dense_weight, "fsdp", axis=0, tiled=True)
     w_up = lax.all_gather(fc1_weight, "fsdp", axis=0, tiled=True)
-    w_down = lax.all_gather(fc2_weight, "fsdp", axis=0, tiled=True)
+    split_down = fsdp_ranks == 4 and seq_ranks == 2
+    ahead = []
+    if split_down:
+        half = fc2_weight.reshape(2, -1, width)
+        far_half = swap(pick(half, 0, lax.axis_index("seq")), "fsdp", 2)
+        ahead = [far_half]
+        far_shard = double(far_half, "seq", 1, 0).reshape(fc2_weight.shape)
+        near = bit_of("fsdp", 2) == 0
+        shards = jnp.where(
+            near, jnp.stack([fc2_weight, far_shard]), jnp.stack([far_shard, fc2_weight])
+        )
+        w_down = double(shards, "fsdp", 1, 1).reshape(-1, width)
+    else:
+        w_down = lax.all_gather(fc2_weight, "fsdp", axis=0, tiled=True)
 
     hidden_all = jnp.moveaxis(gather(hidden_in, "seq"), 0, 1).reshape(-1, width)
     normed = norm_layer(hidden_all.astype(jnp.float32), gain_one, shift_one).astype(jnp.bfloat16)
@@ -318,7 +365,7 @@
     head_ids = lax.axis_index("seq") * heads_here + jnp.arange(heads_here, dtype=jnp.int32)
     slopes = 2.0 ** (-8.0 * (head_ids + 1).astype(jnp.float32) / H)
     doc_starts = doc_starts_of(lengths, seq_length)
-    attended_heads, log_sums = attend_forward(mixed, doc_starts, slopes)
+    attended_heads, log_sums = attend_forward(mixed, doc_starts, slopes, ahead)
     attended = lax.all_to_all(
         attended_heads, "seq", split_axis=1, concat_axis=2, tiled=True
     ).reshape(token_rows, width)
@@ -333,56 +380,62 @@
     grad_out = cotangent.reshape(token_rows, width)
     grad_out_f = grad_out.astype(jnp.float32)
 
-    core_first = labels_of("fsdp")[:1]
+    core = labels_of("fsdp")[:1]
     far = labels_of("fsdp")[1:]
-    g_w_down = contract_rows(gelu_out, grad_out).astype(jnp.bfloat16)
-    g_w_down = reduce_rows(
-        g_w_down, core_first + far + labels_of("seq", "dp"), ("fsdp", "seq", "dp")
-    )
-    result = hidden + jnp.dot(gelu_out, w_down, preferred_element_type=jnp.float32) + bias_down
-    output = result.astype(jnp.bfloat16).reshape(seqs_here, local_len, width)
-
-    g_bias_down = jnp.sum(grad_out_f, axis=0)
+    ranks = labels_of("seq")
+    near_z, far_z = labels_of("dp")[:1], labels_of("dp")[1:]
+    every = ("fsdp", "seq", "dp")
+    order = Order(gelu_out)
+
+    g_w_down = order(contract_rows(gelu_out, grad_out).astype(jnp.bfloat16))
+    down = sum_rows(g_w_down, order, every, [core, far, ranks, near_z, far_z], ("seq", "dp"))
+    next(down)
+    next(down)
+    w_down = order(w_down)
     grad_gelu = contract_cols(grad_out, w_down)
     grad_act = gelu_pull(grad_gelu)[0]
     g_bias_up = jnp.sum(grad_act, axis=0)
-    grad_act_low = grad_act.astype(jnp.bfloat16)
-    g_w_up = contract_rows(normed_two, grad_act_low).astype(jnp.bfloat16)
-    g_w_up = reduce_rows(
-        g_w_up, core_first + labels_of("seq") + far + labels_of("dp"), ("fsdp", "seq", "dp")
-    )
-    grad_normed_two = contract_cols(grad_act_low, w_up)
+    grad_act_low = order(grad_act.astype(jnp.bfloat16))
+    g_w_up = order(contract_rows(normed_two, grad_act_low).astype(jnp.bfloat16))
+    up = sum_rows(g_w_up, order, every, [core, ranks, far, near_z, far_z], ("seq", "dp"))
+    next(up)
+    grad_normed_two = order(contract_cols(grad_act_low, w_up))
     grad_hidden_norm, g_gain_two, g_shift_two = norm_pull_two(grad_normed_two)
     grad_hidden = grad_out_f + grad_hidden_norm
-    g_bias_dense = jnp.sum(grad_hidden, axis=0)
     grad_hidden_low = grad_hidden.astype(jnp.bfloat16)
-    grad_attended = contract_cols(grad_hidden_low, w_dense).astype(jnp.bfloat16)
-    grad_heads = lax.all_to_all(
-        grad_attended.reshape(seqs_here, local_len, width),
-        "seq",
-        split_axis=2,
-        concat_axis=1,
-        tiled=True,
-    )
-    g_w_dense = contract_rows(attended, grad_hidden_low).astype(jnp.bfloat16)
-    g_w_dense = reduce_rows(
-        g_w_dense, core_first + far + labels_of("seq", "dp"), ("fsdp", "seq", "dp")
-    )
-    early = sum_all(
-        pack([g_gain_two, g_shift_two, g_bias_up, g_bias_down, g_bias_dense]),
-        ("fsdp", "seq", "dp"),
-    ).reshape(-1)
-
-    grad_mixed = attend_backward(mixed, grad_heads, log_sums, doc_starts, slopes)
+    grad_attended = order(contract_cols(grad_hidden_low, w_dense).astype(jnp.bfloat16))
+    grad_heads = order(
+        lax.all_to_all(
+            grad_attended.reshape(seqs_here, local_len, width),
+            "seq",
+            split_axis=2,
+            concat_axis=1,
+            tiled=True,
+        )
+    )
+    ahead = [next(up).value]
+    g_w_dense = order(contract_rows(attended, grad_hidden_low).astype(jnp.bfloat16))
+    dense = sum_rows(g_w_dense, order, every, [core, far, ranks, near_z, far_z], ("seq", "dp"))
+    next(dense)
+    ahead += [next(down).value, next(dense).value]
+
+    grad_mixed = order(
+        attend_backward(mixed, grad_heads, log_sums, doc_starts, slopes, ahead)
+    )
     grad_mixed = grad_mixed.reshape(-1, columns)
-    partial = contract_cols(grad_mixed, w_mixed).astype(jnp.bfloat16)
+    partial = order(contract_cols(grad_mixed, w_mixed).astype(jnp.bfloat16))
     seq_labels = [("seq", step) for step in reversed(steps_of("seq"))]
     partial = partial.reshape((seqs_here,) + (2,) * len(seq_labels) + (local_len, width))
-    for label in list(seq_labels):
-        partial = halve(partial, label[0], label[1], 1)
-    g_w_mixed = contract_rows(normed, grad_mixed).astype(jnp.bfloat16)
-    g_w_mixed = reduce_rows(g_w_mixed, core_first + far + labels_of("dp"), ("fsdp", "dp"))
-    grad_normed = partial.reshape(token_rows, width).astype(jnp.float32)
+    partial = jnp.moveaxis(partial, 0, len(seq_labels))
+    token_sums = halves(partial, order, list(seq_labels), [ranks])
+    next(token_sums)
+    g_w_mixed = order(contract_rows(normed, grad_mixed).astype(jnp.bfloat16))
+    qkv = sum_rows(g_w_mixed, order, ("fsdp", "dp"), [core, far, near_z, far_z], ("dp",))
+    next(qkv)
+    next(up)
+    next(down)
+    next(qkv)
+    grad_normed = finish(token_sums).reshape(token_rows, width).astype(jnp.float32)
     norm_pull_one = jax.vjp(norm_layer, tokens, gain_one, shift_one)[1]
     grad_token_norm, g_gain_one, g_shift_one = norm_pull_one(grad_normed)
     grad_input = (
@@ -390,34 +443,74 @@
         .astype(jnp.bfloat16)
         .reshape(seqs_here, local_len, width)
     )
+    next(down)
+    g_bias_down = jnp.sum(grad_out_f, axis=0)
+    g_bias_dense = jnp.sum(grad_hidden, axis=0)
     bias_total = jnp.sum(grad_mixed, axis=0, dtype=jnp.float32).reshape(heads_here, 3, HD)
     pair_total = jnp.concatenate([bias_total[:, :1], bias_total[:, 2:]], axis=1)
     g_pair_bias = lax.dynamic_update_slice_in_dim(
         jnp.zeros((H, 2, HD), jnp.float32), pair_total, lax.axis_index("seq") * heads_here, 0
     ).reshape(2 * H * HD)
-    late = sum_all(pack([g_gain_one, g_shift_one, g_pair_bias]), ("fsdp", "seq", "dp"))
-    late = late.reshape(-1)
+    packed = pack(
+        [
+            g_gain_two,
+            g_shift_two,
+            g_bias_up,
+            g_bias_down,
+            g_bias_dense,
+            g_gain_one,
+            g_shift_one,
+            g_pair_bias,
+        ]
+    )
+    vector_sums = sum_all(order(packed), order, every)
+    next(vector_sums)
+    next(dense)
+    next(down)
+    next(vector_sums)
+    next(up)
+    next(qkv)
+    next(vector_sums)
+    next(down)
+    next(dense)
+    result = hidden + jnp.dot(gelu_out, w_down, preferred_element_type=jnp.float32) + bias_down
+    output = order(result.astype(jnp.bfloat16)).reshape(seqs_here, local_len, width)
+    next(vector_sums)
+    next(up)
+    next(qkv)
+    next(dense)
+    next(vector_sums)
+    next(up)
+    next(qkv)
+    next(dense)
+    next(up)
+    next(qkv)
+    next(dense)
+    g_w_down = finish(down).astype(jnp.float32)
+    small_sums = finish(vector_sums).reshape(-1)
+    next(up)
+    g_w_mixed = finish(qkv)
+    g_w_mixed = gather(g_w_mixed, "seq")
+    next(dense)
+    g_w_up = finish(up).astype(jnp.float32)
+    g_w_dense = finish(dense).astype(jnp.float32)
+    g_w_mixed = jnp.moveaxis(g_w_mixed, 0, 1).astype(jnp.float32)
+    g_w_mixed = g_w_mixed.reshape(-1, seq_ranks * columns)
 
     def own(packed, start, size):
         here = size // fsdp_ranks
         return lax.dynamic_slice_in_dim(packed, start + fsdp_rank * here, here, 0)
 
     hidden_units = bias_up.shape[0]
-    g_gain_two = own(early, 0, width)
-    g_shift_two = own(early, width, width)
-    g_bias_up = own(early, 2 * width, hidden_units)
-    g_bias_down = own(early, 2 * width + hidden_units, width)
-    g_bias_dense = own(early, 3 * width + hidden_units, width)
-    g_gain_one = own(late, 0, width)
-    g_shift_one = own(late, width, width)
-    g_pair_bias = own(late, 2 * width, 2 * H * HD)
-
-    g_w_down = spread_rows(g_w_down, ("seq", "dp")).astype(jnp.float32)
-    g_w_up = spread_rows(g_w_up, ("seq", "dp")).astype(jnp.float32)
-    g_w_dense = spread_rows(g_w_dense, ("seq", "dp")).astype(jnp.float32)
-    g_w_mixed = spread_rows(g_w_mixed, ("dp",))
-    g_w_mixed = jnp.moveaxis(gather(g_w_mixed, "seq"), 0, 1).astype(jnp.float32)
-    g_w_mixed = g_w_mixed.reshape(-1, seq_ranks * columns)
+    g_gain_two = own(small_sums, 0, width)
+    g_shift_two = own(small_sums, width, width)
+    g_bias_up = own(small_sums, 2 * width, hidden_units)
+    g_bias_down = own(small_sums, 2 * width + hidden_units, width)
+    g_bias_dense = own(small_sums, 3 * width + hidden_units, width)
+    g_gain_one = own(small_sums, 4 * width + hidden_units, width)
+    g_shift_one = own(small_sums, 5 * width + hidden_units, width)
+    g_pair_bias = own(small_sums, 6 * width + hidden_units, 2 * H * HD)
+
     return (
         output,
         grad_input,

time: 597 us -> 576 us (0.965)
  waiting for transfers between devices: 251 us -> 195 us
  blocking collectives: 5.7 us -> 39.5 us
  other arithmetic: 57.7 us -> 85.4 us
  starting transfers between devices: 61.8 us -> 48.7 us
  local copies, waits for them, and re-layouts: 72.5 us -> 59.6 us
    all_gather x1 -> x0, waiting for transfers between devices: 39 us -> none  [per_device(): w_down = lax.all_gather(fc2_weight, 'fsdp', axis=0, tiled=True)]
    all_gather x1, blocking collectives: 5.7 us -> 39.5 us  [per_device(): lax.all_gather(jnp.concatenate(small), 'fsdp', axis=0).astype(jnp.float32)]
    dynamic_slice x8 -> x2, local copies, waits for them, and re-layouts: 21 us -> 2.73 us  [pick(): return lax.dynamic_index_in_dim(value, index, dim, keepdims=False)]
    squeeze x16 -> x20, local copies, waits for them, and re-layouts: 1.03 us -> 16 us  [pick(): return lax.dynamic_index_in_dim(value, index, dim, keepdims=False)]
    convert_element_type x22 -> x23, other arithmetic: 20.1 us -> 33.4 us  [the longest x20 27.1 us: halves(): value = order((kept + received.astype(jnp.float32)).astype(jnp.bfloat16))]
    ppermute x43 -> x41, starting transfers between devices: 52.6 us -> 40.5 us  [swap(): return lax.ppermute(value, axis, pairs)]
    unnamed x94 -> x119, local copies, waits for them, and re-layouts: 31 us -> 22.3 us
    all_gather x1, waiting for transfers between devices: 11.7 us -> 3.88 us  [per_device(): w_up = lax.all_gather(fc1_weight, 'fsdp', axis=0, tiled=True)]
  transfers between devices with their start and end apart: 49 -> 46, of which waited for: 27 -> 22; matrix products, arithmetic and copies ran while one was open for 25% -> 32% of each run, Pallas kernels for 8% -> 8%
where the time goes in v2:
time: 576 us; the launch traced here: 572 us
  waiting for transfers between devices  195 us (34%)
  other arithmetic  85.4 us (15%)
  matrix products  79.9 us (14%)
  local copies, waits for them, and re-layouts  59.6 us (10%)
  starting transfers between devices  48.7 us (8%)
  Pallas kernels  48.3 us (8%)
  blocking collectives  39.5 us (7%)
  between operations  15.1 us (3%)
    ppermute x41, waiting for transfers between devices, swap(): return lax.ppermute(value, axis, pairs)  181 us
    ppermute x41, starting transfers between devices, swap(): return lax.ppermute(value, axis, pairs)  40.5 us
    all_gather x1, blocking collectives, per_device(): lax.all_gather(jnp.concatenate(small), 'fsdp', axis=0).astype(jnp.float32)  39.5 us
    dot_general x4, matrix products, contract_cols(): lax.dot_general(left_side, right_side, (((1,), (1,)), ((), ())), preferre...  28.4 us
    pallas_call x1, Pallas kernels, attend_backward(): pl.pallas_call(functools.partial(attend_backward_kernel, block=min(ROWS,...  27.8 us
    convert_element_type x20, other arithmetic, halves(): value = order((kept + received.astype(jnp.float32)).astype(jnp.bfloat16))  27.1 us
    unnamed x119, local copies, waits for them, and re-layouts  22.3 us
    pallas_call x1, Pallas kernels, attend_forward(): pl.pallas_call(functools.partial(attend_forward_kernel, block=min(ROWS, l...  20.5 us
  transfers between devices with their start and end apart: 46, of which 22 were waited for; matrix products, arithmetic and copies ran while one was open for 32% of the time, Pallas kernels for 8%

profile of v2, /device:TPU:0, one launch (start us, length us, event | category | flops | bytes accessed | tf_op | source)
XLA Modules:
  0.0 571.8 jit_solution(12791889782789211525)
XLA Ops:
  11.2 3.0 collective-permute-start
  19.7 39.5 %all-gather = bf16[12288]{0:T(1024)(128)(2,1)S(1)} all-gather(bf16[3072]{0:T(1024)(128)(2,1)S(1)} %dynamic-update-slice.15), channel_id=2, replica_groups=mesh['dp'=4,'fsdp'=4,'seq'=2] {'fsdp'}, dimensions={0}, use_global_device_ids=true | all-gather | bytes 30720 | tf_op jit(solution)/shard_map/all_gather | solution.py:329
  61.9 3.4 fusion.15
  65.3 6.2 %fusion.16.refs_2_ = bf16[1,1024,1536]{2,1,0:T(8,128)(2,1)S(1)} fusion(bf16[1024,1024]{1,0:T(8,128)(2,1)} %fusion.15, bf16[1024,1536]{1,0:T(8,128)(2,1)} %all-gather.5.cloned.1.call-done, f32[1536]{0:T(1024)S(1)} %add.365), kind=kOutput, calls=%fused_computation.41 | convolution fusion | flops 3224371200 | bytes 8394752 | tf_op jit(solution)/shard_map/dot_general | solution.py:361
  71.5 20.5 %shard_map.254 = (bf16[1,1024,512]{2,1,0:T(8,128)(2,1)S(1)}, f32[1,4,2,1024]{3,2,1,0:T(2,128)S(1)}) custom-call(s32[1,1,1024]{2,1,0:T(1,128)S(1)} %bitcast.345, f32[8]{0:T(128)S(1)} %multiply_power_fusion.refs_1_, bf16[1,1024,1536]{2,1,0:T(8,128)(2,1)S(1)} %fusion.16.refs_2_, bf16[512,1024]{1,0:T(8,128)(2,1)S(1)} %collective-permute-done.1.refs_3_), custom_call_target="tpu_custom_call" | custom-call | flops 4294967296 | bytes 6291456 | tf_op jit(solution)/shard_map/pallas_call | solution.py:251
  92.1 2.9 copy.133
  95.6 9.1 %reduce.7 = bf16[1024,512]{1,0:T(8,128)(2,1)} reduce(bf16[1024,1,512]{2,1,0:T(2,128)(2,1)} %bitcast.372, bf16[]{:T(256)} %broadcast.394), dimensions={1}, to_apply=%bitcast.342.reduce_sub_computation | reduce | bytes 2097154
  104.7 2.6 reshape.761
  107.3 4.4 all-to-all-start
  114.0 2.8 maximum_select_fusion.2
  117.0 9.1 %all-to-all-done = bf16[2,2,131072]{2,1,0:T(2,128)(2,1)} async-done(((bf16[2,2,131072]{2,1,0:T(2,128)(2,1)}), bf16[2,2,131072]{2,1,0:T(2,128)(2,1)}, u32[]{:S(2)}, u32[]{:S(2)}) %all-to-all-start) | async-done | bytes 1048608 | tf_op jit(solution)/shard_map/all_to_all | solution.py:369
  126.0 2.9 reshape.762
  132.1 4.5 fusion.70
  138.6 3.9 all-gather.9.cloned.1.call-done
  142.5 12.7 %multiply_convert_fusion = (bf16[512,4096]{1,0:T(8,128)(2,1)S(1)}, f32[512,4096]{1,0:T(8,128)}) fusion(f32[4096]{0:T(1024)S(1)} %bitcast.426, bf16[1024,4096]{1,0:T(8,128)(2,1)} %all-gather.9.cloned.1.call-done, f32[512,1024]{1,0:T(8,128)} %get-tuple-element.395, f32[1024]{0:T(1024)S(1)} %bitcast.430, f32[1024]{0:T(1024)S(1)} %bitcast.420, ...), kind=kOutput, calls=%fused_computation.19 | convolution fusion | flops 4318560256 | bytes 23097344 | tf_op jit(solution)/shard_map/dot_general | solution.py:377
  155.2 4.8 convolution_convert_fusion.1
  160.0 3.1 dynamic-slice_bitcast_fusion.1
  168.7 5.7 maximum_select_fusion
  174.5 9.4 %fusion.6 = bf16[2,2,2,2,128,1024]{5,4,3,2,1,0:T(8,128)(2,1)} fusion(bf16[2,2,2,2,128,1024]{5,4,3,2,1,0:T(8,128)(2,1)} %collective-permute-done.4, bf16[2,2,2,2,2,128,1024]{6,5,4,3,2,1,0:T(8,128)(2,1)S(1)} %bitcast.369, s32[]{:T(128)S(6)} %select_n.370), kind=kLoop, calls=%fused_computation.13 | loop fusion | flops 8388608 | bytes 12582916 | tf_op jit(solution)/shard_map/convert_element_type | solution.py:107
  183.8 13.2 %fusion.65 = (f32[4096]{0:T(1024)S(1)}, bf16[512,4096]{1,0:T(8,128)(2,1)S(1)}) fusion(f32[512,4096]{1,0:T(8,128)} %get-tuple-element.397, f32[4096]{0:T(1024)S(1)} %bitcast.427, bf16[4096,1024]{1,0:T(8,128)(2,1)S(1)} %bitcast.362, bf16[1,512,1024]{2,1,0:T(8,128)(2,1)S(1)} %copy-done.25), kind=kOutput, calls=%fused_computation.194 | convolution fusion | flops 4349489152 | bytes 22052864 | tf_op jit(solution)/shard_map/dot_general | solution.py:41
  197.0 6.9 %convolution_convert_fusion = bf16[1024,4096]{1,0:T(8,128)(2,1)S(1)} fusion(bf16[512,4096]{1,0:T(8,128)(2,1)S(1)} %get-tuple-element.165, f32[512,1024]{1,0:T(8,128)} %get-tuple-element.395, f32[1024]{0:T(1024)S(1)} %bitcast.431, f32[1024]{0:T(1024)S(1)} %bitcast.421, f32[512]{0:T(512)S(1)} %fusion.59, f32[512]{0:T(512)S(1)} %broadcast_multiply_fusion.2), kind=kOutput, calls=%fused_computation.20 | convolution fusion | flops 4301783040 | bytes 14692352 | tf_op jit(solution)/shard_map/dot_general | solution.py:35
  203.9 2.5 dynamic-slice_bitcast_fusion
  208.7 7.2 %fusion.71 = f32[512,1024]{1,0:T(8,128)S(1)} fusion(bf16[512,4096]{1,0:T(8,128)(2,1)S(1)} %get-tuple-element.165, bf16[1024,4096]{1,0:T(8,128)(2,1)} %all-gather.9.cloned.1.call-done), kind=kOutput, calls=%fused_computation.200 | convolution fusion | flops 4294967296 | bytes 14680064 | tf_op jit(solution)/shard_map/dot_general | solution.py:41
  215.8 2.4 multiply_reduce_fusion.1
  218.3 2.4 fusion.67
  220.8 2.3 convolution_convert_fusion.4
  223.1 6.0 %copy.97 = bf16[1,512,1024]{1,0,2:T(2,128)(2,1)} copy(bf16[1,512,1024]{2,1,0:T(8,128)(2,1)} %bitcast.392) | data formatting | bytes 2097152 | tf_op jit(solution)/shard_map/reshape | solution.py:409
  229.1 8.0 %reduce.8 = bf16[1024,512]{1,0:T(8,128)(2,1)S(1)} reduce(bf16[1024,1,512]{2,1,0:T(2,128)(2,1)} %bitcast.373, bf16[]{:T(256)} %broadcast.394), dimensions={1}, to_apply=%bitcast.318.reduce_sub_computation | reduce | bytes 2097154
  238.7 3.6 all-to-all-start.1
  242.3 3.3 dynamic-slice_bitcast_fusion.3
  245.9 9.7 %add_convert_fusion.3 = bf16[512,1024]{1,0:T(8,128)(2,1)} fusion(f32[512,1024]{1,0:T(8,128)} %get-tuple-element.395, bf16[512,4096]{1,0:T(8,128)(2,1)S(1)} %copy-done.40, bf16[4096,1024]{1,0:T(8,128)(2,1)} %bitcast.363, f32[1024]{0:T(1024)S(1)} %bitcast.432), kind=kOutput, calls=%fused_computation.88 | convolution fusion | flops 4296540160 | bytes 15732736 | tf_op jit(solution)/shard_map/dot_general | solution.py:476
  255.7 2.7 convolution_convert_fusion.3
  261.0 5.2 fusion.5.refs_5_
  266.3 27.4 %collective-permute-done.7 = bf16[2,2,2,128,1024]{4,3,2,1,0:T(8,128)(2,1)} collective-permute-done((bf16[2,2,2,128,1024]{4,3,2,1,0:T(8,128)(2,1)}, bf16[2,2,2,128,1024]{4,3,2,1,0:T(8,128)(2,1)}, u32[]{:S(2)}, u32[]{:S(2)}) %collective-permute-start.7) | collective-permute-done | bytes 2097184 | tf_op jit(solution)/shard_map/ppermute | solution.py:57
  293.7 2.6 fusion.11.refs_6_
  301.7 27.8 %shard_map.255 = bf16[1,1024,1536]{2,1,0:T(8,128)(2,1)} custom-call(s32[1,1,1024]{2,1,0:T(1,128)S(1)} %bitcast.346, f32[8]{0:T(128)S(1)} %multiply_power_fusion.refs_1_, bf16[1,1024,1536]{2,1,0:T(8,128)(2,1)} %copy-done.3, bf16[1,1024,512]{2,1,0:T(8,128)(2,1)S(1)} %bitcast.344, f32[1,4,2,1024]{3,2,1,0:T(2,128)S(1)} %get-tuple-element.187.refs_4_, ...), custom_call_target="tpu_custom_call" | custom-call | flops 10737418240 | bytes 9437184 | tf_op jit(solution)/shard_map/pallas_call | solution.py:278
  329.5 5.7 fusion.38
  335.3 4.0 convolution_convert_fusion.2
  346.6 3.0 fusion.10
  349.6 19.5 %collective-permute-done.11 = bf16[2,2,128,1024]{3,2,1,0:T(8,128)(2,1)} collective-permute-done((bf16[2,2,128,1024]{3,2,1,0:T(8,128)(2,1)}, bf16[2,2,128,1024]{3,2,1,0:T(8,128)(2,1)}, u32[]{:S(2)}, u32[]{:S(2)}) %collective-permute-start.11) | collective-permute-done | bytes 1048608 | tf_op jit(solution)/shard_map/ppermute | solution.py:57
  375.0 14.9 %collective-permute-done.9 = bf16[1,512,1024]{2,1,0:T(8,128)(2,1)} collective-permute-done((bf16[1,512,1024]{2,1,0:T(8,128)(2,1)}, bf16[1,512,1024]{2,1,0:T(8,128)(2,1)}, u32[]{:S(2)}, u32[]{:S(2)}) %collective-permute-start.9) | collective-permute-done | bytes 1048608 | tf_op jit(solution)/shard_map/ppermute | solution.py:57
  391.9 2.5 collective-permute-start.15
  396.3 2.3 fusion.64
  401.4 3.8 collective-permute-done.15
  406.0 13.7 %collective-permute-done.19 = bf16[2,2,64,1536]{3,2,0,1:T(8,128)(2,1)S(1)} collective-permute-done((bf16[2,2,64,1536]{3,2,0,1:T(8,128)(2,1)S(1)}, bf16[2,2,64,1536]{3,2,0,1:T(8,128)(2,1)S(1)}, u32[]{:S(2)}, u32[]{:S(2)}) %collective-permute-start.19) | collective-permute-done | bytes 786464 | tf_op jit(solution)/shard_map/ppermute | solution.py:57
  424.1 2.9 collective-permute-done.23
  429.9 8.8 %collective-permute-done.31 = bf16[32,1024]{1,0:T(8,128)(2,1)S(1)} collective-permute-done((bf16[32,1024]{1,0:T(8,128)(2,1)S(1)}, bf16[32,1024]{1,0:T(8,128)(2,1)S(1)}, u32[]{:S(2)}, u32[]{:S(2)}) %collective-permute-start.31) | collective-permute-done | bytes 65568 | tf_op jit(solution)/shard_map/ppermute | solution.py:57
  438.7 3.4 collective-permute-start.34
  442.4 7.2 %collective-permute-done.34 = bf16[32,1024]{1,0:T(8,128)(2,1)S(1)} collective-permute-done((bf16[32,1024]{1,0:T(8,128)(2,1)S(1)}, bf16[32,1024]{1,0:T(8,128)(2,1)S(1)}, u32[]{:S(2)}, u32[]{:S(2)}) %collective-permute-start.34) | collective-permute-done | bytes 65568 | tf_op jit(solution)/shard_map/ppermute | solution.py:57
  454.8 3.7 collective-permute-done.28
  458.7 15.5 %collective-permute-done.27 = bf16[64,1536]{1,0:T(8,128)(2,1)S(1)} collective-permute-done((bf16[64,1536]{1,0:T(8,128)(2,1)S(1)}, bf16[64,1536]{1,0:T(8,128)(2,1)S(1)}, u32[]{:S(2)}, u32[]{:S(2)}) %collective-permute-start.27) | collective-permute-done | bytes 196640 | tf_op jit(solution)/shard_map/ppermute | solution.py:57
  474.3 3.0 collective-permute-start.26
  477.2 9.5 %collective-permute-done.26 = f32[96,128]{1,0:T(8,128)S(1)} collective-permute-done((f32[96,128]{1,0:T(8,128)S(1)}, f32[96,128]{1,0:T(8,128)S(1)}, u32[]{:S(2)}, u32[]{:S(2)}) %collective-permute-start.26) | collective-permute-done | bytes 49184 | tf_op jit(solution)/shard_map/ppermute | solution.py:57
  492.5 5.6 collective-permute-done.39
  499.9 6.6 %collective-permute-done.32 = bf16[2,64,1536]{2,1,0:T(8,128)(2,1)S(1)} collective-permute-done((bf16[2,64,1536]{2,1,0:T(8,128)(2,1)S(1)}, bf16[2,64,1536]{2,1,0:T(8,128)(2,1)S(1)}, u32[]{:S(2)}, u32[]{:S(2)}) %collective-permute-start.32) | collective-permute-done | bytes 393248 | tf_op jit(solution)/shard_map/ppermute | solution.py:57
  508.1 8.0 %collective-permute-done.37 = bf16[2,32,4096]{2,1,0:T(8,128)(2,1)S(1)} collective-permute-done((bf16[2,32,4096]{2,1,0:T(8,128)(2,1)S(1)}, bf16[2,32,4096]{2,1,0:T(8,128)(2,1)S(1)}, u32[]{:S(2)}, u32[]{:S(2)}) %collective-permute-start.37) | collective-permute-done | bytes 524320 | tf_op jit(solution)/shard_map/ppermute | solution.py:57
  519.8 4.7 collective-permute-done.40
  524.8 2.6 bitcast_convert_fusion
  527.5 13.9 %collective-permute-done.33 = bf16[1,256,1536]{2,1,0:T(8,128)(2,1)S(1)} collective-permute-done((bf16[1,256,1536]{2,1,0:T(8,128)(2,1)S(1)}, bf16[1,256,1536]{2,1,0:T(8,128)(2,1)S(1)}, u32[]{:S(2)}, u32[]{:S(2)}) %collective-permute-start.33) | collective-permute-done | bytes 786464 | tf_op jit(solution)/shard_map/ppermute | solution.py:57
  541.6 2.4 copy.102
  544.0 3.5 copy.109
  547.5 12.2 %collective-permute-done.38 = bf16[128,4096]{1,0:T(8,128)(2,1)} collective-permute-done((bf16[128,4096]{1,0:T(8,128)(2,1)}, bf16[128,4096]{1,0:T(8,128)(2,1)}, u32[]{:S(2)}, u32[]{:S(2)}) %collective-permute-start.38) | collective-permute-done | bytes 1048608 | tf_op jit(solution)/shard_map/ppermute | solution.py:57
  559.7 2.7 maximum_select_fusion.5
  562.4 2.6 bitcast_convert_fusion.1
  (286 shorter events, 84.9 us)
Async XLA Ops:
  7.2 58.1 %all-gather.5.cloned.1.call-start = ((), (), s32[]{:S(2)}) async-start(), calls=%async_computation.2 | async-start | bytes 3932160 | tf_op jit(solution)/shard_map/all_gather | solution.py:340
  9.6 122.6 %all-gather.7.cloned.1.call-start = ((), (), s32[]{:S(2)}) async-start(), calls=%async_computation.3 | async-start | bytes 2621440 | tf_op jit(solution)/shard_map/all_gather | solution.py:341
  10.3 8.0 %copy-start.30 = (bf16[512]{0:T(512)(128)(2,1)S(1)}, bf16[512]{0:T(512)(128)(2,1)}, u32[]{:S(2)}) copy-start(bf16[512]{0:T(512)(128)(2,1)} %param.20) | copy-start | bytes 3076
  10.3 8.2 %copy-start.33 = (bf16[256]{0:T(256)(128)(2,1)S(1)}, bf16[256]{0:T(256)(128)(2,1)}, u32[]{:S(2)}) copy-start(bf16[256]{0:T(256)(128)(2,1)} %param.22) | copy-start | bytes 1540
  10.4 8.4 %copy-start.34 = (bf16[256]{0:T(256)(128)(2,1)S(1)}, bf16[256]{0:T(256)(128)(2,1)}, u32[]{:S(2)}) copy-start(bf16[256]{0:T(256)(128)(2,1)} %param.23) | copy-start | bytes 1540
  10.4 8.6 %copy-start.35 = (bf16[256]{0:T(256)(128)(2,1)S(1)}, bf16[256]{0:T(256)(128)(2,1)}, u32[]{:S(2)}) copy-start(bf16[256]{0:T(256)(128)(2,1)} %param.24) | copy-start | bytes 1540
  10.4 8.9 %copy-start.29 = (bf16[1024]{0:T(1024)(128)(2,1)S(1)}, bf16[1024]{0:T(1024)(128)(2,1)}, u32[]{:S(2)}) copy-start(bf16[1024]{0:T(1024)(128)(2,1)} %param.26) | copy-start | bytes 6148
  10.4 9.1 %copy-start.36 = (bf16[256]{0:T(256)(128)(2,1)S(1)}, bf16[256]{0:T(256)(128)(2,1)}, u32[]{:S(2)}) copy-start(bf16[256]{0:T(256)(128)(2,1)} %param.28) | copy-start | bytes 1540
  10.4 49.2 %copy-start.38 = (s32[1,4]{1,0:T(1,128)S(1)}, s32[1,4]{1,0:T(1,128)}, u32[]{:S(2)}) copy-start(s32[1,4]{1,0:T(1,128)} %param.16) | copy-start | bytes 52
  10.4 132.0 %all-gather.9.cloned.1.call-start = ((), (), s32[]{:S(2)}) async-start(), calls=%async_computation.4 | async-start | bytes 10485760 | tf_op jit(solution)/shard_map/all_gather | solution.py:342
  11.2 48.7 %collective-permute-start = (bf16[1,1,512,1024]{3,2,1,0:T(8,128)(2,1)S(1)}, bf16[1,1,512,1024]{3,2,1,0:T(8,128)(2,1)S(1)}, u32[]{:S(2)}, u32[]{:S(2)}) collective-permute-start(bf16[1,1,512,1024]{3,2,1,0:T(8,128)(2,1)S(1)} %bitcast.347), channel_id=1, source_target_pairs={{0,1},{1,0},{2,3},{3,2},{4,5},{5,4},{6,7},{7,6},{8,9},{9,8},{10,11... | collective-permute-start | bytes 3145736 | tf_op jit(solution)/shard_map/ppermute | solution.py:57
  16.5 45.1 %collective-permute-start.1 = (bf16[512,1024]{1,0:T(8,128)(2,1)}, bf16[512,1024]{1,0:T(8,128)(2,1)S(1)}, u32[]{:S(2)}, u32[]{:S(2)}) collective-permute-start(bf16[512,1024]{1,0:T(8,128)(2,1)} %dynamic-slice_bitcast_fusion.8), channel_id=1, source_target_pairs={{0,4},{2,6},{4,0},{6,2},{1,5},{3,7},{5,1},{7,3},{8,12},{10,14},{12... | collective-permute-start | bytes 3145736 | tf_op jit(solution)/shard_map/ppermute | solution.py:57
  61.6 50.2 %collective-permute-start.2 = (bf16[512,1024]{1,0:T(8,128)(2,1)S(1)}, bf16[512,1024]{1,0:T(8,128)(2,1)}, u32[]{:S(2)}, u32[]{:S(2)}) collective-permute-start(bf16[512,1024]{1,0:T(8,128)(2,1)S(1)} %collective-permute-done.1.refs_3_), channel_id=1, source_target_pairs={{0,1},{1,0},{2,3},{3,2},{4,5},{5,4},{6,7},{7,6},{8,9},{9,8},{10,11... | collective-permute-start | bytes 3145736 | tf_op jit(solution)/shard_map/ppermute | solution.py:57
  71.5 20.6 %copy-start.3 = (bf16[1,1024,1536]{2,1,0:T(8,128)(2,1)}, bf16[1,1024,1536]{2,1,0:T(8,128)(2,1)S(1)}, u32[]{:S(2)}) copy-start(bf16[1,1024,1536]{2,1,0:T(8,128)(2,1)S(1)} %fusion.16.refs_2_) | copy-start | bytes 9437188
  107.3 18.7 %all-to-all-start = ((bf16[2,2,131072]{2,1,0:T(2,128)(2,1)}), bf16[2,2,131072]{2,1,0:T(2,128)(2,1)}, u32[]{:S(2)}, u32[]{:S(2)}) async-start(bf16[2,2,131072]{2,1,0:T(2,128)(2,1)} %reshape.761), calls=%async_computation | async-start | bytes 2097152 | tf_op jit(solution)/shard_map/all_to_all | solution.py:369
  116.8 51.9 %collective-permute-start.3 = (bf16[2,1024,1024]{2,1,0:T(8,128)(2,1)}, bf16[2,1024,1024]{2,1,0:T(8,128)(2,1)}, u32[]{:S(2)}, u32[]{:S(2)}) collective-permute-start(bf16[2,1024,1024]{2,1,0:T(8,128)(2,1)} %maximum_select_fusion.2), channel_id=1, source_target_pairs={{0,2},{2,0},{4,6},{6,4},{1,3},{3,1},{5,7},{7,5},{8,10},{10,8},{12,... | collective-permute-start | bytes 12582920 | tf_op jit(solution)/shard_map/ppermute | solution.py:57
  142.5 12.7 %copy-start.25 = (bf16[1,512,1024]{2,1,0:T(8,128)(2,1)S(1)}, bf16[1,512,1024]{2,1,0:T(8,128)(2,1)}, u32[]{:S(2)}) copy-start(bf16[1,512,1024]{2,1,0:T(8,128)(2,1)} %param.29) | copy-start | bytes 3145732
  164.5 9.9 %collective-permute-start.4 = (bf16[2,2,2,2,128,1024]{5,4,3,2,1,0:T(8,128)(2,1)}, bf16[2,2,2,2,128,1024]{5,4,3,2,1,0:T(8,128)(2,1)}, u32[]{:S(2)}, u32[]{:S(2)}) collective-permute-start(bf16[2,2,2,2,128,1024]{5,4,3,2,1,0:T(8,128)(2,1)} %dynamic-slice_bitcast_fusion.1), channel_id=1, source_target_pairs={{0,2},{2,0},{4,6},{6,4},{1,3},{3,1},{5,7},{7,5},{8,10},{10,8},{12,... | collective-permute-start | bytes 12582920 | tf_op jit(solution)/shard_map/ppermute | solution.py:57
  174.4 9.4 %copy-start.12 = (bf16[2,2,1024,1024]{3,2,1,0:T(8,128)(2,1)}, bf16[2,2,1024,1024]{3,2,1,0:T(8,128)(2,1)S(1)}, u32[]{:S(2)}) copy-start(bf16[2,2,1024,1024]{3,2,1,0:T(8,128)(2,1)S(1)} %maximum_select_fusion) | copy-start | bytes 25165828
  208.4 52.5 %collective-permute-start.5 = (bf16[2,2,2,2,32,4096]{5,4,3,2,1,0:T(8,128)(2,1)}, bf16[2,2,2,2,32,4096]{5,4,3,2,1,0:T(8,128)(2,1)}, u32[]{:S(2)}, u32[]{:S(2)}) collective-permute-start(bf16[2,2,2,2,32,4096]{5,4,3,2,1,0:T(8,128)(2,1)} %dynamic-slice_bitcast_fusion), channel_id=1, source_target_pairs={{0,2},{2,0},{4,6},{6,4},{1,3},{3,1},{5,7},{7,5},{8,10},{10,8},{12,... | collective-permute-start | bytes 12582920 | tf_op jit(solution)/shard_map/ppermute | solution.py:57
  220.7 34.9 %copy-start.13 = (f32[512,1024]{1,0:T(8,128)}, f32[512,1024]{1,0:T(8,128)S(1)}, u32[]{:S(2)}) copy-start(f32[512,1024]{1,0:T(8,128)S(1)} %get-tuple-element.368) | copy-start | bytes 6291460
  238.7 19.7 %all-to-all-start.1 = ((bf16[2,2,131072]{2,1,0:T(2,128)(2,1)}), bf16[2,2,131072]{2,1,0:T(2,128)(2,1)S(1)}, u32[]{:S(2)}, u32[]{:S(2)}) async-start(bf16[2,2,131072]{2,1,0:T(2,128)(2,1)} %reshape.763), calls=%async_computation.1 | async-start | bytes 2097152 | tf_op jit(solution)/shard_map/all_to_all | solution.py:408
  245.6 48.1 %collective-permute-start.7 = (bf16[2,2,2,128,1024]{4,3,2,1,0:T(8,128)(2,1)}, bf16[2,2,2,128,1024]{4,3,2,1,0:T(8,128)(2,1)}, u32[]{:S(2)}, u32[]{:S(2)}) collective-permute-start(bf16[2,2,2,128,1024]{4,3,2,1,0:T(8,128)(2,1)} %dynamic-slice_bitcast_fusion.3), channel_id=1, source_target_pairs={{0,4},{2,6},{4,0},{6,2},{1,5},{3,7},{5,1},{7,3},{8,12},{10,14},{12... | collective-permute-start | bytes 6291464 | tf_op jit(solution)/shard_map/ppermute | solution.py:57
  245.9 9.7 %copy-start.18 = (bf16[1,512,2,512]{1,3,2,0:T(8,128)(2,1)S(1)}, bf16[1,512,2,512]{1,3,2,0:T(8,128)(2,1)}, u32[]{:S(2)}) copy-start(bf16[1,512,2,512]{1,3,2,0:T(8,128)(2,1)} %copy.94) | copy-start | bytes 3145732
  245.9 9.7 %copy-start.27 = (bf16[1,512,1024]{2,1,0:T(8,128)(2,1)S(1)}, bf16[1,512,1024]{2,1,0:T(8,128)(2,1)}, u32[]{:S(2)}) copy-start(bf16[1,512,1024]{2,1,0:T(8,128)(2,1)} %param.29) | copy-start | bytes 3145732
  260.9 32.8 %copy-start.8 = (bf16[2,2,2,2,128,1024]{5,4,3,2,1,0:T(8,128)(2,1)S(1)}, bf16[2,2,2,2,128,1024]{5,4,3,2,1,0:T(8,128)(2,1)}, u32[]{:S(2)}) copy-start(bf16[2,2,2,2,128,1024]{5,4,3,2,1,0:T(8,128)(2,1)} %fusion.6) | copy-start | bytes 12582916
  266.1 31.6 %copy-start.9 = (bf16[2,2,2,2,32,4096]{5,4,3,2,1,0:T(8,128)(2,1)}, bf16[2,2,2,2,32,4096]{5,4,3,2,1,0:T(8,128)(2,1)S(1)}, u32[]{:S(2)}) copy-start(bf16[2,2,2,2,32,4096]{5,4,3,2,1,0:T(8,128)(2,1)S(1)} %fusion.5.refs_5_) | copy-start | bytes 12582916
  266.2 34.6 %collective-permute-start.6 = (bf16[2,2,2,2,32,1024]{5,4,3,2,1,0:T(8,128)(2,1)S(1)}, bf16[2,2,2,2,32,1024]{5,4,3,2,1,0:T(8,128)(2,1)S(1)}, u32[]{:S(2)}, u32[]{:S(2)}) collective-permute-start(bf16[2,2,2,2,32,1024]{5,4,3,2,1,0:T(8,128)(2,1)S(1)} %dynamic-slice_bitcast_fusion.7), channel_id=1, source_target_pairs={{0,2},{2,0},{4,6},{6,4},{1,3},{3,1},{5,7},{7,5},{8,10},{10,8},{12,... | collective-permute-start | bytes 3145736 | tf_op jit(solution)/shard_map/ppermute | solution.py:57
  297.7 48.9 %collective-permute-start.12 = (bf16[2,2,2,32,4096]{4,3,2,1,0:T(8,128)(2,1)}, bf16[2,2,2,32,4096]{4,3,2,1,0:T(8,128)(2,1)}, u32[]{:S(2)}, u32[]{:S(2)}) collective-permute-start(bf16[2,2,2,32,4096]{4,3,2,1,0:T(8,128)(2,1)} %dynamic-slice_bitcast_fusion.2), channel_id=1, source_target_pairs={{0,1},{1,0},{2,3},{3,2},{4,5},{5,4},{6,7},{7,6},{8,9},{9,8},{10,11... | collective-permute-start | bytes 6291464 | tf_op jit(solution)/shard_map/ppermute | solution.py:57
  300.5 68.6 %collective-permute-start.11 = (bf16[2,2,128,1024]{3,2,1,0:T(8,128)(2,1)}, bf16[2,2,128,1024]{3,2,1,0:T(8,128)(2,1)}, u32[]{:S(2)}, u32[]{:S(2)}) collective-permute-start(bf16[2,2,128,1024]{3,2,1,0:T(8,128)(2,1)} %dynamic-slice_bitcast_fusion.5), channel_id=1, source_target_pairs={{0,1},{1,0},{2,3},{3,2},{4,5},{5,4},{6,7},{7,6},{8,9},{9,8},{10,11... | collective-permute-start | bytes 3145736 | tf_op jit(solution)/shard_map/ppermute | solution.py:57
  301.7 27.8 %copy-start.37 = (bf16[1024,1536]{1,0:T(8,128)(2,1)S(1)}, bf16[1024,1536]{1,0:T(8,128)(2,1)}, u32[]{:S(2)}) copy-start(bf16[1024,1536]{1,0:T(8,128)(2,1)} %all-gather.5.cloned.1.call-done) | copy-start | bytes 9437188
  342.0 31.0 %collective-permute-start.10 = (bf16[2,2,2,64,1536]{4,3,1,2,0:T(8,128)(2,1)}, bf16[2,2,2,64,1536]{4,3,1,2,0:T(8,128)(2,1)}, u32[]{:S(2)}, u32[]{:S(2)}) collective-permute-start(bf16[2,2,2,64,1536]{4,3,1,2,0:T(8,128)(2,1)} %bitcast.340), channel_id=1, source_target_pairs={{0,2},{2,0},{4,6},{6,4},{1,3},{3,1},{5,7},{7,5},{8,10},{10,8},{12,... | collective-permute-start | bytes 4718600 | tf_op jit(solution)/shard_map/ppermute | solution.py:57
  343.1 46.9 %collective-permute-start.9 = (bf16[1,512,1024]{2,1,0:T(8,128)(2,1)}, bf16[1,512,1024]{2,1,0:T(8,128)(2,1)}, u32[]{:S(2)}, u32[]{:S(2)}) collective-permute-start(bf16[1,512,1024]{2,1,0:T(8,128)(2,1)} %dynamic-slice_bitcast_fusion.6), channel_id=1, source_target_pairs={{0,1},{1,0},{2,3},{3,2},{4,5},{5,4},{6,7},{7,6},{8,9},{9,8},{10,11... | collective-permute-start | bytes 3145736 | tf_op jit(solution)/shard_map/ppermute | solution.py:57
  345.9 53.0 %collective-permute-start.8 = (bf16[2,2,2,32,1024]{4,3,2,1,0:T(8,128)(2,1)}, bf16[2,2,2,32,1024]{4,3,2,1,0:T(8,128)(2,1)S(1)}, u32[]{:S(2)}, u32[]{:S(2)}) collective-permute-start(bf16[2,2,2,32,1024]{4,3,2,1,0:T(8,128)(2,1)} %dynamic-slice_bitcast_fusion.12), channel_id=1, source_target_pairs={{0,4},{2,6},{4,0},{6,2},{1,5},{3,7},{5,1},{7,3},{8,12},{10,14},{12... | collective-permute-start | bytes 1572872 | tf_op jit(solution)/shard_map/ppermute | solution.py:57
  370.8 20.8 %collective-permute-start.13 = (bf16[2,128,1024]{2,1,0:T(8,128)(2,1)S(1)}, bf16[2,128,1024]{2,1,0:T(8,128)(2,1)S(1)}, u32[]{:S(2)}, u32[]{:S(2)}) collective-permute-start(bf16[2,128,1024]{2,1,0:T(8,128)(2,1)S(1)} %dynamic-slice_bitcast_fusion.11), channel_id=1, source_target_pairs={{0,8},{8,0},{16,24},{24,16},{1,9},{9,1},{17,25},{25,17},{2,10},{10... | collective-permute-start | bytes 1572872 | tf_op jit(solution)/shard_map/ppermute | solution.py:57
  372.4 33.3 %collective-permute-start.20 = (bf16[2,2,32,4096]{3,2,1,0:T(8,128)(2,1)S(1)}, bf16[2,2,32,4096]{3,2,1,0:T(8,128)(2,1)S(1)}, u32[]{:S(2)}, u32[]{:S(2)}) collective-permute-start(bf16[2,2,32,4096]{3,2,1,0:T(8,128)(2,1)S(1)} %dynamic-slice_bitcast_fusion.4), channel_id=1, source_target_pairs={{0,4},{2,6},{4,0},{6,2},{1,5},{3,7},{5,1},{7,3},{8,12},{10,14},{12... | collective-permute-start | bytes 3145736 | tf_op jit(solution)/shard_map/ppermute | solution.py:57
  373.1 16.9 %copy-start.21 = (bf16[1024,1024]{1,0:T(8,128)(2,1)S(1)}, bf16[1024,1024]{1,0:T(8,128)(2,1)}, u32[]{:S(2)}) copy-start(bf16[1024,1024]{1,0:T(8,128)(2,1)} %copy-done.20) | copy-start | bytes 6291460
  375.0 19.3 %copy-start.5 = (bf16[1,512,1024]{2,1,0:T(8,128)(2,1)S(1)}, bf16[1,512,1024]{2,1,0:T(8,128)(2,1)}, u32[]{:S(2)}) copy-start(bf16[1,512,1024]{2,1,0:T(8,128)(2,1)} %param.15) | copy-start | bytes 3145732
  391.9 13.3 %collective-permute-start.15 = (bf16[128,1024]{1,0:T(8,128)(2,1)S(1)}, bf16[128,1024]{1,0:T(8,128)(2,1)S(1)}, u32[]{:S(2)}, u32[]{:S(2)}) collective-permute-start(bf16[128,1024]{1,0:T(8,128)(2,1)S(1)} %dynamic-slice_bitcast_fusion.15), channel_id=1, source_target_pairs={{0,16},{8,24},{16,0},{24,8},{1,17},{9,25},{17,1},{25,9},{2,18},{10... | collective-permute-start | bytes 786440 | tf_op jit(solution)/shard_map/ppermute | solution.py:57
  399.1 6.1 %collective-permute-start.17 = (f32[96,128]{1,0:T(8,128)S(1)}, f32[96,128]{1,0:T(8,128)S(1)}, u32[]{:S(2)}, u32[]{:S(2)}) collective-permute-start(f32[96,128]{1,0:T(8,128)S(1)} %bitcast.418), channel_id=1, source_target_pairs={{0,2},{2,0},{4,6},{6,4},{1,3},{3,1},{5,7},{7,5},{8,10},{10,8},{12,... | collective-permute-start | bytes 147464 | tf_op jit(solution)/shard_map/ppermute | solution.py:57
  399.3 20.4 %collective-permute-start.19 = (bf16[2,2,64,1536]{3,2,0,1:T(8,128)(2,1)S(1)}, bf16[2,2,64,1536]{3,2,0,1:T(8,128)(2,1)S(1)}, u32[]{:S(2)}, u32[]{:S(2)}) collective-permute-start(bf16[2,2,64,1536]{3,2,0,1:T(8,128)(2,1)S(1)} %dynamic-slice_bitcast_fusion.9), channel_id=1, source_target_pairs={{0,4},{2,6},{4,0},{6,2},{1,5},{3,7},{5,1},{7,3},{8,12},{10,14},{12... | collective-permute-start | bytes 2359304 | tf_op jit(solution)/shard_map/ppermute | solution.py:57
  399.9 20.5 %collective-permute-start.14 = (bf16[2,2,32,1024]{3,2,1,0:T(8,128)(2,1)S(1)}, bf16[2,2,32,1024]{3,2,1,0:T(8,128)(2,1)S(1)}, u32[]{:S(2)}, u32[]{:S(2)}) collective-permute-start(bf16[2,2,32,1024]{3,2,1,0:T(8,128)(2,1)S(1)} %dynamic-slice_bitcast_fusion.16), channel_id=1, source_target_pairs={{0,1},{1,0},{2,3},{3,2},{4,5},{5,4},{6,7},{7,6},{8,9},{9,8},{10,11... | collective-permute-start | bytes 786440 | tf_op jit(solution)/shard_map/ppermute | solution.py:57
  405.3 15.0 %collective-permute-start.18 = (f32[96,128]{1,0:T(8,128)S(1)}, f32[96,128]{1,0:T(8,128)S(1)}, u32[]{:S(2)}, u32[]{:S(2)}) collective-permute-start(f32[96,128]{1,0:T(8,128)S(1)} %add.411), channel_id=1, source_target_pairs={{0,4},{2,6},{4,0},{6,2},{1,5},{3,7},{5,1},{7,3},{8,12},{10,14},{12... | collective-permute-start | bytes 147464 | tf_op jit(solution)/shard_map/ppermute | solution.py:57
  405.7 14.6 %collective-permute-start.16 = (bf16[128,1024]{1,0:T(8,128)(2,1)S(1)}, bf16[128,1024]{1,0:T(8,128)(2,1)S(1)}, u32[]{:S(2)}, u32[]{:S(2)}) collective-permute-start(bf16[128,1024]{1,0:T(8,128)(2,1)S(1)} %fusion.52), channel_id=1, source_target_pairs={{0,16},{8,24},{16,0},{24,8},{1,17},{9,25},{17,1},{25,9},{2,18},{10... | collective-permute-start | bytes 786440 | tf_op jit(solution)/shard_map/ppermute | solution.py:57
  420.5 6.5 %collective-permute-start.23 = (bf16[2,32,1024]{2,1,0:T(8,128)(2,1)S(1)}, bf16[2,32,1024]{2,1,0:T(8,128)(2,1)S(1)}, u32[]{:S(2)}, u32[]{:S(2)}) collective-permute-start(bf16[2,32,1024]{2,1,0:T(8,128)(2,1)S(1)} %dynamic-slice_bitcast_fusion.18), channel_id=1, source_target_pairs={{0,8},{8,0},{16,24},{24,16},{1,9},{9,1},{17,25},{25,17},{2,10},{10... | collective-permute-start | bytes 393224 | tf_op jit(solution)/shard_map/ppermute | solution.py:57
  422.1 20.0 %collective-permute-start.25 = (bf16[2,32,4096]{2,1,0:T(8,128)(2,1)S(1)}, bf16[2,32,4096]{2,1,0:T(8,128)(2,1)S(1)}, u32[]{:S(2)}, u32[]{:S(2)}) collective-permute-start(bf16[2,32,4096]{2,1,0:T(8,128)(2,1)S(1)} %dynamic-slice_bitcast_fusion.10), channel_id=1, source_target_pairs={{0,8},{8,0},{16,24},{24,16},{1,9},{9,1},{17,25},{25,17},{2,10},{10... | collective-permute-start | bytes 1572872 | tf_op jit(solution)/shard_map/ppermute | solution.py:57
  422.7 6.5 %collective-permute-start.21 = (f32[96,128]{1,0:T(8,128)S(1)}, f32[96,128]{1,0:T(8,128)S(1)}, u32[]{:S(2)}, u32[]{:S(2)}) collective-permute-start(f32[96,128]{1,0:T(8,128)S(1)} %add.414), channel_id=1, source_target_pairs={{0,1},{1,0},{2,3},{3,2},{4,5},{5,4},{6,7},{7,6},{8,9},{9,8},{10,11... | collective-permute-start | bytes 147464 | tf_op jit(solution)/shard_map/ppermute | solution.py:57
  427.1 11.6 %collective-permute-start.31 = (bf16[32,1024]{1,0:T(8,128)(2,1)S(1)}, bf16[32,1024]{1,0:T(8,128)(2,1)S(1)}, u32[]{:S(2)}, u32[]{:S(2)}) collective-permute-start(bf16[32,1024]{1,0:T(8,128)(2,1)S(1)} %dynamic-slice_bitcast_fusion.19), channel_id=1, source_target_pairs={{0,16},{8,24},{16,0},{24,8},{1,17},{9,25},{17,1},{25,9},{2,18},{10... | collective-permute-start | bytes 196616 | tf_op jit(solution)/shard_map/ppermute | solution.py:57
  427.7 25.9 %collective-permute-start.24 = (bf16[2,64,1536]{2,1,0:T(8,128)(2,1)S(1)}, bf16[2,64,1536]{2,1,0:T(8,128)(2,1)S(1)}, u32[]{:S(2)}, u32[]{:S(2)}) collective-permute-start(bf16[2,64,1536]{2,1,0:T(8,128)(2,1)S(1)} %dynamic-slice_bitcast_fusion.13), channel_id=1, source_target_pairs={{0,8},{8,0},{16,24},{24,16},{1,9},{9,1},{17,25},{25,17},{2,10},{10... | collective-permute-start | bytes 1179656 | tf_op jit(solution)/shard_map/ppermute | solution.py:57
  429.3 45.0 %collective-permute-start.22 = (f32[96,128]{1,0:T(8,128)S(1)}, f32[96,128]{1,0:T(8,128)S(1)}, u32[]{:S(2)}, u32[]{:S(2)}) collective-permute-start(f32[96,128]{1,0:T(8,128)S(1)} %add.417), channel_id=1, source_target_pairs={{0,8},{8,0},{16,24},{24,16},{1,9},{9,1},{17,25},{25,17},{2,10},{10... | collective-permute-start | bytes 147464 | tf_op jit(solution)/shard_map/ppermute | solution.py:57
  438.7 10.9 %collective-permute-start.34 = (bf16[32,1024]{1,0:T(8,128)(2,1)S(1)}, bf16[32,1024]{1,0:T(8,128)(2,1)S(1)}, u32[]{:S(2)}, u32[]{:S(2)}) collective-permute-start(bf16[32,1024]{1,0:T(8,128)(2,1)S(1)} %fusion.58), channel_id=1, source_target_pairs={{0,16},{8,24},{16,0},{24,8},{1,17},{9,25},{17,1},{25,9},{2,18},{10... | collective-permute-start | bytes 196616 | tf_op jit(solution)/shard_map/ppermute | solution.py:57
  442.3 16.2 %collective-permute-start.28 = (bf16[32,4096]{1,0:T(8,128)(2,1)S(1)}, bf16[32,4096]{1,0:T(8,128)(2,1)S(1)}, u32[]{:S(2)}, u32[]{:S(2)}) collective-permute-start(bf16[32,4096]{1,0:T(8,128)(2,1)S(1)} %dynamic-slice_bitcast_fusion.14), channel_id=1, source_target_pairs={{0,16},{8,24},{16,0},{24,8},{1,17},{9,25},{17,1},{25,9},{2,18},{10... | collective-permute-start | bytes 786440 | tf_op jit(solution)/shard_map/ppermute | solution.py:57
  449.5 37.3 %collective-permute-start.35 = (bf16[2,32,1024]{2,1,0:T(8,128)(2,1)S(1)}, bf16[2,32,1024]{2,1,0:T(8,128)(2,1)S(1)}, u32[]{:S(2)}, u32[]{:S(2)}) collective-permute-start(bf16[2,32,1024]{2,1,0:T(8,128)(2,1)S(1)} %maximum_select_fusion.16), channel_id=1, source_target_pairs={{0,8},{8,0},{16,24},{24,16},{1,9},{9,1},{17,25},{25,17},{2,10},{10... | collective-permute-start | bytes 393224 | tf_op jit(solution)/shard_map/ppermute | solution.py:57
  453.7 20.5 %collective-permute-start.27 = (bf16[64,1536]{1,0:T(8,128)(2,1)S(1)}, bf16[64,1536]{1,0:T(8,128)(2,1)S(1)}, u32[]{:S(2)}, u32[]{:S(2)}) collective-permute-start(bf16[64,1536]{1,0:T(8,128)(2,1)S(1)} %dynamic-slice_bitcast_fusion.17), channel_id=1, source_target_pairs={{0,16},{8,24},{16,0},{24,8},{1,17},{9,25},{17,1},{25,9},{2,18},{10... | collective-permute-start | bytes 589832 | tf_op jit(solution)/shard_map/ppermute | solution.py:57
  458.6 29.7 %collective-permute-start.30 = (bf16[32,4096]{1,0:T(8,128)(2,1)S(1)}, bf16[32,4096]{1,0:T(8,128)(2,1)S(1)}, u32[]{:S(2)}, u32[]{:S(2)}) collective-permute-start(bf16[32,4096]{1,0:T(8,128)(2,1)S(1)} %fusion.51), channel_id=1, source_target_pairs={{0,16},{8,24},{16,0},{24,8},{1,17},{9,25},{17,1},{25,9},{2,18},{10... | collective-permute-start | bytes 786440 | tf_op jit(solution)/shard_map/ppermute | solution.py:57
  474.2 14.2 %collective-permute-start.29 = (bf16[64,1536]{1,0:T(8,128)(2,1)S(1)}, bf16[64,1536]{1,0:T(8,128)(2,1)S(1)}, u32[]{:S(2)}, u32[]{:S(2)}) collective-permute-start(bf16[64,1536]{1,0:T(8,128)(2,1)S(1)} %fusion.56), channel_id=1, source_target_pairs={{0,16},{8,24},{16,0},{24,8},{1,17},{9,25},{17,1},{25,9},{2,18},{10... | collective-permute-start | bytes 589832 | tf_op jit(solution)/shard_map/ppermute | solution.py:57
  474.3 12.5 %collective-permute-start.26 = (f32[96,128]{1,0:T(8,128)S(1)}, f32[96,128]{1,0:T(8,128)S(1)}, u32[]{:S(2)}, u32[]{:S(2)}) collective-permute-start(f32[96,128]{1,0:T(8,128)S(1)} %add.421), channel_id=1, source_target_pairs={{0,16},{8,24},{16,0},{24,8},{1,17},{9,25},{17,1},{25,9},{2,18},{10... | collective-permute-start | bytes 147464 | tf_op jit(solution)/shard_map/ppermute | solution.py:57
  477.2 20.8 %collective-permute-start.39 = (bf16[2,128,1024]{2,1,0:T(8,128)(2,1)S(1)}, bf16[2,128,1024]{2,1,0:T(8,128)(2,1)S(1)}, u32[]{:S(2)}, u32[]{:S(2)}) collective-permute-start(bf16[2,128,1024]{2,1,0:T(8,128)(2,1)S(1)} %maximum_select_fusion.11), channel_id=1, source_target_pairs={{0,8},{8,0},{16,24},{24,16},{1,9},{9,1},{17,25},{25,17},{2,10},{10... | collective-permute-start | bytes 1572872 | tf_op jit(solution)/shard_map/ppermute | solution.py:57
  486.9 12.9 %collective-permute-start.36 = (bf16[128,1024]{1,0:T(8,128)(2,1)S(1)}, bf16[128,1024]{1,0:T(8,128)(2,1)S(1)}, u32[]{:S(2)}, u32[]{:S(2)}) collective-permute-start(bf16[128,1024]{1,0:T(8,128)(2,1)S(1)} %bitcast.393), channel_id=1, source_target_pairs={{0,1},{1,0},{2,3},{3,2},{4,5},{5,4},{6,7},{7,6},{8,9},{9,8},{10,11... | collective-permute-start | bytes 786440 | tf_op jit(solution)/shard_map/ppermute | solution.py:57
  488.4 18.1 %collective-permute-start.32 = (bf16[2,64,1536]{2,1,0:T(8,128)(2,1)S(1)}, bf16[2,64,1536]{2,1,0:T(8,128)(2,1)S(1)}, u32[]{:S(2)}, u32[]{:S(2)}) collective-permute-start(bf16[2,64,1536]{2,1,0:T(8,128)(2,1)S(1)} %maximum_select_fusion.14), channel_id=1, source_target_pairs={{0,8},{8,0},{16,24},{24,16},{1,9},{9,1},{17,25},{25,17},{2,10},{10... | collective-permute-start | bytes 1179656 | tf_op jit(solution)/shard_map/ppermute | solution.py:57
  488.6 27.5 %collective-permute-start.37 = (bf16[2,32,4096]{2,1,0:T(8,128)(2,1)S(1)}, bf16[2,32,4096]{2,1,0:T(8,128)(2,1)S(1)}, u32[]{:S(2)}, u32[]{:S(2)}) collective-permute-start(bf16[2,32,4096]{2,1,0:T(8,128)(2,1)S(1)} %maximum_select_fusion.13), channel_id=1, source_target_pairs={{0,8},{8,0},{16,24},{24,16},{1,9},{9,1},{17,25},{25,17},{2,10},{10... | collective-permute-start | bytes 1572872 | tf_op jit(solution)/shard_map/ppermute | solution.py:57
  498.3 26.2 %collective-permute-start.40 = (bf16[512,1024]{1,0:T(8,128)(2,1)S(1)}, bf16[512,1024]{1,0:T(8,128)(2,1)S(1)}, u32[]{:S(2)}, u32[]{:S(2)}) collective-permute-start(bf16[512,1024]{1,0:T(8,128)(2,1)S(1)} %bitcast.374), channel_id=1, source_target_pairs={{0,1},{1,0},{2,3},{3,2},{4,5},{5,4},{6,7},{7,6},{8,9},{9,8},{10,11... | collective-permute-start | bytes 3145736 | tf_op jit(solution)/shard_map/ppermute | solution.py:57
  506.6 34.8 %collective-permute-start.33 = (bf16[1,256,1536]{2,1,0:T(8,128)(2,1)S(1)}, bf16[1,256,1536]{2,1,0:T(8,128)(2,1)S(1)}, u32[]{:S(2)}, u32[]{:S(2)}) collective-permute-start(bf16[1,256,1536]{2,1,0:T(8,128)(2,1)S(1)} %bitcast.380), channel_id=1, source_target_pairs={{0,1},{1,0},{2,3},{3,2},{4,5},{5,4},{6,7},{7,6},{8,9},{9,8},{10,11... | collective-permute-start | bytes 2359304 | tf_op jit(solution)/shard_map/ppermute | solution.py:57
  517.3 42.4 %collective-permute-start.38 = (bf16[128,4096]{1,0:T(8,128)(2,1)}, bf16[128,4096]{1,0:T(8,128)(2,1)}, u32[]{:S(2)}, u32[]{:S(2)}) collective-permute-start(bf16[128,4096]{1,0:T(8,128)(2,1)} %bitcast.100), channel_id=1, source_target_pairs={{0,1},{1,0},{2,3},{3,2},{4,5},{5,4},{6,7},{7,6},{8,9},{9,8},{10,11... | collective-permute-start | bytes 3145736 | tf_op jit(solution)/shard_map/ppermute | solution.py:57
  (25 other events, 104.8 us)
Sparse Core Ops, SparseCore 0:
  10.2 48.1 all-gather.4
  59.9 22.5 all-gather.6
  84.1 58.2 all-gather.8

commit v3 on v2

--- a/solution.py
+++ b/solution.py
@@ -160,6 +160,21 @@
 
 def pack(parts):
     return jnp.concatenate(parts).reshape(-1, 128)
+
+
+def pass_on_kernel(*refs):
+    refs[-1][...] = refs[0][...]
+
+
+def after_arrays(vector, ahead):
+    rows = vector.reshape(-1, 128)
+    return pl.pallas_call(
+        pass_on_kernel,
+        in_specs=[pl.BlockSpec(memory_space=pltpu.VMEM)]
+        + [pl.BlockSpec(memory_space=pl.ANY)] * len(ahead),
+        out_specs=pl.BlockSpec(memory_space=pltpu.VMEM),
+        out_shape=jax.ShapeDtypeStruct(rows.shape, rows.dtype),
+    )(rows, *ahead).reshape(vector.shape)
 
 
 def attend_forward_kernel(*refs, block, heads):
@@ -326,7 +341,7 @@
     fsdp_rank = lax.axis_index("fsdp")
 
     small = [ln1_gain, ln1_bias, qv_bias, dense_bias, ln2_gain, ln2_bias, fc1_bias, fc2_bias]
-    gathered = lax.all_gather(jnp.concatenate(small), "fsdp", axis=0).astype(jnp.float32)
+    gathered = gather(jnp.concatenate(small), "fsdp").astype(jnp.float32)
     vectors, place = [], 0
     for part in small:
         size = part.shape[0]
@@ -372,8 +387,7 @@
 
     tokens = hidden_in.reshape(token_rows, width).astype(jnp.float32)
     hidden = tokens + jnp.dot(attended, w_dense, preferred_element_type=jnp.float32) + bias_dense
-    normed_two_f, norm_pull_two = jax.vjp(norm_layer, hidden, gain_two, shift_two)
-    normed_two = normed_two_f.astype(jnp.bfloat16)
+    normed_two = norm_layer(hidden, gain_two, shift_two).astype(jnp.bfloat16)
     activation = jnp.dot(normed_two, w_up, preferred_element_type=jnp.float32) + bias_up
     gelu_f, gelu_pull = jax.vjp(gelu_tanh, activation)
     gelu_out = gelu_f.astype(jnp.bfloat16)
@@ -400,6 +414,9 @@
     up = sum_rows(g_w_up, order, every, [core, ranks, far, near_z, far_z], ("seq", "dp"))
     next(up)
     grad_normed_two = order(contract_cols(grad_act_low, w_up))
+    summed_down = next(down).value
+    late_gain = after_arrays(gain_two, [summed_down])
+    norm_pull_two = jax.vjp(norm_layer, hidden, late_gain, shift_two)[1]
     grad_hidden_norm, g_gain_two, g_shift_two = norm_pull_two(grad_normed_two)
     grad_hidden = grad_out_f + grad_hidden_norm
     grad_hidden_low = grad_hidden.astype(jnp.bfloat16)
@@ -417,7 +434,7 @@
     g_w_dense = order(contract_rows(attended, grad_hidden_low).astype(jnp.bfloat16))
     dense = sum_rows(g_w_dense, order, every, [core, far, ranks, near_z, far_z], ("seq", "dp"))
     next(dense)
-    ahead += [next(down).value, next(dense).value]
+    ahead += [summed_down, next(dense).value]
 
     grad_mixed = order(
         attend_backward(mixed, grad_heads, log_sums, doc_starts, slopes, ahead)

time: 576 us -> 604 us (1.049)
  waiting for transfers between devices: 195 us -> 253 us
  blocking collectives: 39.5 us -> 0 us
    ppermute x41 -> x43, waiting for transfers between devices: 181 us -> 233 us  [swap(): return lax.ppermute(value, axis, pairs)]
    all_gather x1 -> x0, blocking collectives: 39.5 us -> none  [per_device(): lax.all_gather(jnp.concatenate(small), 'fsdp', axis=0).astype(jnp.float32)]
    all_to_all x1, waiting for transfers between devices: 0.01 us -> 7.82 us  [per_device(): lax.all_to_all(grad_attended.reshape(seqs_here, local_len, width), 'seq',...]
    ppermute x41 -> x43, starting transfers between devices: 40.5 us -> 33.9 us  [swap(): return lax.ppermute(value, axis, pairs)]
    unnamed x119 -> x116, local copies, waits for them, and re-layouts: 22.3 us -> 25.1 us
    unnamed x5 -> x4, other arithmetic: 17.2 us -> 17.1 us
  transfers between devices with their start and end apart: 46 -> 48, of which waited for: 22 -> 23; matrix products, arithmetic and copies ran while one was open for 32% -> 31% of each run, Pallas kernels for 8% -> 8%
where the time goes in v3:
time: 604 us; the launch traced here: 594 us
  waiting for transfers between devices  253 us (42%)
  other arithmetic  88.5 us (15%)
  matrix products  84.5 us (14%)
  local copies, waits for them, and re-layouts  60.3 us (10%)
  Pallas kernels  49.7 us (8%)
  starting transfers between devices  42.8 us (7%)
  between operations  15.2 us (3%)
    ppermute x43, waiting for transfers between devices, swap(): return lax.ppermute(value, axis, pairs)  233 us
    ppermute x43, starting transfers between devices, swap(): return lax.ppermute(value, axis, pairs)  33.9 us
    dot_general x4, matrix products, contract_cols(): lax.dot_general(left_side, right_side, (((1,), (1,)), ((), ())), preferre...  31.9 us
    pallas_call x1, Pallas kernels, attend_backward(): pl.pallas_call(functools.partial(attend_backward_kernel, block=min(ROWS,...  27.8 us
    convert_element_type x20, other arithmetic, halves(): value = order((kept + received.astype(jnp.float32)).astype(jnp.bfloat16))  26.2 us
    unnamed x116, local copies, waits for them, and re-layouts  25.1 us
    pallas_call x1, Pallas kernels, attend_forward(): pl.pallas_call(functools.partial(attend_forward_kernel, block=min(ROWS, l...  20.5 us
    dot_general x4, matrix products, contract_rows(): lax.dot_general(left_side, right_side, (((0,), (0,)), ((), ())), preferre...  18.4 us
  transfers between devices with their start and end apart: 48, of which 23 were waited for; matrix products, arithmetic and copies ran while one was open for 31% of the time, Pallas kernels for 8%

profile of v3, /device:TPU:0, one launch (start us, length us, event | category | flops | bytes accessed | tf_op | source)
XLA Modules:
  0.0 593.8 jit_solution(14183678943092349561)
XLA Ops:
  13.4 2.6 collective-permute-start
  21.0 39.9 %collective-permute-done.2 = bf16[2,3072]{1,0:T(2,128)(2,1)S(1)} collective-permute-done((bf16[2,3072]{1,0:T(2,128)(2,1)S(1)}, bf16[2,3072]{1,0:T(2,128)(2,1)S(1)}, u32[]{:S(2)}, u32[]{:S(2)}) %collective-permute-start.2) | collective-permute-done | bytes 12320 | tf_op jit(solution)/shard_map/ppermute | solution.py:57
  63.3 3.4 fusion.15
  66.7 6.3 %fusion.16.refs_2_ = bf16[1,1024,1536]{2,1,0:T(8,128)(2,1)S(1)} fusion(bf16[1024,1024]{1,0:T(8,128)(2,1)} %fusion.15, bf16[1024,1536]{1,0:T(8,128)(2,1)} %all-gather.4.cloned.1.call-done, f32[1536]{0:T(1024)S(1)} %add.366), kind=kOutput, calls=%fused_computation.41 | convolution fusion | flops 3224371200 | bytes 8394752 | tf_op jit(solution)/shard_map/dot_general | solution.py:376
  73.0 20.5 %shard_map.254 = (bf16[1,1024,512]{2,1,0:T(8,128)(2,1)S(1)}, f32[1,4,2,1024]{3,2,1,0:T(2,128)S(1)}) custom-call(s32[1,1,1024]{2,1,0:T(1,128)S(1)} %bitcast.348, f32[8]{0:T(128)S(1)} %multiply_power_fusion.refs_1_, bf16[1,1024,1536]{2,1,0:T(8,128)(2,1)S(1)} %fusion.16.refs_2_, bf16[512,1024]{1,0:T(8,128)(2,1)S(1)} %collective-permute-done.3.refs_3_), custom_call_target="tpu_custom_call" | custom-call | flops 4294967296 | bytes 6291456 | tf_op jit(solution)/shard_map/pallas_call | solution.py:266
  93.6 2.9 copy.133
  97.0 9.0 %reduce.7 = bf16[1024,512]{1,0:T(8,128)(2,1)} reduce(bf16[1024,1,512]{2,1,0:T(2,128)(2,1)} %bitcast.373, bf16[]{:T(256)} %broadcast.407), dimensions={1}, to_apply=%bitcast.345.reduce_sub_computation | reduce | bytes 2097154
  106.0 2.6 reshape.849
  108.7 4.4 all-to-all-start
  116.5 2.7 maximum_select_fusion.2
  119.2 7.6 %all-to-all-done = bf16[2,2,131072]{2,1,0:T(2,128)(2,1)} async-done(((bf16[2,2,131072]{2,1,0:T(2,128)(2,1)}), bf16[2,2,131072]{2,1,0:T(2,128)(2,1)}, u32[]{:S(2)}, u32[]{:S(2)}) %all-to-all-start) | async-done | bytes 1048608 | tf_op jit(solution)/shard_map/all_to_all | solution.py:384
  126.8 2.9 reshape.850
  133.0 4.6 fusion.72
  139.5 3.0 all-gather.8.cloned.1.call-done
  142.5 12.7 %multiply_convert_fusion = (bf16[512,4096]{1,0:T(8,128)(2,1)S(1)}, f32[512,4096]{1,0:T(8,128)}) fusion(f32[4096]{0:T(1024)S(1)} %bitcast.426, bf16[1024,4096]{1,0:T(8,128)(2,1)} %all-gather.8.cloned.1.call-done, f32[512,1024]{1,0:T(8,128)} %get-tuple-element.396, f32[1024]{0:T(1024)S(1)} %bitcast.433, f32[1024]{0:T(1024)S(1)} %bitcast.431, ...), kind=kOutput, calls=%fused_computation.19 | convolution fusion | flops 4318560256 | bytes 23097344 | tf_op jit(solution)/shard_map/dot_general | solution.py:391
  155.2 4.8 convolution_convert_fusion.1
  160.0 3.1 dynamic-slice_bitcast_fusion.1
  165.6 4.2 maximum_select_fusion.1
  169.8 5.2 maximum_select_fusion
  175.0 8.6 %fusion.6 = bf16[2,2,2,2,128,1024]{5,4,3,2,1,0:T(8,128)(2,1)S(1)} fusion(bf16[2,2,2,2,128,1024]{5,4,3,2,1,0:T(8,128)(2,1)} %collective-permute-done.6, bf16[2,2,2,2,2,128,1024]{6,5,4,3,2,1,0:T(8,128)(2,1)} %bitcast.370, s32[]{:T(128)S(6)} %select_n.410), kind=kLoop, calls=%fused_computation.13 | loop fusion | flops 8388608 | bytes 12582916 | tf_op jit(solution)/shard_map/convert_element_type | solution.py:107
  183.7 13.4 %fusion.66 = (f32[4096]{0:T(1024)S(1)}, bf16[512,4096]{1,0:T(8,128)(2,1)S(1)}) fusion(f32[512,4096]{1,0:T(8,128)} %get-tuple-element.398, f32[4096]{0:T(1024)S(1)} %bitcast.427, bf16[4096,1024]{1,0:T(8,128)(2,1)S(1)} %bitcast.365, bf16[1,512,1024]{2,1,0:T(8,128)(2,1)S(1)} %copy-done.25), kind=kOutput, calls=%fused_computation.198 | convolution fusion | flops 4349489152 | bytes 22052864 | tf_op jit(solution)/shard_map/dot_general | solution.py:41
  199.1 6.8 %convolution_convert_fusion = bf16[1024,4096]{1,0:T(8,128)(2,1)S(1)} fusion(bf16[512,4096]{1,0:T(8,128)(2,1)S(1)} %get-tuple-element.165, f32[512,1024]{1,0:T(8,128)} %get-tuple-element.396, f32[1024]{0:T(1024)S(1)} %bitcast.434, f32[1024]{0:T(1024)S(1)} %bitcast.432, f32[512]{0:T(512)S(1)} %fusion.60, f32[512]{0:T(512)S(1)} %broadcast_multiply_fusion.2), kind=kOutput, calls=%fused_computation.20 | convolution fusion | flops 4301783040 | bytes 14692352 | tf_op jit(solution)/shard_map/dot_general | solution.py:35
  206.5 2.6 dynamic-slice_bitcast_fusion
  210.7 10.5 %fusion.73 = f32[512,1024]{1,0:T(8,128)} fusion(bf16[512,4096]{1,0:T(8,128)(2,1)} %copy-done.41, bf16[1024,4096]{1,0:T(8,128)(2,1)} %all-gather.8.cloned.1.call-done), kind=kOutput, calls=%fused_computation.205 | convolution fusion | flops 4294967296 | bytes 14680064 | tf_op jit(solution)/shard_map/dot_general | solution.py:41
  221.2 32.8 %collective-permute-done.7 = bf16[2,2,2,128,1024]{4,3,2,1,0:T(8,128)(2,1)S(1)} collective-permute-done((bf16[2,2,2,128,1024]{4,3,2,1,0:T(8,128)(2,1)S(1)}, bf16[2,2,2,128,1024]{4,3,2,1,0:T(8,128)(2,1)S(1)}, u32[]{:S(2)}, u32[]{:S(2)}) %collective-permute-start.7) | collective-permute-done | bytes 2097184 | tf_op jit(solution)/shard_map/ppermute | solution.py:57
  254.0 2.3 fusion.11.refs_1_.refs_6_
  257.6 3.1 multiply_reduce_fusion.1
  260.7 2.5 fusion.68
  265.5 6.1 %copy.97 = bf16[1,512,1024]{1,0,2:T(2,128)(2,1)} copy(bf16[1,512,1024]{2,1,0:T(8,128)(2,1)} %bitcast.393) | data formatting | bytes 2097152 | tf_op jit(solution)/shard_map/reshape | solution.py:426
  271.7 8.0 %reduce.8 = bf16[1024,512]{1,0:T(8,128)(2,1)S(1)} reduce(bf16[1024,1,512]{2,1,0:T(2,128)(2,1)} %bitcast.374, bf16[]{:T(256)} %broadcast.407), dimensions={1}, to_apply=%bitcast.321.reduce_sub_computation | reduce | bytes 2097154
  281.3 4.4 all-to-all-start.1
  285.8 2.4 add_convert_fusion.1
  288.7 2.8 convolution_convert_fusion.3
  291.5 7.8 %all-to-all-done.1 = bf16[2,2,131072]{2,1,0:T(2,128)(2,1)} async-done(((bf16[2,2,131072]{2,1,0:T(2,128)(2,1)}), bf16[2,2,131072]{2,1,0:T(2,128)(2,1)}, u32[]{:S(2)}, u32[]{:S(2)}) %all-to-all-start.1) | async-done | bytes 1048608 | tf_op jit(solution)/shard_map/all_to_all | solution.py:425
  302.9 5.2 fusion.5.refs_5_
  308.3 10.6 %add_convert_fusion.3 = bf16[512,1024]{1,0:T(8,128)(2,1)} fusion(f32[512,1024]{1,0:T(8,128)} %get-tuple-element.396, bf16[512,4096]{1,0:T(8,128)(2,1)S(1)} %copy-done.40, bf16[4096,1024]{1,0:T(8,128)(2,1)} %bitcast.366, f32[1024]{0:T(1024)S(1)} %bitcast.435), kind=kOutput, calls=%fused_computation.88 | convolution fusion | flops 4296540160 | bytes 15732736 | tf_op jit(solution)/shard_map/dot_general | solution.py:493
  323.9 27.8 %shard_map.256 = bf16[1,1024,1536]{2,1,0:T(8,128)(2,1)} custom-call(s32[1,1,1024]{2,1,0:T(1,128)S(1)} %bitcast.349, f32[8]{0:T(128)S(1)} %multiply_power_fusion.refs_1_, bf16[1,1024,1536]{2,1,0:T(8,128)(2,1)} %copy-done.4, bf16[1,1024,512]{2,1,0:T(8,128)(2,1)S(1)} %bitcast.347, f32[1,4,2,1024]{3,2,1,0:T(2,128)S(1)} %get-tuple-element.188.refs_4_, ...), custom_call_target="tpu_custom_call" | custom-call | flops 10737418240 | bytes 9437184 | tf_op jit(solution)/shard_map/pallas_call | solution.py:293
  351.8 5.7 fusion.38
  357.5 4.0 convolution_convert_fusion.2
  367.9 23.4 %collective-permute-done.14 = bf16[2,2,2,32,4096]{4,3,2,1,0:T(8,128)(2,1)} collective-permute-done((bf16[2,2,2,32,4096]{4,3,2,1,0:T(8,128)(2,1)}, bf16[2,2,2,32,4096]{4,3,2,1,0:T(8,128)(2,1)}, u32[]{:S(2)}, u32[]{:S(2)}) %collective-permute-start.14) | collective-permute-done | bytes 2097184 | tf_op jit(solution)/shard_map/ppermute | solution.py:57
  391.3 3.0 fusion.10
  400.3 11.7 %collective-permute-done.11 = bf16[1,512,1024]{2,1,0:T(8,128)(2,1)} collective-permute-done((bf16[1,512,1024]{2,1,0:T(8,128)(2,1)}, bf16[1,512,1024]{2,1,0:T(8,128)(2,1)}, u32[]{:S(2)}, u32[]{:S(2)}) %collective-permute-start.11) | collective-permute-done | bytes 1048608 | tf_op jit(solution)/shard_map/ppermute | solution.py:57
  413.9 2.5 collective-permute-start.17
  422.4 4.7 collective-permute-done.17
  427.9 13.9 %collective-permute-done.21 = bf16[2,2,64,1536]{3,2,0,1:T(8,128)(2,1)S(1)} collective-permute-done((bf16[2,2,64,1536]{3,2,0,1:T(8,128)(2,1)S(1)}, bf16[2,2,64,1536]{3,2,0,1:T(8,128)(2,1)S(1)}, u32[]{:S(2)}, u32[]{:S(2)}) %collective-permute-start.21) | collective-permute-done | bytes 786464 | tf_op jit(solution)/shard_map/ppermute | solution.py:57
  445.1 4.0 collective-permute-done.25
  451.9 8.8 %collective-permute-done.33 = bf16[32,1024]{1,0:T(8,128)(2,1)S(1)} collective-permute-done((bf16[32,1024]{1,0:T(8,128)(2,1)S(1)}, bf16[32,1024]{1,0:T(8,128)(2,1)S(1)}, u32[]{:S(2)}, u32[]{:S(2)}) %collective-permute-start.33) | collective-permute-done | bytes 65568 | tf_op jit(solution)/shard_map/ppermute | solution.py:57
  460.8 3.4 collective-permute-start.36
  464.5 7.2 %collective-permute-done.36 = bf16[32,1024]{1,0:T(8,128)(2,1)S(1)} collective-permute-done((bf16[32,1024]{1,0:T(8,128)(2,1)S(1)}, bf16[32,1024]{1,0:T(8,128)(2,1)S(1)}, u32[]{:S(2)}, u32[]{:S(2)}) %collective-permute-start.36) | collective-permute-done | bytes 65568 | tf_op jit(solution)/shard_map/ppermute | solution.py:57
  476.9 3.8 collective-permute-done.30
  480.8 15.4 %collective-permute-done.29 = bf16[64,1536]{1,0:T(8,128)(2,1)S(1)} collective-permute-done((bf16[64,1536]{1,0:T(8,128)(2,1)S(1)}, bf16[64,1536]{1,0:T(8,128)(2,1)S(1)}, u32[]{:S(2)}, u32[]{:S(2)}) %collective-permute-start.29) | collective-permute-done | bytes 196640 | tf_op jit(solution)/shard_map/ppermute | solution.py:57
  496.4 3.0 collective-permute-start.28
  499.4 9.5 %collective-permute-done.28 = f32[96,128]{1,0:T(8,128)S(1)} collective-permute-done((f32[96,128]{1,0:T(8,128)S(1)}, f32[96,128]{1,0:T(8,128)S(1)}, u32[]{:S(2)}, u32[]{:S(2)}) %collective-permute-start.28) | collective-permute-done | bytes 49184 | tf_op jit(solution)/shard_map/ppermute | solution.py:57
  513.5 6.7 %collective-permute-done.41 = bf16[2,128,1024]{2,1,0:T(8,128)(2,1)S(1)} collective-permute-done((bf16[2,128,1024]{2,1,0:T(8,128)(2,1)S(1)}, bf16[2,128,1024]{2,1,0:T(8,128)(2,1)S(1)}, u32[]{:S(2)}, u32[]{:S(2)}) %collective-permute-start.41) | collective-permute-done | bytes 524320 | tf_op jit(solution)/shard_map/ppermute | solution.py:57
  520.9 7.7 %collective-permute-done.34 = bf16[2,64,1536]{2,1,0:T(8,128)(2,1)S(1)} collective-permute-done((bf16[2,64,1536]{2,1,0:T(8,128)(2,1)S(1)}, bf16[2,64,1536]{2,1,0:T(8,128)(2,1)S(1)}, u32[]{:S(2)}, u32[]{:S(2)}) %collective-permute-start.34) | collective-permute-done | bytes 393248 | tf_op jit(solution)/shard_map/ppermute | solution.py:57
  529.1 9.1 %collective-permute-done.39 = bf16[2,32,4096]{2,1,0:T(8,128)(2,1)S(1)} collective-permute-done((bf16[2,32,4096]{2,1,0:T(8,128)(2,1)S(1)}, bf16[2,32,4096]{2,1,0:T(8,128)(2,1)S(1)}, u32[]{:S(2)}, u32[]{:S(2)}) %collective-permute-start.39) | collective-permute-done | bytes 524320 | tf_op jit(solution)/shard_map/ppermute | solution.py:57
  540.8 5.8 collective-permute-done.42
  547.0 2.6 bitcast_convert_fusion
  549.6 13.9 %collective-permute-done.35 = bf16[1,256,1536]{2,1,0:T(8,128)(2,1)S(1)} collective-permute-done((bf16[1,256,1536]{2,1,0:T(8,128)(2,1)S(1)}, bf16[1,256,1536]{2,1,0:T(8,128)(2,1)S(1)}, u32[]{:S(2)}, u32[]{:S(2)}) %collective-permute-start.35) | collective-permute-done | bytes 786464 | tf_op jit(solution)/shard_map/ppermute | solution.py:57
  563.7 2.4 copy.102
  566.1 3.5 copy.109
  569.6 12.1 %collective-permute-done.40 = bf16[128,4096]{1,0:T(8,128)(2,1)} collective-permute-done((bf16[128,4096]{1,0:T(8,128)(2,1)}, bf16[128,4096]{1,0:T(8,128)(2,1)}, u32[]{:S(2)}, u32[]{:S(2)}) %collective-permute-start.40) | collective-permute-done | bytes 1048608 | tf_op jit(solution)/shard_map/ppermute | solution.py:57
  581.8 2.7 maximum_select_fusion.5
  584.4 2.6 bitcast_convert_fusion.1
  (293 shorter events, 85.2 us)
Async XLA Ops:
  7.2 59.5 %all-gather.4.cloned.1.call-start = ((), (), s32[]{:S(2)}) async-start(), calls=%async_computation.2 | async-start | bytes 3932160 | tf_op jit(solution)/shard_map/all_gather | solution.py:355
  9.6 123.4 %all-gather.6.cloned.1.call-start = ((), (), s32[]{:S(2)}) async-start(), calls=%async_computation.3 | async-start | bytes 2621440 | tf_op jit(solution)/shard_map/all_gather | solution.py:356
  10.4 9.4 %copy-start.38 = (s32[1,4]{1,0:T(1,128)S(1)}, s32[1,4]{1,0:T(1,128)}, u32[]{:S(2)}) copy-start(s32[1,4]{1,0:T(1,128)} %param.16) | copy-start | bytes 52
  10.4 132.1 %all-gather.8.cloned.1.call-start = ((), (), s32[]{:S(2)}) async-start(), calls=%async_computation.4 | async-start | bytes 10485760 | tf_op jit(solution)/shard_map/all_gather | solution.py:357
  12.9 7.3 %collective-permute-start.1 = (bf16[1,3072]{1,0:T(2,128)(2,1)S(1)}, bf16[1,3072]{1,0:T(2,128)(2,1)S(1)}, u32[]{:S(2)}, u32[]{:S(2)}) collective-permute-start(bf16[1,3072]{1,0:T(2,128)(2,1)S(1)} %broadcast_in_dim.51), channel_id=1, source_target_pairs={{0,2},{2,0},{4,6},{6,4},{1,3},{3,1},{5,7},{7,5},{8,10},{10,8},{12,... | collective-permute-start | bytes 18440 | tf_op jit(solution)/shard_map/ppermute | solution.py:57
  13.4 47.8 %collective-permute-start = (bf16[1,1,512,1024]{3,2,1,0:T(8,128)(2,1)S(1)}, bf16[1,1,512,1024]{3,2,1,0:T(8,128)(2,1)S(1)}, u32[]{:S(2)}, u32[]{:S(2)}) collective-permute-start(bf16[1,1,512,1024]{3,2,1,0:T(8,128)(2,1)S(1)} %bitcast.350), channel_id=1, source_target_pairs={{0,1},{1,0},{2,3},{3,2},{4,5},{5,4},{6,7},{7,6},{8,9},{9,8},{10,11... | collective-permute-start | bytes 3145736 | tf_op jit(solution)/shard_map/ppermute | solution.py:57
  18.3 44.6 %collective-permute-start.3 = (bf16[512,1024]{1,0:T(8,128)(2,1)}, bf16[512,1024]{1,0:T(8,128)(2,1)S(1)}, u32[]{:S(2)}, u32[]{:S(2)}) collective-permute-start(bf16[512,1024]{1,0:T(8,128)(2,1)} %dynamic-slice_bitcast_fusion.8), channel_id=1, source_target_pairs={{0,4},{2,6},{4,0},{6,2},{1,5},{3,7},{5,1},{7,3},{8,12},{10,14},{12... | collective-permute-start | bytes 3145736 | tf_op jit(solution)/shard_map/ppermute | solution.py:57
  20.3 40.6 %collective-permute-start.2 = (bf16[2,3072]{1,0:T(2,128)(2,1)S(1)}, bf16[2,3072]{1,0:T(2,128)(2,1)S(1)}, u32[]{:S(2)}, u32[]{:S(2)}) collective-permute-start(bf16[2,3072]{1,0:T(2,128)(2,1)S(1)} %broadcast_select_fusion.1), channel_id=1, source_target_pairs={{0,4},{2,6},{4,0},{6,2},{1,5},{3,7},{5,1},{7,3},{8,12},{10,14},{12... | collective-permute-start | bytes 36872 | tf_op jit(solution)/shard_map/ppermute | solution.py:57
  63.0 50.1 %collective-permute-start.4 = (bf16[512,1024]{1,0:T(8,128)(2,1)S(1)}, bf16[512,1024]{1,0:T(8,128)(2,1)}, u32[]{:S(2)}, u32[]{:S(2)}) collective-permute-start(bf16[512,1024]{1,0:T(8,128)(2,1)S(1)} %collective-permute-done.3.refs_3_), channel_id=1, source_target_pairs={{0,1},{1,0},{2,3},{3,2},{4,5},{5,4},{6,7},{7,6},{8,9},{9,8},{10,11... | collective-permute-start | bytes 3145736 | tf_op jit(solution)/shard_map/ppermute | solution.py:57
  73.0 20.6 %copy-start.4 = (bf16[1,1024,1536]{2,1,0:T(8,128)(2,1)}, bf16[1,1024,1536]{2,1,0:T(8,128)(2,1)S(1)}, u32[]{:S(2)}) copy-start(bf16[1,1024,1536]{2,1,0:T(8,128)(2,1)S(1)} %fusion.16.refs_2_) | copy-start | bytes 9437188
  108.7 18.1 %all-to-all-start = ((bf16[2,2,131072]{2,1,0:T(2,128)(2,1)}), bf16[2,2,131072]{2,1,0:T(2,128)(2,1)}, u32[]{:S(2)}, u32[]{:S(2)}) async-start(bf16[2,2,131072]{2,1,0:T(2,128)(2,1)} %reshape.849), calls=%async_computation | async-start | bytes 2097152 | tf_op jit(solution)/shard_map/all_to_all | solution.py:384
  119.2 50.6 %collective-permute-start.5 = (bf16[2,1024,1024]{2,1,0:T(8,128)(2,1)}, bf16[2,1024,1024]{2,1,0:T(8,128)(2,1)}, u32[]{:S(2)}, u32[]{:S(2)}) collective-permute-start(bf16[2,1024,1024]{2,1,0:T(8,128)(2,1)} %maximum_select_fusion.2), channel_id=1, source_target_pairs={{0,2},{2,0},{4,6},{6,4},{1,3},{3,1},{5,7},{7,5},{8,10},{10,8},{12,... | collective-permute-start | bytes 12582920 | tf_op jit(solution)/shard_map/ppermute | solution.py:57
  142.5 12.7 %copy-start.25 = (bf16[1,512,1024]{2,1,0:T(8,128)(2,1)S(1)}, bf16[1,512,1024]{2,1,0:T(8,128)(2,1)}, u32[]{:S(2)}) copy-start(bf16[1,512,1024]{2,1,0:T(8,128)(2,1)} %param.29) | copy-start | bytes 3145732
  155.2 4.8 copy-start.39
  164.6 10.5 %collective-permute-start.6 = (bf16[2,2,2,2,128,1024]{5,4,3,2,1,0:T(8,128)(2,1)}, bf16[2,2,2,2,128,1024]{5,4,3,2,1,0:T(8,128)(2,1)}, u32[]{:S(2)}, u32[]{:S(2)}) collective-permute-start(bf16[2,2,2,2,128,1024]{5,4,3,2,1,0:T(8,128)(2,1)} %dynamic-slice_bitcast_fusion.1), channel_id=1, source_target_pairs={{0,2},{2,0},{4,6},{6,4},{1,3},{3,1},{5,7},{7,5},{8,10},{10,8},{12,... | collective-permute-start | bytes 12582920 | tf_op jit(solution)/shard_map/ppermute | solution.py:57
  175.0 8.7 %copy-start.10 = (bf16[2,2,1024,1024]{3,2,1,0:T(8,128)(2,1)}, bf16[2,2,1024,1024]{3,2,1,0:T(8,128)(2,1)S(1)}, u32[]{:S(2)}) copy-start(bf16[2,2,1024,1024]{3,2,1,0:T(8,128)(2,1)S(1)} %maximum_select_fusion) | copy-start | bytes 25165828
  206.1 47.8 %collective-permute-start.7 = (bf16[2,2,2,128,1024]{4,3,2,1,0:T(8,128)(2,1)S(1)}, bf16[2,2,2,128,1024]{4,3,2,1,0:T(8,128)(2,1)S(1)}, u32[]{:S(2)}, u32[]{:S(2)}) collective-permute-start(bf16[2,2,2,128,1024]{4,3,2,1,0:T(8,128)(2,1)S(1)} %dynamic-slice_bitcast_fusion.3), channel_id=1, source_target_pairs={{0,4},{2,6},{4,0},{6,2},{1,5},{3,7},{5,1},{7,3},{8,12},{10,14},{12... | collective-permute-start | bytes 6291464 | tf_op jit(solution)/shard_map/ppermute | solution.py:57
  210.4 92.5 %collective-permute-start.8 = (bf16[2,2,2,2,32,4096]{5,4,3,2,1,0:T(8,128)(2,1)}, bf16[2,2,2,2,32,4096]{5,4,3,2,1,0:T(8,128)(2,1)}, u32[]{:S(2)}, u32[]{:S(2)}) collective-permute-start(bf16[2,2,2,2,32,4096]{5,4,3,2,1,0:T(8,128)(2,1)} %dynamic-slice_bitcast_fusion), channel_id=1, source_target_pairs={{0,2},{2,0},{4,6},{6,4},{1,3},{3,1},{5,7},{7,5},{8,10},{10,8},{12,... | collective-permute-start | bytes 12582920 | tf_op jit(solution)/shard_map/ppermute | solution.py:57
  281.3 18.0 %all-to-all-start.1 = ((bf16[2,2,131072]{2,1,0:T(2,128)(2,1)}), bf16[2,2,131072]{2,1,0:T(2,128)(2,1)}, u32[]{:S(2)}, u32[]{:S(2)}) async-start(bf16[2,2,131072]{2,1,0:T(2,128)(2,1)} %reshape.851), calls=%async_computation.1 | async-start | bytes 2097152 | tf_op jit(solution)/shard_map/all_to_all | solution.py:425
  302.9 5.2 copy-start.22
  302.9 5.4 copy-start.40
  308.1 12.2 %copy-start.8 = (bf16[2,2,2,2,32,4096]{5,4,3,2,1,0:T(8,128)(2,1)}, bf16[2,2,2,2,32,4096]{5,4,3,2,1,0:T(8,128)(2,1)S(1)}, u32[]{:S(2)}) copy-start(bf16[2,2,2,2,32,4096]{5,4,3,2,1,0:T(8,128)(2,1)S(1)} %fusion.5.refs_5_) | copy-start | bytes 12582916
  308.2 15.3 %collective-permute-start.9 = (bf16[2,2,2,2,32,1024]{5,4,3,2,1,0:T(8,128)(2,1)S(1)}, bf16[2,2,2,2,32,1024]{5,4,3,2,1,0:T(8,128)(2,1)S(1)}, u32[]{:S(2)}, u32[]{:S(2)}) collective-permute-start(bf16[2,2,2,2,32,1024]{5,4,3,2,1,0:T(8,128)(2,1)S(1)} %dynamic-slice_bitcast_fusion.7), channel_id=1, source_target_pairs={{0,2},{2,0},{4,6},{6,4},{1,3},{3,1},{5,7},{7,5},{8,10},{10,8},{12,... | collective-permute-start | bytes 3145736 | tf_op jit(solution)/shard_map/ppermute | solution.py:57
  308.3 10.7 %copy-start.2 = (bf16[2,2,2,128,1024]{4,3,2,1,0:T(8,128)(2,1)S(1)}, bf16[2,2,2,128,1024]{4,3,2,1,0:T(8,128)(2,1)}, u32[]{:S(2)}) copy-start(bf16[2,2,2,128,1024]{4,3,2,1,0:T(8,128)(2,1)} %fusion.11.refs_1_.refs_6_) | copy-start | bytes 6291460
  320.0 74.4 %collective-permute-start.13 = (bf16[2,2,128,1024]{3,2,1,0:T(8,128)(2,1)}, bf16[2,2,128,1024]{3,2,1,0:T(8,128)(2,1)}, u32[]{:S(2)}, u32[]{:S(2)}) collective-permute-start(bf16[2,2,128,1024]{3,2,1,0:T(8,128)(2,1)} %dynamic-slice_bitcast_fusion.5), channel_id=1, source_target_pairs={{0,1},{1,0},{2,3},{3,2},{4,5},{5,4},{6,7},{7,6},{8,9},{9,8},{10,11... | collective-permute-start | bytes 3145736 | tf_op jit(solution)/shard_map/ppermute | solution.py:57
  321.7 69.6 %collective-permute-start.14 = (bf16[2,2,2,32,4096]{4,3,2,1,0:T(8,128)(2,1)}, bf16[2,2,2,32,4096]{4,3,2,1,0:T(8,128)(2,1)}, u32[]{:S(2)}, u32[]{:S(2)}) collective-permute-start(bf16[2,2,2,32,4096]{4,3,2,1,0:T(8,128)(2,1)} %dynamic-slice_bitcast_fusion.2), channel_id=1, source_target_pairs={{0,1},{1,0},{2,3},{3,2},{4,5},{5,4},{6,7},{7,6},{8,9},{9,8},{10,11... | collective-permute-start | bytes 6291464 | tf_op jit(solution)/shard_map/ppermute | solution.py:57
  323.9 27.9 %copy-start.37 = (bf16[1024,1536]{1,0:T(8,128)(2,1)S(1)}, bf16[1024,1536]{1,0:T(8,128)(2,1)}, u32[]{:S(2)}) copy-start(bf16[1024,1536]{1,0:T(8,128)(2,1)} %all-gather.4.cloned.1.call-done) | copy-start | bytes 9437188
  351.8 5.7 copy-start.19
  351.8 5.8 copy-start.24
  357.5 6.8 %copy-start.20 = (bf16[1024,1024]{1,0:T(8,128)(2,1)}, bf16[1024,1024]{1,0:T(8,128)(2,1)S(1)}, u32[]{:S(2)}) copy-start(bf16[1024,1024]{1,0:T(8,128)(2,1)S(1)} %fusion.38) | copy-start | bytes 6291460
  364.3 34.0 %collective-permute-start.12 = (bf16[2,2,2,64,1536]{4,3,1,2,0:T(8,128)(2,1)}, bf16[2,2,2,64,1536]{4,3,1,2,0:T(8,128)(2,1)}, u32[]{:S(2)}, u32[]{:S(2)}) collective-permute-start(bf16[2,2,2,64,1536]{4,3,1,2,0:T(8,128)(2,1)} %bitcast.343), channel_id=1, source_target_pairs={{0,2},{2,0},{4,6},{6,4},{1,3},{3,1},{5,7},{7,5},{8,10},{10,8},{12,... | collective-permute-start | bytes 4718600 | tf_op jit(solution)/shard_map/ppermute | solution.py:57
  365.3 46.7 %collective-permute-start.11 = (bf16[1,512,1024]{2,1,0:T(8,128)(2,1)}, bf16[1,512,1024]{2,1,0:T(8,128)(2,1)}, u32[]{:S(2)}, u32[]{:S(2)}) collective-permute-start(bf16[1,512,1024]{2,1,0:T(8,128)(2,1)} %dynamic-slice_bitcast_fusion.6), channel_id=1, source_target_pairs={{0,1},{1,0},{2,3},{3,2},{4,5},{5,4},{6,7},{7,6},{8,9},{9,8},{10,11... | collective-permute-start | bytes 3145736 | tf_op jit(solution)/shard_map/ppermute | solution.py:57
  367.6 53.4 %collective-permute-start.10 = (bf16[2,2,2,32,1024]{4,3,2,1,0:T(8,128)(2,1)}, bf16[2,2,2,32,1024]{4,3,2,1,0:T(8,128)(2,1)S(1)}, u32[]{:S(2)}, u32[]{:S(2)}) collective-permute-start(bf16[2,2,2,32,1024]{4,3,2,1,0:T(8,128)(2,1)} %dynamic-slice_bitcast_fusion.12), channel_id=1, source_target_pairs={{0,4},{2,6},{4,0},{6,2},{1,5},{3,7},{5,1},{7,3},{8,12},{10,14},{12... | collective-permute-start | bytes 1572872 | tf_op jit(solution)/shard_map/ppermute | solution.py:57
  396.0 17.6 %collective-permute-start.15 = (bf16[2,128,1024]{2,1,0:T(8,128)(2,1)S(1)}, bf16[2,128,1024]{2,1,0:T(8,128)(2,1)S(1)}, u32[]{:S(2)}, u32[]{:S(2)}) collective-permute-start(bf16[2,128,1024]{2,1,0:T(8,128)(2,1)S(1)} %dynamic-slice_bitcast_fusion.11), channel_id=1, source_target_pairs={{0,8},{8,0},{16,24},{24,16},{1,9},{9,1},{17,25},{25,17},{2,10},{10... | collective-permute-start | bytes 1572872 | tf_op jit(solution)/shard_map/ppermute | solution.py:57
  397.7 29.9 %collective-permute-start.22 = (bf16[2,2,32,4096]{3,2,1,0:T(8,128)(2,1)S(1)}, bf16[2,2,32,4096]{3,2,1,0:T(8,128)(2,1)S(1)}, u32[]{:S(2)}, u32[]{:S(2)}) collective-permute-start(bf16[2,2,32,4096]{3,2,1,0:T(8,128)(2,1)S(1)} %dynamic-slice_bitcast_fusion.4), channel_id=1, source_target_pairs={{0,4},{2,6},{4,0},{6,2},{1,5},{3,7},{5,1},{7,3},{8,12},{10,14},{12... | collective-permute-start | bytes 3145736 | tf_op jit(solution)/shard_map/ppermute | solution.py:57
  398.3 13.7 %copy-start.21 = (bf16[1024,1024]{1,0:T(8,128)(2,1)S(1)}, bf16[1024,1024]{1,0:T(8,128)(2,1)}, u32[]{:S(2)}) copy-start(bf16[1024,1024]{1,0:T(8,128)(2,1)} %copy-done.20) | copy-start | bytes 6291460
  400.3 16.1 %copy-start.6 = (bf16[1,512,1024]{2,1,0:T(8,128)(2,1)S(1)}, bf16[1,512,1024]{2,1,0:T(8,128)(2,1)}, u32[]{:S(2)}) copy-start(bf16[1,512,1024]{2,1,0:T(8,128)(2,1)} %param.15) | copy-start | bytes 3145732
  413.9 13.2 %collective-permute-start.17 = (bf16[128,1024]{1,0:T(8,128)(2,1)S(1)}, bf16[128,1024]{1,0:T(8,128)(2,1)S(1)}, u32[]{:S(2)}, u32[]{:S(2)}) collective-permute-start(bf16[128,1024]{1,0:T(8,128)(2,1)S(1)} %dynamic-slice_bitcast_fusion.15), channel_id=1, source_target_pairs={{0,16},{8,24},{16,0},{24,8},{1,17},{9,25},{17,1},{25,9},{2,18},{10... | collective-permute-start | bytes 786440 | tf_op jit(solution)/shard_map/ppermute | solution.py:57
  421.2 5.9 %collective-permute-start.19 = (f32[96,128]{1,0:T(8,128)S(1)}, f32[96,128]{1,0:T(8,128)S(1)}, u32[]{:S(2)}, u32[]{:S(2)}) collective-permute-start(f32[96,128]{1,0:T(8,128)S(1)} %bitcast.419), channel_id=1, source_target_pairs={{0,2},{2,0},{4,6},{6,4},{1,3},{3,1},{5,7},{7,5},{8,10},{10,8},{12,... | collective-permute-start | bytes 147464 | tf_op jit(solution)/shard_map/ppermute | solution.py:57
  421.4 20.4 %collective-permute-start.21 = (bf16[2,2,64,1536]{3,2,0,1:T(8,128)(2,1)S(1)}, bf16[2,2,64,1536]{3,2,0,1:T(8,128)(2,1)S(1)}, u32[]{:S(2)}, u32[]{:S(2)}) collective-permute-start(bf16[2,2,64,1536]{3,2,0,1:T(8,128)(2,1)S(1)} %dynamic-slice_bitcast_fusion.9), channel_id=1, source_target_pairs={{0,4},{2,6},{4,0},{6,2},{1,5},{3,7},{5,1},{7,3},{8,12},{10,14},{12... | collective-permute-start | bytes 2359304 | tf_op jit(solution)/shard_map/ppermute | solution.py:57
  422.0 20.5 %collective-permute-start.16 = (bf16[2,2,32,1024]{3,2,1,0:T(8,128)(2,1)S(1)}, bf16[2,2,32,1024]{3,2,1,0:T(8,128)(2,1)S(1)}, u32[]{:S(2)}, u32[]{:S(2)}) collective-permute-start(bf16[2,2,32,1024]{3,2,1,0:T(8,128)(2,1)S(1)} %dynamic-slice_bitcast_fusion.16), channel_id=1, source_target_pairs={{0,1},{1,0},{2,3},{3,2},{4,5},{5,4},{6,7},{7,6},{8,9},{9,8},{10,11... | collective-permute-start | bytes 786440 | tf_op jit(solution)/shard_map/ppermute | solution.py:57
  427.2 15.2 %collective-permute-start.20 = (f32[96,128]{1,0:T(8,128)S(1)}, f32[96,128]{1,0:T(8,128)S(1)}, u32[]{:S(2)}, u32[]{:S(2)}) collective-permute-start(f32[96,128]{1,0:T(8,128)S(1)} %add.412), channel_id=1, source_target_pairs={{0,4},{2,6},{4,0},{6,2},{1,5},{3,7},{5,1},{7,3},{8,12},{10,14},{12... | collective-permute-start | bytes 147464 | tf_op jit(solution)/shard_map/ppermute | solution.py:57
  427.6 14.8 %collective-permute-start.18 = (bf16[128,1024]{1,0:T(8,128)(2,1)S(1)}, bf16[128,1024]{1,0:T(8,128)(2,1)S(1)}, u32[]{:S(2)}, u32[]{:S(2)}) collective-permute-start(bf16[128,1024]{1,0:T(8,128)(2,1)S(1)} %fusion.52), channel_id=1, source_target_pairs={{0,16},{8,24},{16,0},{24,8},{1,17},{9,25},{17,1},{25,9},{2,18},{10... | collective-permute-start | bytes 786440 | tf_op jit(solution)/shard_map/ppermute | solution.py:57
  442.7 6.5 %collective-permute-start.25 = (bf16[2,32,1024]{2,1,0:T(8,128)(2,1)S(1)}, bf16[2,32,1024]{2,1,0:T(8,128)(2,1)S(1)}, u32[]{:S(2)}, u32[]{:S(2)}) collective-permute-start(bf16[2,32,1024]{2,1,0:T(8,128)(2,1)S(1)} %dynamic-slice_bitcast_fusion.18), channel_id=1, source_target_pairs={{0,8},{8,0},{16,24},{24,16},{1,9},{9,1},{17,25},{25,17},{2,10},{10... | collective-permute-start | bytes 393224 | tf_op jit(solution)/shard_map/ppermute | solution.py:57
  444.2 20.0 %collective-permute-start.27 = (bf16[2,32,4096]{2,1,0:T(8,128)(2,1)S(1)}, bf16[2,32,4096]{2,1,0:T(8,128)(2,1)S(1)}, u32[]{:S(2)}, u32[]{:S(2)}) collective-permute-start(bf16[2,32,4096]{2,1,0:T(8,128)(2,1)S(1)} %dynamic-slice_bitcast_fusion.10), channel_id=1, source_target_pairs={{0,8},{8,0},{16,24},{24,16},{1,9},{9,1},{17,25},{25,17},{2,10},{10... | collective-permute-start | bytes 1572872 | tf_op jit(solution)/shard_map/ppermute | solution.py:57
  444.9 6.5 %collective-permute-start.23 = (f32[96,128]{1,0:T(8,128)S(1)}, f32[96,128]{1,0:T(8,128)S(1)}, u32[]{:S(2)}, u32[]{:S(2)}) collective-permute-start(f32[96,128]{1,0:T(8,128)S(1)} %add.415), channel_id=1, source_target_pairs={{0,1},{1,0},{2,3},{3,2},{4,5},{5,4},{6,7},{7,6},{8,9},{9,8},{10,11... | collective-permute-start | bytes 147464 | tf_op jit(solution)/shard_map/ppermute | solution.py:57
  449.2 11.6 %collective-permute-start.33 = (bf16[32,1024]{1,0:T(8,128)(2,1)S(1)}, bf16[32,1024]{1,0:T(8,128)(2,1)S(1)}, u32[]{:S(2)}, u32[]{:S(2)}) collective-permute-start(bf16[32,1024]{1,0:T(8,128)(2,1)S(1)} %dynamic-slice_bitcast_fusion.19), channel_id=1, source_target_pairs={{0,16},{8,24},{16,0},{24,8},{1,17},{9,25},{17,1},{25,9},{2,18},{10... | collective-permute-start | bytes 196616 | tf_op jit(solution)/shard_map/ppermute | solution.py:57
  449.8 25.8 %collective-permute-start.26 = (bf16[2,64,1536]{2,1,0:T(8,128)(2,1)S(1)}, bf16[2,64,1536]{2,1,0:T(8,128)(2,1)S(1)}, u32[]{:S(2)}, u32[]{:S(2)}) collective-permute-start(bf16[2,64,1536]{2,1,0:T(8,128)(2,1)S(1)} %dynamic-slice_bitcast_fusion.13), channel_id=1, source_target_pairs={{0,8},{8,0},{16,24},{24,16},{1,9},{9,1},{17,25},{25,17},{2,10},{10... | collective-permute-start | bytes 1179656 | tf_op jit(solution)/shard_map/ppermute | solution.py:57
  451.3 45.1 %collective-permute-start.24 = (f32[96,128]{1,0:T(8,128)S(1)}, f32[96,128]{1,0:T(8,128)S(1)}, u32[]{:S(2)}, u32[]{:S(2)}) collective-permute-start(f32[96,128]{1,0:T(8,128)S(1)} %add.418), channel_id=1, source_target_pairs={{0,8},{8,0},{16,24},{24,16},{1,9},{9,1},{17,25},{25,17},{2,10},{10... | collective-permute-start | bytes 147464 | tf_op jit(solution)/shard_map/ppermute | solution.py:57
  460.8 10.9 %collective-permute-start.36 = (bf16[32,1024]{1,0:T(8,128)(2,1)S(1)}, bf16[32,1024]{1,0:T(8,128)(2,1)S(1)}, u32[]{:S(2)}, u32[]{:S(2)}) collective-permute-start(bf16[32,1024]{1,0:T(8,128)(2,1)S(1)} %fusion.58), channel_id=1, source_target_pairs={{0,16},{8,24},{16,0},{24,8},{1,17},{9,25},{17,1},{25,9},{2,18},{10... | collective-permute-start | bytes 196616 | tf_op jit(solution)/shard_map/ppermute | solution.py:57
  464.4 16.3 %collective-permute-start.30 = (bf16[32,4096]{1,0:T(8,128)(2,1)S(1)}, bf16[32,4096]{1,0:T(8,128)(2,1)S(1)}, u32[]{:S(2)}, u32[]{:S(2)}) collective-permute-start(bf16[32,4096]{1,0:T(8,128)(2,1)S(1)} %dynamic-slice_bitcast_fusion.14), channel_id=1, source_target_pairs={{0,16},{8,24},{16,0},{24,8},{1,17},{9,25},{17,1},{25,9},{2,18},{10... | collective-permute-start | bytes 786440 | tf_op jit(solution)/shard_map/ppermute | solution.py:57
  471.7 37.2 %collective-permute-start.37 = (bf16[2,32,1024]{2,1,0:T(8,128)(2,1)S(1)}, bf16[2,32,1024]{2,1,0:T(8,128)(2,1)S(1)}, u32[]{:S(2)}, u32[]{:S(2)}) collective-permute-start(bf16[2,32,1024]{2,1,0:T(8,128)(2,1)S(1)} %maximum_select_fusion.16), channel_id=1, source_target_pairs={{0,8},{8,0},{16,24},{24,16},{1,9},{9,1},{17,25},{25,17},{2,10},{10... | collective-permute-start | bytes 393224 | tf_op jit(solution)/shard_map/ppermute | solution.py:57
  475.8 20.5 %collective-permute-start.29 = (bf16[64,1536]{1,0:T(8,128)(2,1)S(1)}, bf16[64,1536]{1,0:T(8,128)(2,1)S(1)}, u32[]{:S(2)}, u32[]{:S(2)}) collective-permute-start(bf16[64,1536]{1,0:T(8,128)(2,1)S(1)} %dynamic-slice_bitcast_fusion.17), channel_id=1, source_target_pairs={{0,16},{8,24},{16,0},{24,8},{1,17},{9,25},{17,1},{25,9},{2,18},{10... | collective-permute-start | bytes 589832 | tf_op jit(solution)/shard_map/ppermute | solution.py:57
  480.8 28.6 %collective-permute-start.32 = (bf16[32,4096]{1,0:T(8,128)(2,1)S(1)}, bf16[32,4096]{1,0:T(8,128)(2,1)S(1)}, u32[]{:S(2)}, u32[]{:S(2)}) collective-permute-start(bf16[32,4096]{1,0:T(8,128)(2,1)S(1)} %fusion.51), channel_id=1, source_target_pairs={{0,16},{8,24},{16,0},{24,8},{1,17},{9,25},{17,1},{25,9},{2,18},{10... | collective-permute-start | bytes 786440 | tf_op jit(solution)/shard_map/ppermute | solution.py:57
  496.3 13.0 %collective-permute-start.31 = (bf16[64,1536]{1,0:T(8,128)(2,1)S(1)}, bf16[64,1536]{1,0:T(8,128)(2,1)S(1)}, u32[]{:S(2)}, u32[]{:S(2)}) collective-permute-start(bf16[64,1536]{1,0:T(8,128)(2,1)S(1)} %fusion.56), channel_id=1, source_target_pairs={{0,16},{8,24},{16,0},{24,8},{1,17},{9,25},{17,1},{25,9},{2,18},{10... | collective-permute-start | bytes 589832 | tf_op jit(solution)/shard_map/ppermute | solution.py:57
  496.4 12.5 %collective-permute-start.28 = (f32[96,128]{1,0:T(8,128)S(1)}, f32[96,128]{1,0:T(8,128)S(1)}, u32[]{:S(2)}, u32[]{:S(2)}) collective-permute-start(f32[96,128]{1,0:T(8,128)S(1)} %add.422), channel_id=1, source_target_pairs={{0,16},{8,24},{16,0},{24,8},{1,17},{9,25},{17,1},{25,9},{2,18},{10... | collective-permute-start | bytes 147464 | tf_op jit(solution)/shard_map/ppermute | solution.py:57
  499.4 20.8 %collective-permute-start.41 = (bf16[2,128,1024]{2,1,0:T(8,128)(2,1)S(1)}, bf16[2,128,1024]{2,1,0:T(8,128)(2,1)S(1)}, u32[]{:S(2)}, u32[]{:S(2)}) collective-permute-start(bf16[2,128,1024]{2,1,0:T(8,128)(2,1)S(1)} %maximum_select_fusion.11), channel_id=1, source_target_pairs={{0,8},{8,0},{16,24},{24,16},{1,9},{9,1},{17,25},{25,17},{2,10},{10... | collective-permute-start | bytes 1572872 | tf_op jit(solution)/shard_map/ppermute | solution.py:57
  509.0 11.8 %collective-permute-start.38 = (bf16[128,1024]{1,0:T(8,128)(2,1)S(1)}, bf16[128,1024]{1,0:T(8,128)(2,1)S(1)}, u32[]{:S(2)}, u32[]{:S(2)}) collective-permute-start(bf16[128,1024]{1,0:T(8,128)(2,1)S(1)} %bitcast.394), channel_id=1, source_target_pairs={{0,1},{1,0},{2,3},{3,2},{4,5},{5,4},{6,7},{7,6},{8,9},{9,8},{10,11... | collective-permute-start | bytes 786440 | tf_op jit(solution)/shard_map/ppermute | solution.py:57
  509.4 19.2 %collective-permute-start.34 = (bf16[2,64,1536]{2,1,0:T(8,128)(2,1)S(1)}, bf16[2,64,1536]{2,1,0:T(8,128)(2,1)S(1)}, u32[]{:S(2)}, u32[]{:S(2)}) collective-permute-start(bf16[2,64,1536]{2,1,0:T(8,128)(2,1)S(1)} %maximum_select_fusion.14), channel_id=1, source_target_pairs={{0,8},{8,0},{16,24},{24,16},{1,9},{9,1},{17,25},{25,17},{2,10},{10... | collective-permute-start | bytes 1179656 | tf_op jit(solution)/shard_map/ppermute | solution.py:57
  509.6 28.6 %collective-permute-start.39 = (bf16[2,32,4096]{2,1,0:T(8,128)(2,1)S(1)}, bf16[2,32,4096]{2,1,0:T(8,128)(2,1)S(1)}, u32[]{:S(2)}, u32[]{:S(2)}) collective-permute-start(bf16[2,32,4096]{2,1,0:T(8,128)(2,1)S(1)} %maximum_select_fusion.13), channel_id=1, source_target_pairs={{0,8},{8,0},{16,24},{24,16},{1,9},{9,1},{17,25},{25,17},{2,10},{10... | collective-permute-start | bytes 1572872 | tf_op jit(solution)/shard_map/ppermute | solution.py:57
  520.4 26.2 %collective-permute-start.42 = (bf16[512,1024]{1,0:T(8,128)(2,1)S(1)}, bf16[512,1024]{1,0:T(8,128)(2,1)S(1)}, u32[]{:S(2)}, u32[]{:S(2)}) collective-permute-start(bf16[512,1024]{1,0:T(8,128)(2,1)S(1)} %bitcast.375), channel_id=1, source_target_pairs={{0,1},{1,0},{2,3},{3,2},{4,5},{5,4},{6,7},{7,6},{8,9},{9,8},{10,11... | collective-permute-start | bytes 3145736 | tf_op jit(solution)/shard_map/ppermute | solution.py:57
  528.7 34.8 %collective-permute-start.35 = (bf16[1,256,1536]{2,1,0:T(8,128)(2,1)S(1)}, bf16[1,256,1536]{2,1,0:T(8,128)(2,1)S(1)}, u32[]{:S(2)}, u32[]{:S(2)}) collective-permute-start(bf16[1,256,1536]{2,1,0:T(8,128)(2,1)S(1)} %bitcast.381), channel_id=1, source_target_pairs={{0,1},{1,0},{2,3},{3,2},{4,5},{5,4},{6,7},{7,6},{8,9},{9,8},{10,11... | collective-permute-start | bytes 2359304 | tf_op jit(solution)/shard_map/ppermute | solution.py:57
  539.4 42.3 %collective-permute-start.40 = (bf16[128,4096]{1,0:T(8,128)(2,1)}, bf16[128,4096]{1,0:T(8,128)(2,1)}, u32[]{:S(2)}, u32[]{:S(2)}) collective-permute-start(bf16[128,4096]{1,0:T(8,128)(2,1)} %bitcast.103), channel_id=1, source_target_pairs={{0,1},{1,0},{2,3},{3,2},{4,5},{5,4},{6,7},{7,6},{8,9},{9,8},{10,11... | collective-permute-start | bytes 3145736 | tf_op jit(solution)/shard_map/ppermute | solution.py:57
  581.8 5.3 copy-start.1
  (26 other events, 72.6 us)
Sparse Core Ops, SparseCore 0:
  10.2 48.0 all-gather.3
  59.8 22.7 all-gather.5
  84.2 58.2 all-gather.7
